TPU v7x, 512 devices: a whole 4x8x8 slice. The times are simulated.
512 devices in a mesh: sec: 2 (over core), wide: 32 (over z, x), narrow: 8 (over y).
Axes of the slice: x: 4, y: 8, z: 8, core: 2. Of those that a mesh axis runs over, the one named last changes fastest.
Arguments:
- voltages: bfloat16 [2, 32, 64, 2, 2, 32768], P('sec', None, 'wide', None, None, 'narrow'), may hold values from -6 to 6
- prototype: float32 [16, 256], replicated, may hold values from -1.5 to 1.5
- beam_delays: float32 [128, 64], replicated, may hold values from -0.5 to 0.5
- station_shifts: int32 [64], P('wide'), may hold values from 0 to 128, as said below
- dm_index: int32 [32], replicated, may hold values from 1 to 63
- owners: int32 [32], replicated, may hold values from 0 to 31, as said below
Outputs:
- power: float32 [2, 64, 128, 128], P('sec', 'wide', 'narrow')
Inputs may be any that keep to these rules, and one draw needn't show every extreme that they name: `owners`: no index along wide owns more than 2 subbands, and some index owns exactly 2. `station_shifts`: some station's shift is exactly 128.
All inputs are finite; a program needn't handle non-finite values.
Results may differ from a plain program's by a relative error of at most 0.00069.
Values may be sent and summed in bfloat16 or wider, within the bound.
No kernel may reach another device: no remote copies, remote signals or barrier semaphores. Data moves between devices by JAX's collectives and lax.ppermute only.
A program may use at most 128 MiB of HBM per device.

v0:
```python
import math

import jax
import jax.numpy as jnp
from jax import lax
from jax.sharding import PartitionSpec as P

MAXD = 128
SEG = 16
SUBBAND_LIMIT = 2


TWO_PI = 2.0 * math.pi


def shifted_2(value, axis, steps):
    count = lax.axis_size(axis)
    initial, last = (max(0, -steps), min(count, count - steps))
    return lax.ppermute(value, axis, [(source, source + steps) for source in range(initial, last)])


def beamset_slot_tables(owners, slot_count, capacity):
    sub_count = owners.shape[0]
    sub_order = jnp.arange(sub_count, dtype=jnp.int32)
    same_owner = owners[:, None] == owners[None, :]
    before = sub_order[None, :] < sub_order[:, None]
    rank_in_set = jnp.sum(jnp.where(same_owner & before, 1, 0), axis=1).astype(jnp.int32)
    slot_lookup = owners * capacity + rank_in_set
    slot_numbers = jnp.arange(slot_count, dtype=jnp.int32)
    slot_match = slot_lookup[None, :] == slot_numbers[:, None]
    subband_per_slot = jnp.sum(jnp.where(slot_match, sub_order[None, :], 0), axis=1)
    filled_slots = jnp.any(slot_match, axis=1)
    return (slot_lookup, subband_per_slot, filled_slots)


def beam_weights(subs, channels, chan_count, beam_delays):
    frequency = (
        subs.astype(jnp.float32)[:, None] + channels.astype(jnp.float32)[None, :] / chan_count
    )
    phase_arg = (TWO_PI * frequency)[:, :, None, None] * beam_delays[None, None, :, :]
    norm_scale = 1.0 / math.sqrt(beam_delays.shape[1])
    weight_real = (jnp.cos(phase_arg) * norm_scale).astype(jnp.bfloat16)
    weight_imag = (-jnp.sin(phase_arg) * norm_scale).astype(jnp.bfloat16)
    upper = jnp.stack([weight_real, -weight_imag], axis=4)
    lower = jnp.stack([weight_imag, weight_real], axis=4)
    return jnp.stack([upper, lower], axis=3)


def chirp_matrix(dm_values, channels, seg_len):
    dft_len = 2 * seg_len
    bin_index = jnp.arange(dft_len, dtype=jnp.int32)
    signed = jnp.where(bin_index < dft_len // 2, bin_index, bin_index - dft_len)
    phase_index = jnp.mod(
        dm_values[:, None, None]
        * signed[None, None, :]
        * (signed[None, None, :] + channels[None, :, None]),
        2 * dft_len,
    )
    offsets = jnp.arange(dft_len, dtype=jnp.int32)
    angle_index = jnp.mod(
        phase_index[:, :, None, :]
        + 2 * offsets[None, None, :, None] * bin_index[None, None, None, :],
        2 * dft_len,
    )
    angles = angle_index.astype(jnp.float32) * (math.pi / dft_len)
    kern_real = jnp.sum(jnp.cos(angles), axis=-1) / dft_len
    kern_imag = jnp.sum(jnp.sin(angles), axis=-1) / dft_len
    row_ids = jnp.arange(seg_len, dtype=jnp.int32)
    lag_index = jnp.mod(row_ids[:, None] + seg_len - offsets[None, :], dft_len)
    mat_real = jnp.take(kern_real, lag_index, axis=-1).astype(jnp.bfloat16)
    mat_imag = jnp.take(kern_imag, lag_index, axis=-1).astype(jnp.bfloat16)
    upper = jnp.stack([mat_real, -mat_imag], axis=3)
    lower = jnp.stack([mat_imag, mat_real], axis=3)
    return jnp.stack([upper, lower], axis=2)


def shards(voltages, prototype, beam_delays, station_shifts, dm_index, owners):
    wide_count = lax.axis_size("wide")
    narrow_count = lax.axis_size("narrow")
    local_volts = voltages[0]
    sub_count = local_volts.shape[0]
    station_local = local_volts.shape[1]
    pol_count = local_volts.shape[2]
    tap_count = prototype.shape[0]
    chan_count = prototype.shape[1]
    spec_local = local_volts.shape[4] // chan_count
    block_len = spec_local * narrow_count
    chan_local = chan_count // narrow_count
    beam_count = beam_delays.shape[0]
    station_count = beam_delays.shape[1]
    rim_len = (tap_count - 1) * chan_count + MAXD
    ahead_part = shifted_2(local_volts[..., :rim_len], "narrow", -1)
    extended = jnp.concatenate([local_volts, ahead_part], axis=-1)
    span_len = (spec_local + tap_count - 1) * chan_count

    def delay_one(samples, offset):
        return lax.dynamic_slice_in_dim(samples, offset, span_len, axis=-1)

    shifted = jax.vmap(delay_one, in_axes=(1, 0), out_axes=1)(extended, station_shifts)
    frames = shifted.reshape(
        sub_count, station_local, pol_count, 2, spec_local + tap_count - 1, chan_count
    )
    filtered = frames[:, :, :, :, 0:spec_local, :].astype(jnp.float32) * prototype[0]
    for tap_index in range(1, tap_count):
        filtered = (
            filtered
            + frames[:, :, :, :, tap_index : tap_index + spec_local, :].astype(jnp.float32)
            * prototype[tap_index]
        )
    chan_ids = jnp.arange(chan_count, dtype=jnp.int32)
    dft_index = jnp.mod(chan_ids[:, None] * chan_ids[None, :], chan_count)
    dft_angle = dft_index.astype(jnp.float32) * (TWO_PI / chan_count)
    cos_table = jnp.cos(dft_angle)
    sin_table = jnp.sin(dft_angle)
    dft_table = jnp.stack(
        [jnp.stack([cos_table, -sin_table], axis=1), jnp.stack([sin_table, cos_table], axis=1)],
        axis=0,
    )
    spectra = jnp.einsum(
        "ispxtm,xmyc->ispyct", filtered, dft_table, precision=lax.Precision.HIGHEST
    ) / math.sqrt(chan_count)
    spectra = spectra.astype(jnp.bfloat16).reshape(
        sub_count, station_local, pol_count, 2, narrow_count, chan_local * spec_local
    )
    turned = lax.all_to_all(spectra, "narrow", split_axis=4, concat_axis=4, tiled=True)
    turned = turned.reshape(
        sub_count, station_local, pol_count, 2, narrow_count * chan_local * spec_local
    )
    slot_count = wide_count * SUBBAND_LIMIT
    slot_lookup, subband_per_slot, filled_slots = beamset_slot_tables(
        owners, slot_count, SUBBAND_LIMIT
    )
    wide_index = lax.axis_index("wide")
    picked = jnp.take(turned, subband_per_slot, axis=0)
    outgoing = jnp.where(
        filled_slots[:, None, None, None, None], picked, jnp.zeros((), jnp.bfloat16)
    )
    received = lax.all_to_all(outgoing, "wide", split_axis=0, concat_axis=1, tiled=True)
    my_subs = lax.dynamic_slice_in_dim(subband_per_slot, wide_index * SUBBAND_LIMIT, SUBBAND_LIMIT)
    held_count = received.shape[0]
    inputs = received.reshape(
        held_count, station_count, pol_count, 2, narrow_count, chan_local, spec_local
    )
    channels = lax.axis_index("narrow") * chan_local + jnp.arange(chan_local, dtype=jnp.int32)
    weights = beam_weights(my_subs, channels, chan_count, beam_delays)
    beam_data = jnp.einsum(
        "kcbysx,kspxnct->kcbypnt", weights, inputs, preferred_element_type=jnp.float32
    ).astype(jnp.bfloat16)
    beam_data = beam_data.reshape(held_count, chan_local, beam_count, 2, pol_count, block_len)
    last_part = beam_data[..., block_len - SEG :].reshape(
        held_count, chan_local, beam_count * 2 * pol_count * SEG
    )
    moved_part = shifted_2(last_part, "sec", 1)
    earlier = moved_part.reshape(held_count, chan_local, beam_count, 2, pol_count, SEG)
    series = jnp.concatenate([earlier, beam_data], axis=-1)
    seg_count = block_len // SEG
    early_half = series[..., :block_len].reshape(
        held_count, chan_local, beam_count, 2, pol_count, seg_count, SEG
    )
    late_half = series[..., SEG:].reshape(
        held_count, chan_local, beam_count, 2, pol_count, seg_count, SEG
    )
    dm_values = jnp.take(dm_index, my_subs)
    chirp_mat = chirp_matrix(dm_values, channels, SEG)
    cleaned = jnp.einsum(
        "kcyjxe,kcbxpge->kcbypgj",
        chirp_mat[..., :SEG],
        early_half,
        preferred_element_type=jnp.float32,
    )
    cleaned = cleaned + jnp.einsum(
        "kcyjxe,kcbxpge->kcbypgj",
        chirp_mat[..., SEG:],
        late_half,
        preferred_element_type=jnp.float32,
    )
    partial_power = (jnp.sum(cleaned * cleaned, axis=(1, 3, 4)) / chan_count).reshape(
        held_count, beam_count, block_len
    )
    share_power = lax.psum_scatter(partial_power, "narrow", scatter_dimension=1, tiled=True)
    return share_power[None]


def solution(mesh):
    placed = (P("sec", None, "wide", None, None, "narrow"), P(), P(), P("wide"), P(), P())
    return jax.shard_map(
        shards,
        mesh=mesh,
        in_specs=placed,
        out_specs=P("sec", "wide", "narrow", None),
        check_vma=False,
    )
```

profile of v0, /device:TPU:6, one launch (start us, length us, event | category | flops | bytes accessed | tf_op | source)
XLA Modules:
  0.0 589.1 jit_solution(10871689170626598839)
XLA Ops:
  6.5 3.8 copy.208
  10.4 3.1 slice.178
  13.5 1.3 collective-permute-start
  14.8 0.1 copy.117
  15.1 1.0 fusion.48
  16.0 1.0 fusion.46
  17.1 0.1 maximum_bitcast_fusion.9
  17.3 44.4 %collective-permute-done = bf16[32,2,2,2,3968]{4,3,2,0,1:T(2,128)(2,1)} collective-permute-done((bf16[32,2,2,2,3968]{4,3,2,0,1:T(2,128)(2,1)}, bf16[32,2,2,2,3968]{4,3,2,0,1:T(2,128)(2,1)}, u32[]{:S(2)}, u32[]{:S(2)}) %collective-permute-start) | collective-permute-done | bytes 2031648 | tf_op jit(solution)/shard_map/ppermute | solution.py:19
  61.7 7.4 %maximum_bitcast_fusion.2 = bf16[2,32,2,2,8064]{4,3,2,1,0:T(2,128)(2,1)} fusion(bf16[32,2,2,2,3968]{4,3,2,0,1:T(2,128)(2,1)} %collective-permute-done, bf16[32,2,2,2,4096]{4,3,2,0,1:T(2,128)(2,1)S(1)} %bitcast.148), kind=kLoop, calls=%fused_computation.28 | loop fusion | flops 8257536 | bytes 8257536 | tf_op jit(solution)/shard_map/vmap()/transpose | solution.py:97
  69.1 16.7 %while.1 = (s32[]{:T(128)}, bf16[2,32,2,2,8064]{4,3,2,1,0:T(2,128)(2,1)}, s32[2,5]{1,0:T(2,128)S(1)}, bf16[2,32,2,2,7936]{4,3,2,1,0:T(2,128)(2,1)}, s32[]{:T(128)}) while((s32[]{:T(128)}, bf16[2,32,2,2,8064]{4,3,2,1,0:T(2,128)(2,1)}, s32[2,5]{1,0:T(2,128)S(1)}, bf16[2,32,2,2,7936]{4,3,2,1,0:T(2,128)(2,1)}, s32[]{:T(128)}) %tuple.59), condition=%wide.while_cond, body=%wide.while_body.sunk | while | flops 2 | bytes 4064889 | solution.py:97
  69.3 0.6 fusion.68
  69.9 7.6 %dynamic-slice_dynamic-update-slice_fusion.2 = bf16[2,32,2,2,7936]{4,3,2,1,0:T(2,128)(2,1)} fusion(bf16[2,32,2,2,7936]{4,3,2,1,0:T(2,128)(2,1)} %get-tuple-element.111, s32[]{:T(128)} %get-tuple-element.108, bf16[2,32,2,2,8064]{4,3,2,1,0:T(2,128)(2,1)} %get-tuple-element.114, s32[]{:T(128)} %bitcast.141, s32[]{:T(128)} %bitcast.142), kind=kLoop, calls=%fused_computation.4.clone.1 | loop fusion | bytes 4064768 | tf_op jit(solution)/shard_map/vmap()/gather
  77.5 0.6 fusion.68
  78.1 7.6 %dynamic-slice_dynamic-update-slice_fusion.2 = bf16[2,32,2,2,7936]{4,3,2,1,0:T(2,128)(2,1)} fusion(bf16[2,32,2,2,7936]{4,3,2,1,0:T(2,128)(2,1)} %get-tuple-element.111, s32[]{:T(128)} %get-tuple-element.108, bf16[2,32,2,2,8064]{4,3,2,1,0:T(2,128)(2,1)} %get-tuple-element.114, s32[]{:T(128)} %bitcast.141, s32[]{:T(128)} %bitcast.142), kind=kLoop, calls=%fused_computation.4.clone.1 | loop fusion | bytes 4064768 | tf_op jit(solution)/shard_map/vmap()/gather
  85.7 10.1 %reshape.436 = bf16[32,2,2,2,31,256]{5,4,3,2,0,1:T(8,128)(2,1)} reshape(bf16[32,2,2,2,7936]{4,3,2,0,1:T(2,128)(2,1)} %bitcast.152) | data formatting | bytes 8126464 | tf_op jit(solution)/shard_map/reshape | solution.py:100
  95.8 30.3 %fusion.64 = (bf16[32,2,2,2,16,256]{5,4,3,2,0,1:T(8,128)(2,1)S(1)}, bf16[32,2,2,2,16,256]{5,4,3,2,0,1:T(8,128)(2,1)S(1)}, bf16[32,2,2,2,16,256]{5,4,3,2,0,1:T(8,...) fusion(bf16[32,2,2,2,31,256]{5,4,3,2,0,1:T(8,128)(2,1)} %reshap, ...), kind=kLoop, calls=%fused_computation.136 | loop fusion | bytes 67108864 | tf_op jit(solution)/shard_map/slice | solution.py:103
  126.2 11.6 %multiply_add_fusion = f32[32,2,2,2,16,256]{5,4,0,3,2,1:T(8,128)S(1)} fusion(bf16[32,2,2,2,16,256]{5,4,3,2,0,1:T(8,128)(2,1)} %get-tuple-element.41, bf16[32,2,2,2,16,256]{5,4,3,2,0,1:T(8,128)(2,1)S(1)} %get-tuple-element.27, bf16[32,2,2,2,16,256]{5,4,3,2,0,1:T(8,128)(2,1)S(1)} %get-tuple-element.28, ...), kind=kLoop, calls=%fused_computation.27 | loop fusion | flops 49283072 | bytes 37765120 | tf_op jit(solution)/shard_map/add | solution.py:106
  137.8 8.7 %fusion.23 = bf16[32,2,2,2,256,16]{4,0,5,2,1,3:T(8,128)(2,1)S(1)} fusion(f32[32,2,2,2,16,256]{5,4,0,3,2,1:T(8,128)S(1)} %multiply_add_fusion, f32[1,256,2,256]{3,1,0,2:T(8,128)S(1)} %get-tuple-element.47, f32[1,256,2,256]{3,1,0,2:T(8,128)S(1)} %get-tuple-element.46), kind=kOutput, calls=%fused_computation.36 | convolution fusion | flops 6444810240 | bytes 7340032 | tf_op jit(solution)/shard_map/ispxtm,xmyc->ispyct/dot_general | solution.py:119
  146.5 8.6 %copy.120 = bf16[32,2,2,2,256,16]{0,5,4,3,2,1:T(8,128)(2,1)} copy(bf16[32,2,2,2,256,16]{4,0,5,2,1,3:T(8,128)(2,1)S(1)} %fusion.23) | data formatting | bytes 4194304 | tf_op jit(solution)/shard_map/convert_element_type | solution.py:122
  155.1 8.0 %copy.121 = bf16[32,2,2,2,8,512]{5,0,3,2,1,4:T(8,128)(2,1)} copy(bf16[32,2,2,2,8,512]{0,5,4,3,2,1:T(8,128)(2,1)} %bitcast.146) | data formatting | bytes 4194304 | tf_op jit(solution)/shard_map/reshape | solution.py:122
  163.1 7.2 %all-to-all-start = ((bf16[32,2,2,2,8,512]{5,0,3,2,1,4:T(8,128)(2,1)}), bf16[32,2,2,2,8,512]{5,0,3,2,1,4:T(8,128)(2,1)S(1)}, u32[]{:S(2)}, u32[]{:S(2)}) async-start(bf16[32,2,2,2,8,512]{5,0,3,2,1,4:T(8,128)(2,1)} %copy.121), calls=%async_computation | async-start | bytes 4194304 | tf_op jit(solution)/shard_map/all_to_all | solution.py:125
  170.4 0.2 select_reduce_fusion.1
  170.6 0.1 select_reduce_fusion
  170.7 0.1 fusion.51
  170.8 50.0 %all-to-all-done = bf16[32,2,2,2,8,512]{5,0,3,2,1,4:T(8,128)(2,1)S(1)} async-done(((bf16[32,2,2,2,8,512]{5,0,3,2,1,4:T(8,128)(2,1)}), bf16[32,2,2,2,8,512]{5,0,3,2,1,4:T(8,128)(2,1)S(1)}, u32[]{:S(2)}, u32[]{:S(2)}) %all-to-all-start) | async-done | bytes 2097184 | tf_op jit(solution)/shard_map/all_to_all | solution.py:125
  220.7 2.5 copy.122
  223.3 3.3 reshape.342
  226.6 10.7 %gather_fusion = bf16[64,2,2,2,4096]{4,3,2,1,0:T(2,128)(2,1)} fusion(bf16[32,2,2,2,4096]{4,3,2,1,0:T(2,128)(2,1)S(1)} %reshape.342, s32[1024]{0:T(1024)S(1)} %pad_clamp_fusion.2), kind=kCustom, calls=%fused_computation.2 | custom fusion | bytes 8388864 | tf_op jit(solution)/shard_map/jit(_take)/gather | solution.py:134
  237.2 8.5 %broadcast_select_fusion.1 = bf16[64,2,2,2,4096]{4,3,2,1,0:T(2,128)(2,1)} fusion(pred[64]{0:T(512)(128)(4,1)S(1)} %fusion.51, bf16[64,2,2,2,4096]{4,3,2,1,0:T(2,128)(2,1)} %gather_fusion, pred[64]{0:T(512)(128)(4,1)S(1)} %compare_and_fusion.1), kind=kLoop, calls=%fused_computation.18 | loop fusion | flops 4194304 | bytes 8388736 | tf_op jit(solution)/shard_map/jit(_where)/select_n | solution.py:135
  245.7 13.5 %all-to-all-start.1 = ((bf16[64,2,2,2,4096]{4,3,2,1,0:T(2,128)(2,1)}), bf16[64,2,2,2,4096]{4,3,2,1,0:T(2,128)(2,1)}, u32[]{:S(2)}, u32[]{:S(2)}) async-start(bf16[64,2,2,2,4096]{4,3,2,1,0:T(2,128)(2,1)} %broadcast_select_fusion.1), calls=%async_computation.1 | async-start | bytes 8388608 | tf_op jit(solution)/shard_map/all_to_all | solution.py:138
  259.2 0.1 compare_select_fusion.2
  259.3 0.6 gather_fusion.1
  260.2 4.9 sine_reduce_fusion
  265.1 0.1 copy.131
  265.2 0.1 compare_select_fusion
  265.4 2.1 gather_fusion.3
  267.5 0.3 copy.156
  267.8 0.1 copy.129
  267.9 2.1 gather_fusion.2
  270.0 0.3 copy.155
  270.3 0.1 compare_and_fusion
  270.5 0.1 fusion.49
  270.6 0.2 maximum_bitcast_fusion.11
  270.9 7.2 %fusion.45 = bf16[2,32,128,64,1]{2,3,4,1,0:T(8,128)(2,1)S(1)} fusion(f32[128,64]{0,1:T(8,128)S(1)} %copy-done.2, f32[2,32]{1,0:T(2,128)S(1)} %add_multiply_fusion), kind=kLoop, calls=%fused_computation.78 | loop fusion | flops 3670016 | bytes 1081600 | tf_op jit(solution)/shard_map/neg | solution.py:44
  278.1 8.3 %fusion.22 = (bf16[2,32,128,64,1]{2,3,4,1,0:T(8,128)(2,1)S(1)}, bf16[2,32,128,64,1]{2,3,4,1,0:T(8,128)(2,1)S(1)}) fusion(f32[128,64]{0,1:T(8,128)S(1)} %copy-done.2, f32[2,32]{1,0:T(2,128)S(1)} %add_multiply_fusion), kind=kLoop, calls=%fused_computation.35 | loop fusion | flops 3145728 | bytes 2130176 | tf_op jit(solution)/shard_map/convert_element_type | solution.py:43
  286.4 1.7 maximum_bitcast_fusion.3
  288.0 67.0 %all-to-all-done.1 = bf16[64,2,2,2,4096]{4,3,2,1,0:T(2,128)(2,1)} async-done(((bf16[64,2,2,2,4096]{4,3,2,1,0:T(2,128)(2,1)}), bf16[64,2,2,2,4096]{4,3,2,1,0:T(2,128)(2,1)}, u32[]{:S(2)}, u32[]{:S(2)}) %all-to-all-start.1) | async-done | bytes 4194336 | tf_op jit(solution)/shard_map/all_to_all | solution.py:138
  355.0 12.0 %copy.123 = bf16[2,32,2,2,2,4096]{5,4,3,2,1,0:T(2,128)(2,1)} copy(bf16[2,32,2,2,2,4096]{5,4,3,2,0,1:T(2,128)(2,1)} %bitcast.38) | data formatting | bytes 8388608 | tf_op jit(solution)/shard_map/all_to_all | solution.py:138
  367.1 35.8 %reshape.343 = bf16[2,64,2,2,8,32,16]{6,5,4,3,2,1,0:T(8,128)(2,1)} reshape(bf16[2,32,2,2,2,4096]{5,4,3,2,1,0:T(2,128)(2,1)} %copy.123) | data formatting | bytes 8388608 | tf_op jit(solution)/shard_map/reshape | solution.py:141
  402.9 53.7 %bitcast_convert_fusion = bf16[2,32,128,2,2,8,16]{2,6,5,4,3,1,0:T(8,128)(2,1)} fusion(bf16[2,64,2,2,8,32,16,1]{6,5,4,3,2,1,0,7:T(8,128)(2,1)} %bitcast.143, bf16[2,32,128,1,64,2]{2,4,5,3,1,0:T(8,128)(2,1)} %get-tuple-element.43, bf16[2,32,128,1,64,2]{2,4,5,3,1,0:T(8,128)(2,1)S(1)} %get-tuple-element.42), kind=kOutput, calls=%fused_computation.11 | convolution fusion | flops 1086324736 | bytes 16777216 | tf_op jit(solution)/shard_map/kcbysx,kspxnct->kcbypnt/dot_general | solution.py:146
  456.6 1.4 slice.195
  458.0 6.8 %copy.125 = bf16[2,32,128,2,2,16]{1,5,4,3,2,0:T(8,128)(2,1)} copy(bf16[2,32,128,2,2,16]{2,5,4,3,1,0:T(8,128)(2,1)S(1)} %slice.195) | data formatting | bytes 2097152 | tf_op jit(solution)/shard_map/slice | solution.py:150
  464.7 3.5 copy.126
  468.2 1.4 collective-permute-start.1
  469.6 11.3 %fusion.4 = f32[2,32,128,2,8,2,16,1]{2,6,7,5,4,3,1,0:T(8,128)} fusion(bf16[2,32,1,16,2,32]{5,3,4,2,1,0:T(8,128)(2,1)S(1)} %get-tuple-element.45, bf16[2,32,1,16,2,32]{5,3,4,2,1,0:T(8,128)(2,1)S(1)} %get-tuple-element.44, bf16[2,32,128,2,2,8,16]{2,6,5,4,3,1,0:T(8,128)(2,1)} %bitcast_convert_fusion), kind=kOutput, calls=%fused_computation.13 | convolution fusion | flops 268697600 | bytes 25427968 | tf_op jit(solution)/shard_map/kcyjxe,kcbxpge->kcbypgj/dot_general | solution.py:171
  480.9 3.1 copy.127
  484.1 6.9 %copy.128 = bf16[2,32,128,2,2,16]{2,5,4,3,1,0:T(8,128)(2,1)S(1)} copy(bf16[2,32,128,2,2,16]{1,5,4,3,2,0:T(8,128)(2,1)} %bitcast.150) | data formatting | bytes 2097152 | tf_op jit(solution)/shard_map/reshape | solution.py:154
  491.0 9.9 %pad_maximum_fusion = bf16[2,32,128,2,2,128]{2,5,4,3,1,0:T(8,128)(2,1)} fusion(bf16[2,32,128,2,2,128]{2,5,4,3,1,0:T(8,128)(2,1)} %bitcast.145, bf16[2,32,128,2,2,16]{2,5,4,3,1,0:T(8,128)(2,1)S(1)} %copy.128), kind=kLoop, calls=%fused_computation.12 | loop fusion | flops 16777216 | bytes 17825792 | tf_op jit(solution)/shard_map/concatenate | solution.py:155
  500.9 9.6 %fusion.3 = f32[2,128,8,16]{1,3,2,0:T(8,128)S(1)} fusion(f32[2,32,128,2,8,2,16,1]{2,6,7,5,4,3,1,0:T(8,128)} %fusion.4, bf16[2,32,128,2,2,8,16,1]{2,6,5,4,3,1,0,7:T(8,128)(2,1)} %bitcast.151, bf16[2,32,1,16,2,32]{5,3,4,2,1,0:T(8,128)(2,1)S(1)} %get-tuple-element.45, bf16[2,32,1,16,2,32]{5,3,4,2,1,0:T(8,128)(2,1)S(1)} %get-tuple-element.44), kind=kOutput, calls=%fused_computation.10 | convolution fusion | flops 281247744 | bytes 25559040 | tf_op jit(solution)/shard_map/kcyjxe,kcbxpge->kcbypgj/dot_general | solution.py:165
  510.5 0.8 copy.137
  511.3 1.3 dynamic-slice.4
  513.2 67.3 %all-reduce.3.cloned.1.call-done = f32[2,128,128]{2,0,1:T(2,128)} async-done(((f32[2,128,128]{2,0,1:T(2,128)}), f32[2,128,128]{2,0,1:T(2,128)}) %all-reduce.3.cloned.1.call-update) | async-done | bytes 131088
  580.5 0.7 dynamic-slice_bitcast_fusion
  581.2 0.6 copy.138
  (46 shorter events, 0.9 us)
Async XLA Ops:
  6.5 252.8 %copy-start = (s32[32]{0:T(128)S(1)}, s32[32]{0:T(128)}, u32[]{:S(2)}) copy-start(s32[32]{0:T(128)} %param.12) | copy-start | bytes 388
  6.5 8.3 %copy-start.4 = (s32[2]{0:T(128)S(1)}, s32[2]{0:T(128)}, u32[]{:S(2)}) copy-start(s32[2]{0:T(128)} %param.11) | copy-start | bytes 28
  10.3 6.9 %copy-start.3 = (f32[16,256]{1,0:T(8,128)S(1)}, f32[16,256]{1,0:T(8,128)}, u32[]{:S(2)}) copy-start(f32[16,256]{1,0:T(8,128)} %param.9) | copy-start | bytes 49156
  13.5 48.2 %collective-permute-start = (bf16[32,2,2,2,3968]{4,3,2,0,1:T(2,128)(2,1)}, bf16[32,2,2,2,3968]{4,3,2,0,1:T(2,128)(2,1)}, u32[]{:S(2)}, u32[]{:S(2)}) collective-permute-start(bf16[32,2,2,2,3968]{4,3,2,0,1:T(2,128)(2,1)} %slice.178), channel_id=1, source_target_pairs={{1,0},{2,1},{3,2},{4,3},{5,4},{6,5},{7,6},{9,8},{10,9},{11,10},{12... | collective-permute-start | bytes 6094856 | tf_op jit(solution)/shard_map/ppermute | solution.py:19
  163.1 7.2 %copy-start.5 = (s32[32]{0:T(128)S(1)}, s32[32]{0:T(128)}, u32[]{:S(2)}) copy-start(s32[32]{0:T(128)} %param.13) | copy-start | bytes 388
  163.1 57.6 %all-to-all-start = ((bf16[32,2,2,2,8,512]{5,0,3,2,1,4:T(8,128)(2,1)}), bf16[32,2,2,2,8,512]{5,0,3,2,1,4:T(8,128)(2,1)S(1)}, u32[]{:S(2)}, u32[]{:S(2)}) async-start(bf16[32,2,2,2,8,512]{5,0,3,2,1,4:T(8,128)(2,1)} %copy.121), calls=%async_computation | async-start | bytes 4194304 | tf_op jit(solution)/shard_map/all_to_all | solution.py:125
  245.7 109.4 %all-to-all-start.1 = ((bf16[64,2,2,2,4096]{4,3,2,1,0:T(2,128)(2,1)}), bf16[64,2,2,2,4096]{4,3,2,1,0:T(2,128)(2,1)}, u32[]{:S(2)}, u32[]{:S(2)}) async-start(bf16[64,2,2,2,4096]{4,3,2,1,0:T(2,128)(2,1)} %broadcast_select_fusion.1), calls=%async_computation.1 | async-start | bytes 8388608 | tf_op jit(solution)/shard_map/all_to_all | solution.py:138
  259.2 11.7 %copy-start.2 = (f32[128,64]{0,1:T(8,128)S(1)}, f32[128,64]{0,1:T(8,128)}, u32[]{:S(2)}) copy-start(f32[128,64]{0,1:T(8,128)} %param.10) | copy-start | bytes 98308
  259.2 321.3 %all-reduce.3.cloned.1.call-start = ((), (), s32[]{:S(2)}) async-start(), calls=%async_computation.2 | async-start | bytes 262144
  468.2 12.7 %collective-permute-start.1 = (bf16[2,32,8192]{2,1,0:T(8,128)(2,1)S(1)}, bf16[2,32,8192]{2,1,0:T(8,128)(2,1)S(1)}, u32[]{:S(2)}, u32[]{:S(2)}) collective-permute-start(bf16[2,32,8192]{2,1,0:T(8,128)(2,1)S(1)} %copy.126), channel_id=1, source_target_pairs={{0,256},{1,257},{2,258},{3,259},{4,260},{5,261},{6,262},{7,263},{8... | collective-permute-start | bytes 3145736 | tf_op jit(solution)/shard_map/ppermute | solution.py:19
  500.9 80.9 %copy-start.1 = (s32[32]{0:T(128)S(1)}, s32[32]{0:T(128)}, u32[]{:S(2)}) copy-start(s32[32]{0:T(128)} %param.12) | copy-start | bytes 388
Sparse Core Ops, SparseCore 0:
  511.4 69.0 all-reduce.2
where the time goes:
time: 599 us; the launch traced here: 589 us
  waiting for transfers between devices  229 us (38%)
  local copies, waits for them, and re-layouts  176 us (29%)
  matrix products  83.3 us (14%)
  other arithmetic  63 us (11%)
  starting transfers between devices  23.4 us (4%)
  between operations  14.8 us (2%)
    unnamed x2, waiting for transfers between devices  67.3 us
    all_to_all x1, waiting for transfers between devices, shards(): lax.all_to_all(outgoing, 'wide', split_axis=0, concat_axis=1, tiled=True)  67 us
    dot_general x1, matrix products, shards(): jnp.einsum('kcbysx,kspxnct->kcbypnt', weights, inputs, preferred_element_...  53.7 us
    all_to_all x1, waiting for transfers between devices, shards(): lax.all_to_all(spectra, 'narrow', split_axis=4, concat_axis=4, tiled=True)  50 us
    ppermute x2, waiting for transfers between devices, shifted_2(): lax.ppermute(value, axis, [(source, source + steps) for source in range(i...  44.4 us
    reshape x1, local copies, waits for them, and re-layouts, shards(): received.reshape(held_count, station_count, pol_count, 2, narrow_count, c...  35.8 us
    slice x1, local copies, waits for them, and re-layouts, shards(): frames[:, :, :, :, 0:spec_local, :].astype(jnp.float32) * prototype[0]  30.3 us
    gather x6, local copies, waits for them, and re-layouts  16.4 us
  transfers between devices with their start and end apart: 5, of which 4 were waited for; matrix products, arithmetic and copies ran while one was open for 7% of the time, Pallas kernels for 0%

commit v1 on v0

v1 whole, which is shorter than its diff:
```python
import math

import jax
import jax.numpy as jnp
from jax import lax
from jax.experimental import pallas as pl
from jax.experimental.pallas import tpu as pltpu
from jax.sharding import PartitionSpec as P

SEG = 16
SUBBAND_LIMIT = 2
TWO_PI = 2.0 * math.pi
VMEM_BYTES = 56 * 1024 * 1024
T_BLOCK = 8


def slot_tables(owners, slot_count):
    sub_count = owners.shape[0]
    order = jnp.arange(sub_count, dtype=jnp.int32)
    same = owners[:, None] == owners[None, :]
    before = order[None, :] < order[:, None]
    rank = jnp.sum(jnp.where(same & before, 1, 0), axis=1).astype(jnp.int32)
    lookup = owners * SUBBAND_LIMIT + rank
    slots = jnp.arange(slot_count, dtype=jnp.int32)
    match = lookup[None, :] == slots[:, None]
    subband = jnp.sum(jnp.where(match, order[None, :], 0), axis=1)
    return subband, jnp.any(match, axis=1)


def filter_kernel(volts_ref, taps_ref, table_ref, out_ref, frames, filtered, packed):
    source_count, group_size, rows, piece_len = volts_ref.shape
    tap_count, _, chan_count = taps_ref.shape
    block_count = 2
    pieces = source_count // block_count
    piece_frames = piece_len // chan_count
    frame_count = pieces * piece_frames
    station_count = table_ref.shape[0]
    pol_count = rows // (2 * station_count)
    frames[frame_count:] = jnp.zeros_like(frames[frame_count:])

    def one(index, carry):
        sub = index // block_count
        block = index % block_count
        for piece in range(pieces):
            for frame in range(piece_frames):
                frames[piece * piece_frames + frame] = volts_ref[
                    block * pieces + piece, sub, :, frame * chan_count : (frame + 1) * chan_count
                ].astype(jnp.float32)
        for low in range(0, chan_count, 128):
            lanes = slice(low, low + 128)
            taps = [taps_ref[tap, :, lanes] for tap in range(tap_count)]

            def some(step, inner):
                start = pl.multiple_of(step * T_BLOCK, T_BLOCK)
                loaded = [frames[start + i, :, lanes] for i in range(T_BLOCK + tap_count - 1)]
                for i in range(T_BLOCK):
                    total = taps[0] * loaded[i]
                    for tap in range(1, tap_count):
                        total = total + taps[tap] * loaded[i + tap]
                    at = pl.multiple_of((start + i) * rows, rows)
                    filtered[low // 128, pl.ds(at, rows), :] = total
                return inner

            lax.fori_loop(0, frame_count // T_BLOCK, some, 0)
        for station in range(station_count):
            parts = []
            for pol in range(pol_count):
                pair = [
                    filtered[
                        half,
                        pl.ds((station * pol_count + pol) * 2 + r, frame_count, stride=rows),
                        :,
                    ].astype(jnp.bfloat16)
                    for r in range(2)
                    for half in range(chan_count // 128)
                ]
                parts.append(jnp.concatenate(pair, axis=1))
            series = jnp.concatenate(parts, axis=0)
            spectra = lax.dot_general(
                table_ref[station],
                series,
                (((1,), (1,)), ((), ())),
                preferred_element_type=jnp.float32,
            )
            for r in range(2):
                for pol in range(pol_count):
                    packed[
                        block, pl.ds((station * 2 + r) * pol_count + pol, chan_count, stride=rows), :
                    ] = spectra[
                        r * chan_count : (r + 1) * chan_count,
                        pol * frame_count : (pol + 1) * frame_count,
                    ]

        @pl.when(block == block_count - 1)
        def _():
            for b in range(block_count):
                out_ref[sub, :, :, b * frame_count : (b + 1) * frame_count] = (
                    packed[b].reshape(chan_count, rows, frame_count).astype(jnp.bfloat16)
                )

        return carry

    lax.fori_loop(0, group_size * block_count, one, 0)


def beam_kernel(spectra_ref, weights_ref, kern_ref, power_ref, held):
    source_count, chan_local, rows, length = spectra_ref.shape
    block_count, beam_count, block_len = power_ref.shape
    pol_count = 2
    depth = source_count * rows // pol_count
    span = 2 * SEG
    from_seg = lax.broadcasted_iota(jnp.int32, (block_len, block_len), 0) // SEG
    to_seg = lax.broadcasted_iota(jnp.int32, (block_len, block_len), 1) // SEG
    own_mask = (from_seg == to_seg) | (from_seg + 1 == to_seg)
    cross_mask = (from_seg == block_len // SEG - 1) & (to_seg == 0)
    power_ref[...] = jnp.zeros_like(power_ref)

    def one(chan, carry):
        for block in range(block_count):
            lanes = slice(block * block_len, (block + 1) * block_len)
            held[block] = (
                spectra_ref[:, chan, :, lanes]
                .astype(jnp.float32)
                .reshape(source_count * rows, block_len)
            )
        inputs = jnp.concatenate(
            [
                held[block, pl.ds(pol, depth, stride=pol_count), :].astype(jnp.bfloat16)
                for pol in range(pol_count)
                for block in range(block_count)
            ],
            axis=1,
        )
        beams = jnp.dot(
            weights_ref[chan], inputs, preferred_element_type=jnp.float32
        ).astype(jnp.bfloat16)
        tiled = [
            jnp.concatenate([kern_ref[chan, part]] * (block_len // span), axis=0)
            for part in range(2)
        ]

        def matrix(mask):
            real, imag = [jnp.where(mask, part, 0.0) for part in tiled]
            return jnp.concatenate(
                [
                    jnp.concatenate([real, imag], axis=1),
                    jnp.concatenate([-imag, real], axis=1),
                ],
                axis=0,
            ).astype(jnp.bfloat16)

        def series(block):
            parts = []
            for pol in range(pol_count):
                at = pol * length + block * block_len
                parts.append(
                    jnp.concatenate(
                        [
                            beams[:beam_count, at : at + block_len],
                            beams[beam_count:, at : at + block_len],
                        ],
                        axis=1,
                    )
                )
            return jnp.concatenate(parts, axis=0)

        own = matrix(own_mask)
        first, second = series(0), series(1)
        clean = [
            jnp.dot(first, own, preferred_element_type=jnp.float32),
            jnp.dot(second, own, preferred_element_type=jnp.float32)
            + jnp.dot(first, matrix(cross_mask), preferred_element_type=jnp.float32),
        ]
        for block in range(block_count):
            square = clean[block] * clean[block]
            both = square[:beam_count] + square[beam_count:]
            power_ref[block] += both[:, :block_len] + both[:, block_len:]
        return carry

    lax.fori_loop(0, chan_local, one, 0)


def shards(voltages, prototype, beam_delays, station_shifts, dm_index, owners):
    wide_count = lax.axis_size("wide")
    source_count = lax.axis_size("sec") * lax.axis_size("narrow")
    narrow_count = lax.axis_size("narrow")
    block_count = lax.axis_size("sec")
    _, sub_count, station_local, pol_count, _, piece_len = voltages.shape
    tap_count, chan_count = prototype.shape
    beam_count, station_count = beam_delays.shape
    rows = station_local * pol_count * 2
    group_size = sub_count // source_count
    chan_local = group_size * chan_count // wide_count
    chan_groups = chan_count // chan_local
    block_len = piece_len * narrow_count // chan_count
    length = block_count * block_len
    together = ("sec", "narrow")

    volts = voltages.reshape(sub_count, rows, piece_len)
    volts = lax.all_to_all(volts, together, 0, 0, tiled=True)
    volts = volts.reshape(source_count, group_size, rows, piece_len)

    flat = prototype.reshape(-1)
    taps = jnp.stack(
        [
            lax.dynamic_update_slice(
                jnp.zeros((tap_count + 1) * chan_count, jnp.float32), flat, (station_shifts[s],)
            ).reshape(tap_count + 1, chan_count)
            for s in range(station_local)
        ],
        axis=1,
    )
    taps = jnp.repeat(taps, 2 * pol_count, axis=1)
    ids = jnp.arange(chan_count, dtype=jnp.int32)
    turn = jnp.mod(
        ids[None, :, None] * (ids[None, None, :] - station_shifts[:, None, None]), chan_count
    )
    angle = turn.astype(jnp.float32) * (TWO_PI / chan_count)
    scale = 1.0 / math.sqrt(chan_count)
    cosine, sine = jnp.cos(angle) * scale, jnp.sin(angle) * scale
    table = jnp.concatenate(
        [
            jnp.concatenate([cosine, sine], axis=2),
            jnp.concatenate([-sine, cosine], axis=2),
        ],
        axis=1,
    ).astype(jnp.bfloat16)
    whole = pl.BlockSpec(memory_space=pltpu.VMEM)
    spectra = pl.pallas_call(
        filter_kernel,
        out_shape=jax.ShapeDtypeStruct((group_size, chan_count, rows, length), jnp.bfloat16),
        in_specs=[whole] * 3,
        out_specs=whole,
        scratch_shapes=[
            pltpu.VMEM((block_len + tap_count, rows, chan_count), jnp.float32),
            pltpu.VMEM((chan_count // 128, block_len * rows, 128), jnp.float32),
            pltpu.VMEM((block_count, chan_count * rows, block_len), jnp.float32),
        ],
        compiler_params=pltpu.CompilerParams(vmem_limit_bytes=VMEM_BYTES),
        name="filter",
    )(volts, taps, table)

    spectra = spectra.reshape(wide_count, chan_local, rows, length)
    spectra = lax.all_to_all(spectra, "wide", 0, 0, tiled=True)

    wide_index = lax.axis_index("wide")
    group = lax.axis_index("sec") * narrow_count + lax.axis_index("narrow")
    member = wide_index // chan_groups
    sub = group * group_size + member
    channels = (wide_index % chan_groups) * chan_local + jnp.arange(chan_local, dtype=jnp.int32)

    frequency = sub.astype(jnp.float32) + channels.astype(jnp.float32) / chan_count
    delays = jnp.repeat(beam_delays, 2, axis=1)
    phase = (TWO_PI * frequency)[:, None, None] * delays[None]
    norm = 1.0 / math.sqrt(station_count)
    cosine, sine = jnp.cos(phase) * norm, jnp.sin(phase) * norm
    is_real = jnp.arange(2 * station_count)[None, None, :] % 2 == 0
    weights = jnp.concatenate(
        [jnp.where(is_real, cosine, sine), jnp.where(is_real, -sine, cosine)], axis=1
    ).astype(jnp.bfloat16)

    span = 2 * SEG
    bins = jnp.arange(span, dtype=jnp.int32)
    signed = jnp.where(bins < span // 2, bins, bins - span)
    dm_value = jnp.sum(jnp.where(jnp.arange(sub_count) == sub, dm_index, 0))
    phase_index = dm_value * signed[None, :] * (signed[None, :] + channels[:, None])
    angle_index = jnp.mod(
        phase_index[:, None, :] + 2 * bins[None, :, None] * bins[None, None, :], 2 * span
    )
    angles = angle_index.astype(jnp.float32) * (math.pi / span)
    kern = jnp.stack(
        [jnp.sum(jnp.cos(angles), axis=-1) / span, jnp.sum(jnp.sin(angles), axis=-1) / span],
        axis=1,
    ).astype(jnp.bfloat16)
    lag = jnp.mod(jnp.arange(block_len)[None, :] - bins[:, None], span)
    pick = (lag[None] == bins[:, None, None]).astype(jnp.bfloat16)
    kern = jnp.einsum("crd,dab->crab", kern, pick, preferred_element_type=jnp.float32)

    partial = pl.pallas_call(
        beam_kernel,
        out_shape=jax.ShapeDtypeStruct((block_count, beam_count, block_len), jnp.float32),
        in_specs=[whole] * 3,
        out_specs=whole,
        scratch_shapes=[pltpu.VMEM((block_count, wide_count * rows, block_len), jnp.float32)],
        compiler_params=pltpu.CompilerParams(vmem_limit_bytes=VMEM_BYTES),
        name="beams",
    )(spectra, weights, kern)

    partial = partial.reshape(source_count, beam_count // narrow_count, block_len)
    partial = lax.all_to_all(partial, together, 0, 0, tiled=True)
    slot_count = wide_count * SUBBAND_LIMIT
    slot_sub, filled = slot_tables(owners, slot_count)
    mine = filled & (slot_sub % group_size == member)
    outgoing = jnp.where(
        mine[:, None, None], jnp.take(partial, slot_sub // group_size, axis=0), 0.0
    )
    arrived = lax.all_to_all(outgoing, "wide", 0, 0, tiled=True)
    arrived = arrived.reshape(wide_count, SUBBAND_LIMIT, beam_count // narrow_count, block_len)
    return (jnp.sum(arrived, axis=0) / chan_count)[None]


def solution(mesh):
    placed = (P("sec", None, "wide", None, None, "narrow"), P(), P(), P("wide"), P(), P())
    return jax.shard_map(
        shards,
        mesh=mesh,
        in_specs=placed,
        out_specs=P("sec", "wide", "narrow", None),
        check_vma=False,
    )
```

time: 599 us -> 188 us (0.31); the launches traced: 589 us -> 186 us
  local copies, waits for them, and re-layouts: 176 us -> 10.6 us
  waiting for transfers between devices: 229 us -> 87.1 us
  matrix products: 83.3 us -> 0.23 us
  other arithmetic: 63 us -> 12.7 us
  blocking collectives: 0 us -> 22.5 us
  Pallas kernels: 0 us -> 22.2 us
  between operations: 14.8 us -> 4.07 us
    dot_general x4 -> x1, matrix products: 83.3 us -> 0.23 us  [shards(): jnp.einsum('crd,dab->crab', kern, pick, preferred_element_type=jnp.float32)]
    unnamed x2 -> x0, waiting for transfers between devices: 67.3 us -> none
    reshape x6 -> x2, local copies, waits for them, and re-layouts: 67.7 us -> 4.81 us  [the longest x1 4.11 us: shards(): volts = voltages.reshape(sub_count, rows, piece_len)]
    ppermute x2 -> x0, waiting for transfers between devices: 44.4 us -> none  [shifted_2(): lax.ppermute(value, axis, [(source, source + steps) for source in range(i...]
    slice x5 -> x1, local copies, waits for them, and re-layouts: 41.6 us -> 0.59 us  [shards(): station_shifts[s]]
    gather x14 -> x1, local copies, waits for them, and re-layouts: 32.7 us -> 0.63 us  [shards(): jnp.take(partial, slot_sub // group_size, axis=0)]
    all_to_all x2 -> x3, waiting for transfers between devices: 117 us -> 87.1 us  [the longest x1 39.9 us: shards(): spectra = lax.all_to_all(spectra, 'wide', 0, 0, tiled=True)]
    all_to_all x0 -> x1, blocking collectives: none -> 22.5 us  [shards(): arrived = lax.all_to_all(outgoing, 'wide', 0, 0, tiled=True)]
  transfers between devices with their start and end apart: 5 -> 3, of which waited for: 4 -> 3; matrix products, arithmetic and copies ran while one was open for 7% -> 8% of each run, Pallas kernels for 0% -> 0%
where the time goes in v1:
time: 188 us; the launch traced here: 186 us
  waiting for transfers between devices  87.1 us (46%)
  starting transfers between devices  26.7 us (14%)
  blocking collectives  22.5 us (12%)
  Pallas kernels  22.2 us (12%)
  other arithmetic  12.7 us (7%)
  local copies, waits for them, and re-layouts  10.6 us (6%)
  between operations  4.07 us (2%)
    all_to_all x1, waiting for transfers between devices, shards(): spectra = lax.all_to_all(spectra, 'wide', 0, 0, tiled=True)  39.9 us
    all_to_all x1, waiting for transfers between devices, shards(): volts = lax.all_to_all(volts, together, 0, 0, tiled=True)  38.7 us
    all_to_all x1, blocking collectives, shards(): arrived = lax.all_to_all(outgoing, 'wide', 0, 0, tiled=True)  22.5 us
    all_to_all x1, starting transfers between devices, shards(): spectra = lax.all_to_all(spectra, 'wide', 0, 0, tiled=True)  13.6 us
    pallas_call x1, Pallas kernels, shards(): pl.pallas_call(filter_kernel, out_shape=jax.ShapeDtypeStruct((group_size,...  11.9 us
    pallas_call x1, Pallas kernels, shards(): pl.pallas_call(beam_kernel, out_shape=jax.ShapeDtypeStruct((block_count,...  10.2 us
    all_to_all x1, waiting for transfers between devices, shards(): partial = lax.all_to_all(partial, together, 0, 0, tiled=True)  8.44 us
    all_to_all x1, starting transfers between devices, shards(): volts = lax.all_to_all(volts, together, 0, 0, tiled=True)  7.34 us
  transfers between devices with their start and end apart: 3, of which 3 were waited for; matrix products, arithmetic and copies ran while one was open for 8% of the time, Pallas kernels for 0%

profile of v1, /device:TPU:6, one launch (start us, length us, event | category | flops | bytes accessed | tf_op | source)
XLA Modules:
  0.0 186.1 jit_solution(11038404814949114284)
XLA Ops:
  0.0 4.1 %reshape.282 = bf16[32,8,4096]{2,1,0:T(8,128)(2,1)} reshape(bf16[1,32,2,2,2,4096]{5,4,3,2,1,0:T(2,128)(2,1)} %param.6) | data formatting | bytes 4194304 | tf_op jit(solution)/shard_map/reshape | solution.py:199
  4.1 0.0 copy-start.4
  4.1 0.0 copy-start.3
  4.1 7.3 %all-to-all-start = ((bf16[32,8,4096]{2,1,0:T(8,128)(2,1)}), bf16[32,8,4096]{2,1,0:T(8,128)(2,1)S(1)}, u32[]{:S(2)}, u32[]{:S(2)}) async-start(bf16[32,8,4096]{2,1,0:T(8,128)(2,1)} %reshape.282), calls=%async_computation | async-start | bytes 4194304 | tf_op jit(solution)/shard_map/all_to_all | solution.py:200
  11.5 0.0 copy-done.4
  11.5 0.6 fusion.35
  14.6 0.0 copy-done.3
  15.3 0.4 dynamic_update_slice.7
  16.3 0.4 dynamic_update_slice.6
  16.8 0.7 reshape.285.taps_ref
  17.5 0.1 iota_subtract_fusion
  17.5 2.3 %fusion.16 = (bf16[2,256,256]{2,1,0:T(8,128)(2,1)S(1)}, bf16[2,256,256]{2,1,0:T(8,128)(2,1)S(1)}, bf16[2,256,256]{2,1,0:T(8,128)(2,1)S(1)}) fusion(s32[2,256]{1,0:T(2,128)S(1)} %iota_subtract_fusion), kind=kLoop, calls=%fused_computation.31 | loop fusion | flops 2621440 | bytes 788480 | tf_op jit(solution)/shard_map/convert.11
  19.8 1.1 maximum_maximum_fusion.table_ref
  20.9 38.7 %all-to-all-done = bf16[32,8,4096]{2,1,0:T(8,128)(2,1)S(1)} async-done(((bf16[32,8,4096]{2,1,0:T(8,128)(2,1)}), bf16[32,8,4096]{2,1,0:T(8,128)(2,1)S(1)}, u32[]{:S(2)}, u32[]{:S(2)}) %all-to-all-start) | async-done | bytes 2097184 | tf_op jit(solution)/shard_map/all_to_all | solution.py:200
  59.6 0.0 copy-start.1
  59.6 1.3 copy-done.1
  60.9 11.9 %filter.1 = bf16[2,256,8,256]{3,2,1,0:T(8,128)(2,1)} custom-call(bf16[16,2,8,4096]{3,2,1,0:T(8,128)(2,1)} %bitcast.36, f32[17,8,256]{2,1,0:T(8,128)} %reshape.285.taps_ref, bf16[2,512,512]{2,1,0:T(8,128)(2,1)} %maximum_maximum_fusion.table_ref), custom_call_target="tpu_custom_call" | custom-call | tf_op jit(solution)/shard_map/filter/pallas_call | solution.py:229
  72.8 0.0 copy-start.2
  72.8 0.0 copy-start.5
  72.8 0.0 copy-start.6
  72.8 13.6 %all-to-all-start.1 = ((bf16[32,16,8,256]{3,2,1,0:T(8,128)(2,1)}), bf16[32,16,8,256]{3,2,1,0:T(8,128)(2,1)S(1)}, u32[]{:S(2)}, u32[]{:S(2)}) async-start(bf16[32,16,8,256]{3,2,1,0:T(8,128)(2,1)} %bitcast.35), calls=%async_computation.1 | async-start | bytes 4194304 | tf_op jit(solution)/shard_map/all_to_all | solution.py:244
  86.4 0.0 copy-done.2
  86.4 0.1 copy.11
  86.6 0.0 copy-done.5
  86.6 0.6 fusion.32
  87.2 0.6 compare_select_fusion.1
  87.9 0.1 add_multiply_fusion
  88.0 0.1 iota_multiply_fusion
  88.1 1.3 cosine_reduce_fusion
  89.3 0.2 fusion.14
  89.6 1.0 copy.12.kern_ref
  90.5 0.0 copy-done.6
  90.5 0.2 select_reduce_fusion.1
  90.7 0.1 select_reduce_fusion
  90.8 0.1 fusion.24
  90.9 4.2 %fusion.3 = (bf16[16,128,128]{2,1,0:T(8,128)(2,1)S(1)}, bf16[16,128,128]{2,1,0:T(8,128)(2,1)S(1)}) fusion(f32[128,128]{1,0:T(8,128)S(1)} %copy.11, f32[16]{0:T(128)S(1)} %add_multiply_fusion.1, pred[128]{0:T(512)(128)(4,1)S(1)} %fusion.31), kind=kLoop, calls=%fused_computation.6 | loop fusion | flops 2097152 | bytes 1114304 | tf_op jit(solution)/shard_map/convert.4
  95.1 1.1 pad_maximum_fusion.weights_ref
  96.2 39.9 %all-to-all-done.1.spectra_ref = bf16[32,16,8,256]{3,2,1,0:T(8,128)(2,1)S(1)} async-done(((bf16[32,16,8,256]{3,2,1,0:T(8,128)(2,1)}), bf16[32,16,8,256]{3,2,1,0:T(8,128)(2,1)S(1)}, u32[]{:S(2)}, u32[]{:S(2)}) %all-to-all-start.1) | async-done | bytes 2097184 | tf_op jit(solution)/shard_map/all_to_all | solution.py:244
  136.2 0.0 copy-start
  136.2 1.3 copy-done
  137.5 10.2 %beams.1 = f32[2,128,128]{2,1,0:T(8,128)} custom-call(bf16[32,16,8,256]{3,2,1,0:T(8,128)(2,1)} %copy-done, bf16[16,256,128]{2,1,0:T(8,128)(2,1)} %pad_maximum_fusion.weights_ref, f32[16,2,32,128]{3,2,1,0:T(8,128)} %copy.12.kern_ref), custom_call_target="tpu_custom_call" | custom-call | tf_op jit(solution)/shard_map/beams/pallas_call | solution.py:279
  147.7 5.8 %all-to-all-start.2 = ((f32[16,16,128]{2,1,0:T(8,128)}), f32[16,16,128]{2,1,0:T(8,128)S(1)}, u32[]{:S(2)}, u32[]{:S(2)}) async-start(f32[16,16,128]{2,1,0:T(8,128)} %bitcast.38), calls=%async_computation.2 | async-start | bytes 262144 | tf_op jit(solution)/shard_map/all_to_all | solution.py:290
  153.6 8.4 %all-to-all-done.2 = f32[16,16,128]{2,1,0:T(8,128)S(1)} async-done(((f32[16,16,128]{2,1,0:T(8,128)}), f32[16,16,128]{2,1,0:T(8,128)S(1)}, u32[]{:S(2)}, u32[]{:S(2)}) %all-to-all-start.2) | async-done | bytes 131104 | tf_op jit(solution)/shard_map/all_to_all | solution.py:290
  162.0 0.6 gather_fusion
  162.7 0.2 select_select_fusion
  162.9 22.5 %all_to_all.20 = f32[64,16,128]{2,1,0:T(8,128)S(1)} all-to-all(f32[64,16,128]{2,1,0:T(8,128)S(1)} %select_select_fusion), channel_id=1, replica_groups=mesh['sec'=2,'wide'=32,'narrow'=8] {'wide'}, dimensions={0} | all-to-all | bytes 1048576 | tf_op jit(solution)/shard_map/all_to_all | solution.py:297
  185.4 0.6 multiply_bitcast_fusion
  (20 shorter events, 0.3 us)
Async XLA Ops:
  4.1 7.4 %copy-start.4 = (s32[2]{0:T(128)S(1)}, s32[2]{0:T(128)}, u32[]{:S(2)}) copy-start(s32[2]{0:T(128)} %param.9) | copy-start | bytes 28
  4.1 10.5 %copy-start.3 = (f32[16,256]{1,0:T(8,128)S(1)}, f32[16,256]{1,0:T(8,128)}, u32[]{:S(2)}) copy-start(f32[16,256]{1,0:T(8,128)} %param.7) | copy-start | bytes 49156
  4.1 55.5 %all-to-all-start = ((bf16[32,8,4096]{2,1,0:T(8,128)(2,1)}), bf16[32,8,4096]{2,1,0:T(8,128)(2,1)S(1)}, u32[]{:S(2)}, u32[]{:S(2)}) async-start(bf16[32,8,4096]{2,1,0:T(8,128)(2,1)} %reshape.282), calls=%async_computation | async-start | bytes 4194304 | tf_op jit(solution)/shard_map/all_to_all | solution.py:200
  59.6 1.3 copy-start.1
  72.8 13.6 %copy-start.2 = (f32[128,64]{0,1:T(8,128)S(1)}, f32[128,64]{0,1:T(8,128)}, u32[]{:S(2)}) copy-start(f32[128,64]{0,1:T(8,128)} %param.8) | copy-start | bytes 98308
  72.8 13.8 %copy-start.5 = (s32[32]{0:T(128)S(1)}, s32[32]{0:T(128)}, u32[]{:S(2)}) copy-start(s32[32]{0:T(128)} %param.10) | copy-start | bytes 388
  72.8 17.7 %copy-start.6 = (s32[32]{0:T(128)S(1)}, s32[32]{0:T(128)}, u32[]{:S(2)}) copy-start(s32[32]{0:T(128)} %param.11) | copy-start | bytes 388
  72.8 63.3 %all-to-all-start.1 = ((bf16[32,16,8,256]{3,2,1,0:T(8,128)(2,1)}), bf16[32,16,8,256]{3,2,1,0:T(8,128)(2,1)S(1)}, u32[]{:S(2)}, u32[]{:S(2)}) async-start(bf16[32,16,8,256]{3,2,1,0:T(8,128)(2,1)} %bitcast.35), calls=%async_computation.1 | async-start | bytes 4194304 | tf_op jit(solution)/shard_map/all_to_all | solution.py:244
  136.2 1.4 copy-start
  147.7 14.3 %all-to-all-start.2 = ((f32[16,16,128]{2,1,0:T(8,128)}), f32[16,16,128]{2,1,0:T(8,128)S(1)}, u32[]{:S(2)}, u32[]{:S(2)}) async-start(f32[16,16,128]{2,1,0:T(8,128)} %bitcast.38), calls=%async_computation.2 | async-start | bytes 262144 | tf_op jit(solution)/shard_map/all_to_all | solution.py:290

commit v2 on v1

v2 whole, which is shorter than its diff:
```python
import math

import jax
import jax.numpy as jnp
from jax import lax
from jax.experimental import pallas as pl
from jax.experimental.pallas import tpu as pltpu
from jax.sharding import PartitionSpec as P

SEG = 16
SUBBAND_LIMIT = 2
TWO_PI = 2.0 * math.pi
VMEM_BYTES = 56 * 1024 * 1024
T_BLOCK = 8


def slot_tables(owners, slot_count):
    sub_count = owners.shape[0]
    order = jnp.arange(sub_count, dtype=jnp.int32)
    same = owners[:, None] == owners[None, :]
    before = order[None, :] < order[:, None]
    rank = jnp.sum(jnp.where(same & before, 1, 0), axis=1).astype(jnp.int32)
    lookup = owners * SUBBAND_LIMIT + rank
    slots = jnp.arange(slot_count, dtype=jnp.int32)
    match = lookup[None, :] == slots[:, None]
    subband = jnp.sum(jnp.where(match, order[None, :], 0), axis=1)
    return subband, jnp.any(match, axis=1)


def filter_body(place, sources, taps_ref, table_ref, out_ref, frames, filtered, packed):
    tap_count, rows, chan_count = taps_ref.shape
    block_count, row_count, _ = packed.shape
    piece_frames = sources[0].shape[-1] // chan_count
    frame_count = filtered.shape[2] // rows
    station_count = table_ref.shape[0]
    member_count = rows // (2 * station_count)
    halves = chan_count // 128
    quad = 2 * station_count
    frames[frame_count:] = jnp.zeros_like(frames[frame_count:])

    def one(block, carry):
        for number, source in enumerate(sources):
            at, start = place(number, block)
            for frame in range(piece_frames):
                frames[start + frame] = source[
                    at, :, frame * chan_count : (frame + 1) * chan_count
                ].astype(jnp.float32)
        for half in range(halves):
            lanes = slice(half * 128, half * 128 + 128)
            taps = [taps_ref[tap, :, lanes] for tap in range(tap_count)]

            def some(step, inner):
                start = pl.multiple_of(step * T_BLOCK, T_BLOCK)
                loaded = [frames[start + i, :, lanes] for i in range(T_BLOCK + tap_count - 1)]
                for i in range(T_BLOCK):
                    total = taps[0] * loaded[i]
                    for tap in range(1, tap_count):
                        total = total + taps[tap] * loaded[i + tap]
                    at = pl.multiple_of((start + i) * rows, rows)
                    filtered[block, half, pl.ds(at, rows), :] = total
                return inner

            lax.fori_loop(0, frame_count // T_BLOCK, some, 0)
        return carry

    lax.fori_loop(0, block_count, one, 0)

    for member in range(member_count):
        for station in range(station_count):
            parts = []
            for block in range(block_count):
                pair = [
                    filtered[
                        block,
                        half,
                        pl.ds((member * station_count + station) * 2 + r, frame_count, stride=rows),
                        :,
                    ].astype(jnp.bfloat16)
                    for r in range(2)
                    for half in range(halves)
                ]
                parts.append(jnp.concatenate(pair, axis=1))
            spectra = lax.dot_general(
                table_ref[station],
                jnp.concatenate(parts, axis=0),
                (((1,), (1,)), ((), ())),
                preferred_element_type=jnp.float32,
            )
            for r in range(2):
                for block in range(block_count):
                    packed[block, pl.ds(station * 2 + r, chan_count, stride=quad), :] = spectra[
                        r * chan_count : (r + 1) * chan_count,
                        block * frame_count : (block + 1) * frame_count,
                    ]
        for block in range(block_count):
            out_ref[member, :, block * frame_count : (block + 1) * frame_count] = packed[
                block
            ].astype(jnp.bfloat16)


def filter_first(volts_ref, after_ref, *refs):
    taps_ref, packed = refs[0], refs[-1]
    pieces = volts_ref.shape[0] // packed.shape[0]
    step = volts_ref.shape[-1] // taps_ref.shape[-1]

    def place(piece, block):
        return block * pieces + piece, piece * step

    filter_body(place, [volts_ref] * pieces, *refs)


def filter_second(where_ref, *refs):
    pieces = len(refs) - 6
    sources, refs = refs[:pieces], refs[pieces:]
    step = sources[0].shape[-1] // refs[0].shape[-1]

    def place(distance, block):
        piece = lax.rem(where_ref[1] + (pieces - distance), pieces)
        return lax.rem(block + where_ref[0], 2), piece * step

    filter_body(place, sources, *refs)


def turn_kernel(where_ref, pair_ref, after_ref, *refs):
    outs, sems = refs[:-1], refs[-1]
    pieces = len(outs)
    copies = []
    for distance, out in enumerate(outs):
        piece = lax.rem(where_ref[1] + distance, pieces)
        copies.append(pltpu.make_async_copy(pair_ref.at[:, piece], out, sems.at[distance]))
    for copy in copies:
        copy.start()
    for copy in copies:
        copy.wait()


def beam_body(spectra_ref, weights_ref, kern_ref, power_ref, held):
    source_count, row_count, length = spectra_ref.shape
    block_count, beam_count, block_len = power_ref.shape
    chan_local = weights_ref.shape[0]
    quad = row_count // chan_local
    step_chans = held.shape[1] // (source_count * quad)
    step_rows = step_chans * quad
    span = 2 * SEG
    from_seg = lax.broadcasted_iota(jnp.int32, (block_len, block_len), 0) // SEG
    to_seg = lax.broadcasted_iota(jnp.int32, (block_len, block_len), 1) // SEG
    own_mask = (from_seg == to_seg) | (from_seg + 1 == to_seg)
    cross_mask = (from_seg == block_len // SEG - 1) & (to_seg == 0)

    def one(step, carry):
        at = pl.multiple_of(step * step_rows, step_rows)
        for block in range(block_count):
            held[block] = (
                spectra_ref[:, pl.ds(at, step_rows), block * block_len : (block + 1) * block_len]
                .astype(jnp.float32)
                .reshape(source_count * step_rows, block_len)
            )
        for inner in range(step_chans):
            chan = step * step_chans + inner
            inputs = jnp.concatenate(
                [
                    jnp.concatenate(
                        [
                            held[
                                block, pl.ds(inner * quad + q, source_count, stride=step_rows), :
                            ].astype(jnp.bfloat16)
                            for q in range(quad)
                        ],
                        axis=0,
                    )
                    for block in range(block_count)
                ],
                axis=1,
            )
            beams = jnp.dot(
                weights_ref[chan], inputs, preferred_element_type=jnp.float32
            ).astype(jnp.bfloat16)
            tiled = [
                jnp.concatenate([kern_ref[chan, part]] * (block_len // span), axis=0)
                for part in range(2)
            ]

            def matrix(mask):
                real, imag = [jnp.where(mask, part, 0.0) for part in tiled]
                return jnp.concatenate(
                    [
                        jnp.concatenate([real, imag], axis=1),
                        jnp.concatenate([-imag, real], axis=1),
                    ],
                    axis=0,
                ).astype(jnp.bfloat16)

            series = [
                jnp.concatenate(
                    [
                        beams[part * beam_count : (part + 1) * beam_count, low : low + block_len]
                        for part in range(2)
                    ],
                    axis=1,
                )
                for low in range(0, length, block_len)
            ]
            own = jnp.dot(
                jnp.concatenate(series, axis=0),
                matrix(own_mask),
                preferred_element_type=jnp.float32,
            )
            cross = jnp.dot(series[0], matrix(cross_mask), preferred_element_type=jnp.float32)
            clean = [own[:beam_count], own[beam_count:] + cross]
            for block in range(block_count):
                square = clean[block] * clean[block]
                power_ref[block] += square[:, :block_len] + square[:, block_len:]
        return carry

    lax.fori_loop(0, chan_local // step_chans, one, 0)


def beam_first(spectra_ref, weights_ref, kern_ref, power_ref, held):
    power_ref[...] = jnp.zeros_like(power_ref)
    beam_body(spectra_ref, weights_ref, kern_ref, power_ref, held)


def beam_second(spectra_ref, weights_ref, kern_ref, before_ref, power_ref, held):
    power_ref[...] = before_ref[...]
    beam_body(spectra_ref, weights_ref, kern_ref, power_ref, held)


def shards(voltages, prototype, beam_delays, station_shifts, dm_index, owners):
    wide_count = lax.axis_size("wide")
    source_count = lax.axis_size("sec") * lax.axis_size("narrow")
    narrow_count = lax.axis_size("narrow")
    block_count = lax.axis_size("sec")
    _, sub_count, station_local, pol_count, _, piece_len = voltages.shape
    tap_count, chan_count = prototype.shape
    beam_count, station_count = beam_delays.shape
    group_size = sub_count // source_count
    rows = group_size * station_local * 2
    quad = station_local * 2
    chan_local = group_size * chan_count // wide_count
    chan_groups = chan_count // chan_local
    block_len = piece_len * narrow_count // chan_count
    length = block_count * block_len
    together = ("sec", "narrow")
    whole = pl.BlockSpec(memory_space=pltpu.VMEM)
    anywhere = pl.BlockSpec(memory_space=pl.ANY)
    scalars = pl.BlockSpec(memory_space=pltpu.SMEM)
    params = pltpu.CompilerParams(vmem_limit_bytes=VMEM_BYTES)
    where = jnp.stack([lax.axis_index("sec"), lax.axis_index("narrow")]).astype(jnp.int32)

    first, second = [
        voltages[0, :, :, pol].reshape(source_count, rows, piece_len) for pol in range(pol_count)
    ]
    first = lax.all_to_all(first, together, 0, 0, tiled=True)

    second = second.reshape(block_count, narrow_count, rows, piece_len)
    mine = lax.dynamic_index_in_dim(second, where[0], 0, keepdims=False)
    theirs = lax.dynamic_index_in_dim(second, 1 - where[0], 0, keepdims=False)
    pair = jnp.stack([mine, lax.ppermute(theirs, "sec", [(0, 1), (1, 0)])])
    turned = pl.pallas_call(
        turn_kernel,
        out_shape=[
            jax.ShapeDtypeStruct((block_count, rows, piece_len), jnp.bfloat16)
        ] * narrow_count,
        in_specs=[scalars, anywhere, anywhere],
        out_specs=[anywhere] * narrow_count,
        scratch_shapes=[pltpu.SemaphoreType.DMA((narrow_count,))],
        name="turn",
    )(where, pair, first)
    moved = [turned[0]] + [
        lax.ppermute(
            turned[distance],
            "narrow",
            [(i, (i + distance) % narrow_count) for i in range(narrow_count)],
        )
        for distance in range(1, narrow_count)
    ]

    flat = prototype.reshape(-1)
    taps = jnp.stack(
        [
            lax.dynamic_update_slice(
                jnp.zeros((tap_count + 1) * chan_count, jnp.float32), flat, (station_shifts[s],)
            ).reshape(tap_count + 1, chan_count)
            for s in range(station_local)
        ],
        axis=1,
    )
    taps = jnp.tile(jnp.repeat(taps, 2, axis=1), (1, group_size, 1))
    ids = jnp.arange(chan_count, dtype=jnp.int32)
    turn = jnp.mod(
        ids[None, :, None] * (ids[None, None, :] - station_shifts[:, None, None]), chan_count
    )
    angle = turn.astype(jnp.float32) * (TWO_PI / chan_count)
    scale = 1.0 / math.sqrt(chan_count)
    cosine, sine = jnp.cos(angle) * scale, jnp.sin(angle) * scale
    table = jnp.concatenate(
        [
            jnp.concatenate([cosine, sine], axis=2),
            jnp.concatenate([-sine, cosine], axis=2),
        ],
        axis=1,
    ).astype(jnp.bfloat16)
    filter_args = dict(
        out_shape=jax.ShapeDtypeStruct((group_size, chan_count * quad, length), jnp.bfloat16),
        out_specs=whole,
        scratch_shapes=[
            pltpu.VMEM((block_len + tap_count, rows, chan_count), jnp.float32),
            pltpu.VMEM((block_count, chan_count // 128, block_len * rows, 128), jnp.float32),
            pltpu.VMEM((block_count, chan_count * quad, block_len), jnp.float32),
        ],
        compiler_params=params,
    )

    def to_stations(spectra):
        spectra = spectra.reshape(wide_count, chan_local * quad, length)
        return lax.all_to_all(spectra, "wide", 0, 0, tiled=True)

    spectra_first = to_stations(
        pl.pallas_call(
            filter_first,
            in_specs=[whole, anywhere, whole, whole],
            name="filter0",
            **filter_args,
        )(first, turned[0], taps, table)
    )
    spectra_second = to_stations(
        pl.pallas_call(
            filter_second,
            in_specs=[scalars] + [whole] * (narrow_count + 2),
            name="filter1",
            **filter_args,
        )(where, *moved, taps, table)
    )

    wide_index = lax.axis_index("wide")
    group = lax.axis_index("sec") * narrow_count + lax.axis_index("narrow")
    member = wide_index // chan_groups
    sub = group * group_size + member
    channels = (wide_index % chan_groups) * chan_local + jnp.arange(chan_local, dtype=jnp.int32)

    frequency = sub.astype(jnp.float32) + channels.astype(jnp.float32) / chan_count
    delays = jnp.transpose(beam_delays.reshape(beam_count, wide_count, station_local), (0, 2, 1))
    delays = jnp.repeat(delays, 2, axis=1).reshape(beam_count, 2 * station_count)
    phase = (TWO_PI * frequency)[:, None, None] * delays[None]
    norm = 1.0 / math.sqrt(station_count)
    cosine, sine = jnp.cos(phase) * norm, jnp.sin(phase) * norm
    is_real = jnp.arange(2 * station_count)[None, None, :] // wide_count % 2 == 0
    weights = jnp.concatenate(
        [jnp.where(is_real, cosine, sine), jnp.where(is_real, -sine, cosine)], axis=1
    ).astype(jnp.bfloat16)

    span = 2 * SEG
    bins = jnp.arange(span, dtype=jnp.int32)
    signed = jnp.where(bins < span // 2, bins, bins - span)
    dm_value = jnp.sum(jnp.where(jnp.arange(sub_count) == sub, dm_index, 0))
    phase_index = dm_value * signed[None, :] * (signed[None, :] + channels[:, None])
    angle_index = jnp.mod(
        phase_index[:, None, :] + 2 * bins[None, :, None] * bins[None, None, :], 2 * span
    )
    angles = angle_index.astype(jnp.float32) * (math.pi / span)
    kern = jnp.stack(
        [jnp.sum(jnp.cos(angles), axis=-1) / span, jnp.sum(jnp.sin(angles), axis=-1) / span],
        axis=1,
    ).astype(jnp.bfloat16)
    lag = jnp.mod(jnp.arange(block_len)[None, :] - bins[:, None], span)
    pick = (lag[None] == bins[:, None, None]).astype(jnp.bfloat16)
    kern = jnp.einsum("crd,dab->crab", kern, pick, preferred_element_type=jnp.float32)

    beam_args = dict(
        out_shape=jax.ShapeDtypeStruct((block_count, beam_count, block_len), jnp.float32),
        out_specs=whole,
        scratch_shapes=[pltpu.VMEM((block_count, wide_count * 8, block_len), jnp.float32)],
        compiler_params=params,
    )
    partial = pl.pallas_call(beam_first, in_specs=[whole] * 3, name="beams0", **beam_args)(
        spectra_first, weights, kern
    )
    partial = pl.pallas_call(beam_second, in_specs=[whole] * 4, name="beams1", **beam_args)(
        spectra_second, weights, kern, partial
    )

    partial = partial.reshape(source_count, beam_count // narrow_count, block_len)
    partial = lax.all_to_all(partial, together, 0, 0, tiled=True)
    slot_count = wide_count * SUBBAND_LIMIT
    slot_sub, filled = slot_tables(owners, slot_count)
    mine = filled & (slot_sub % group_size == member)
    outgoing = jnp.where(
        mine[:, None, None], jnp.take(partial, slot_sub // group_size, axis=0), 0.0
    )
    arrived = lax.all_to_all(outgoing, "wide", 0, 0, tiled=True)
    arrived = arrived.reshape(wide_count, SUBBAND_LIMIT, beam_count // narrow_count, block_len)
    return (jnp.sum(arrived, axis=0) / chan_count)[None]


def solution(mesh):
    placed = (P("sec", None, "wide", None, None, "narrow"), P(), P(), P("wide"), P(), P())
    return jax.shard_map(
        shards,
        mesh=mesh,
        in_specs=placed,
        out_specs=P("sec", "wide", "narrow", None),
        check_vma=False,
    )
```

time: 188 us -> 227 us (1.21)
  waiting for transfers between devices: 87.1 us -> 43.1 us
  starting transfers between devices: 26.7 us -> 66.5 us
  Pallas kernels: 22.2 us -> 61.8 us
    all_to_all x2 -> x3, waiting for transfers between devices: 78.6 us -> 24.4 us  [the longest x2 13 us: to_stations(): return lax.all_to_all(spectra, 'wide', 0, 0, tiled=True)]
    pallas_call x2 -> x5, Pallas kernels: 22.2 us -> 61.8 us  [the longest x1 33.6 us: shards(): pl.pallas_call(turn_kernel, out_shape=[jax.ShapeDtypeStruct((block_count,...]
    ppermute x0 -> x8, starting transfers between devices: none -> 30.5 us  [the longest x7 28.2 us: shards(): lax.ppermute(turned[distance], 'narrow', [(i, (i + distance) % narrow_cou...]
    ppermute x0 -> x8, waiting for transfers between devices: none -> 10.3 us  [the longest x7 10.3 us: shards(): lax.ppermute(turned[distance], 'narrow', [(i, (i + distance) % narrow_cou...]
    all_to_all x2 -> x3, starting transfers between devices: 20.9 us -> 30.4 us  [the longest x2 23.2 us: to_stations(): return lax.all_to_all(spectra, 'wide', 0, 0, tiled=True)]
    reshape x2 -> x1, local copies, waits for them, and re-layouts: 4.81 us -> 0.01 us  [shards(): beam_delays.reshape(beam_count, wide_count, station_local)]
    slice x0 -> x1, local copies, waits for them, and re-layouts: none -> 3.44 us  [shards(): voltages[0, :, :, pol].reshape(source_count, rows, piece_len)]
    another operation x2 -> x7, local copies, waits for them, and re-layouts: 0.01 us -> 2.45 us  [the longest x1 1.22 us: shards(): voltages[0, :, :, pol].reshape(source_count, rows, piece_len)]
  transfers between devices with their start and end apart: 3 -> 12, of which waited for: 3 -> 6; matrix products, arithmetic and copies ran while one was open for 8% -> 8% of each run, Pallas kernels for 0% -> 6%
where the time goes in v2:
time: 227 us; the launch traced here: 225 us
  starting transfers between devices  66.5 us (29%)
  Pallas kernels  61.8 us (27%)
  waiting for transfers between devices  43.1 us (19%)
  blocking collectives  21.6 us (10%)
  other arithmetic  14.5 us (6%)
  local copies, waits for them, and re-layouts  12.6 us (6%)
  between operations  4.48 us (2%)
    pallas_call x1, Pallas kernels, shards(): pl.pallas_call(turn_kernel, out_shape=[jax.ShapeDtypeStruct((block_count,...  33.6 us
    ppermute x7, starting transfers between devices, shards(): lax.ppermute(turned[distance], 'narrow', [(i, (i + distance) % narrow_cou...  28.2 us
    all_to_all x2, starting transfers between devices, to_stations(): return lax.all_to_all(spectra, 'wide', 0, 0, tiled=True)  23.2 us
    all_to_all x1, blocking collectives, shards(): arrived = lax.all_to_all(outgoing, 'wide', 0, 0, tiled=True)  21.6 us
    all_to_all x2, waiting for transfers between devices, to_stations(): return lax.all_to_all(spectra, 'wide', 0, 0, tiled=True)  13 us
    all_to_all x1, waiting for transfers between devices, shards(): first = lax.all_to_all(first, together, 0, 0, tiled=True)  11.4 us
    ppermute x7, waiting for transfers between devices, shards(): lax.ppermute(turned[distance], 'narrow', [(i, (i + distance) % narrow_cou...  10.3 us
    all_to_all x1, waiting for transfers between devices, shards(): partial = lax.all_to_all(partial, together, 0, 0, tiled=True)  8.44 us
  transfers between devices with their start and end apart: 12, of which 6 were waited for; matrix products, arithmetic and copies ran while one was open for 8% of the time, Pallas kernels for 6%

profile of v2, /device:TPU:6, one launch (start us, length us, event | category | flops | bytes accessed | tf_op | source)
XLA Modules:
  0.0 224.9 jit_solution(4020949542858020438)
XLA Ops:
  0.0 3.4 %fusion.36 = (bf16[1,32,2,1,2,4096]{5,4,3,2,1,0:T(2,128)(2,1)S(1)}, bf16[1,32,2,1,2,4096]{5,4,3,2,1,0:T(2,128)(2,1)S(1)}) fusion(bf16[1,32,2,2,2,4096]{5,4,3,2,1,0:T(2,128)(2,1)} %param.6), kind=kLoop, calls=%fused_computation.104 | loop fusion | bytes 4194304 | tf_op jit(solution)/shard_map/slice | solution.py:251
  3.5 1.2 reshape_squeeze.3
  4.7 7.2 %all-to-all-start = ((bf16[16,8,4096]{2,1,0:T(8,128)(2,1)}), bf16[16,8,4096]{2,1,0:T(8,128)(2,1)S(1)}, u32[]{:S(2)}, u32[]{:S(2)}) async-start(bf16[16,8,4096]{2,1,0:T(8,128)(2,1)} %reshape_squeeze.3), calls=%async_computation | async-start | bytes 2097152 | tf_op jit(solution)/shard_map/all_to_all | solution.py:253
  11.9 0.0 copy-start.12
  11.9 0.0 copy-start.11
  11.9 0.4 reshape_reshape_squeeze.3
  12.4 0.9 constant_dynamic-slice_fusion
  13.3 2.3 %collective-permute-start = (bf16[8,8,4096]{2,1,0:T(8,128)(2,1)}, bf16[8,8,4096]{2,1,0:T(8,128)(2,1)S(1)}, u32[]{:S(2)}, u32[]{:S(2)}) collective-permute-start(bf16[8,8,4096]{2,1,0:T(8,128)(2,1)} %get-tuple-element.26), channel_id=1, source_target_pairs={{0,256},{256,0},{1,257},{257,1},{2,258},{258,2},{3,259},{259,3},{4... | collective-permute-start | bytes 1572872 | tf_op jit(solution)/shard_map/ppermute | solution.py:258
  15.6 0.6 fusion.37
  19.5 0.4 dynamic_update_slice.6
  20.5 0.4 dynamic_update_slice.7
  20.9 0.1 iota_subtract_fusion
  21.1 0.1 tile.10
  21.2 0.7 tile.12.refs_8_.refs_0_
  21.9 0.6 pad_add_fusion.where_ref
  22.5 2.3 %fusion.16 = (bf16[2,256,256]{2,1,0:T(8,128)(2,1)S(1)}, bf16[2,256,256]{2,1,0:T(8,128)(2,1)S(1)}, bf16[2,256,256]{2,1,0:T(8,128)(2,1)S(1)}) fusion(s32[2,256]{1,0:T(2,128)S(1)} %iota_subtract_fusion), kind=kLoop, calls=%fused_computation.33 | loop fusion | flops 2621440 | bytes 788480 | tf_op jit(solution)/shard_map/convert.11
  24.8 1.1 maximum_maximum_fusion.refs_9_.refs_1_
  25.9 0.0 collective-permute-done
  25.9 1.1 pad_maximum_fusion.pair_ref
  26.9 11.4 %all-to-all-done.after_ref.volts_ref = bf16[16,8,4096]{2,1,0:T(8,128)(2,1)S(1)} async-done(((bf16[16,8,4096]{2,1,0:T(8,128)(2,1)}), bf16[16,8,4096]{2,1,0:T(8,128)(2,1)S(1)}, u32[]{:S(2)}, u32[]{:S(2)}) %all-to-all-start) | async-done | bytes 1048608 | tf_op jit(solution)/shard_map/all_to_all | solution.py:253
  38.3 1.0 copy-done
  39.3 33.6 %turn.1 = (bf16[2,8,4096]{2,1,0:T(8,128)(2,1)}, bf16[2,8,4096]{2,1,0:T(8,128)(2,1)}, bf16[2,8,4096]{2,1,0:T(8,128)(2,1)}, bf16[2,8,4096]{2,1,0:T(8,128)(2,1)}, b...) custom-call(s32[2]{0:T(128)} %pad_add_fusion.where_ref, ...), custom_call_target="tpu_custom_call" | custom-call | tf_op jit(solution)/shard_map/turn/pallas_call | solution.py:259
  72.9 0.0 copy-start.20
  73.0 6.7 %filter0.1 = bf16[2,1024,256]{2,1,0:T(8,128)(2,1)} custom-call(bf16[16,8,4096]{2,1,0:T(8,128)(2,1)} %copy-done, bf16[2,8,4096]{2,1,0:T(8,128)(2,1)} %get-tuple-element.13.refs_0_.after_ref, f32[17,8,256]{2,1,0:T(8,128)} %tile.12.refs_8_.refs_0_, bf16[2,512,512]{2,1,0:T(8,128)(2,1)} %maximum_maximum_fusion.refs_9_.refs_1_), custom_call_target="tpu_custom_call" | custom-call | tf_op jit(solution)/shard_map/filter0/pallas_call | solution.py:319
  79.7 13.4 %all-to-all-start.2 = ((bf16[32,64,256]{2,1,0:T(8,128)(2,1)}), bf16[32,64,256]{2,1,0:T(8,128)(2,1)S(1)}, u32[]{:S(2)}, u32[]{:S(2)}) async-start(bf16[32,64,256]{2,1,0:T(8,128)(2,1)} %bitcast.44), calls=%async_computation.2 | async-start | bytes 2097152 | tf_op jit(solution)/shard_map/all_to_all | solution.py:316
  93.1 0.6 fusion.32
  93.8 0.6 compare_select_fusion.1
  94.4 0.1 iota_multiply_fusion
  94.5 4.2 %collective-permute-start.1 = (bf16[2,8,4096]{2,1,0:T(8,128)(2,1)S(1)}, bf16[2,8,4096]{2,1,0:T(8,128)(2,1)S(1)}, u32[]{:S(2)}, u32[]{:S(2)}) collective-permute-start(bf16[2,8,4096]{2,1,0:T(8,128)(2,1)S(1)} %copy-done.19), channel_id=1, source_target_pairs={{0,1},{1,2},{2,3},{3,4},{4,5},{5,6},{6,7},{7,0},{8,9},{9,10},{10,1... | collective-permute-start | bytes 393224 | tf_op jit(solution)/shard_map/ppermute | solution.py:270
  98.8 3.8 %collective-permute-start.2 = (bf16[2,8,4096]{2,1,0:T(8,128)(2,1)S(1)}, bf16[2,8,4096]{2,1,0:T(8,128)(2,1)S(1)}, u32[]{:S(2)}, u32[]{:S(2)}) collective-permute-start(bf16[2,8,4096]{2,1,0:T(8,128)(2,1)S(1)} %copy-done.18), channel_id=1, source_target_pairs={{0,2},{1,3},{2,4},{3,5},{4,6},{5,7},{6,0},{7,1},{8,10},{9,11},{10,... | collective-permute-start | bytes 393224 | tf_op jit(solution)/shard_map/ppermute | solution.py:270
  102.6 0.1 add_multiply_fusion
  102.6 4.3 %collective-permute-start.3 = (bf16[2,8,4096]{2,1,0:T(8,128)(2,1)S(1)}, bf16[2,8,4096]{2,1,0:T(8,128)(2,1)S(1)}, u32[]{:S(2)}, u32[]{:S(2)}) collective-permute-start(bf16[2,8,4096]{2,1,0:T(8,128)(2,1)S(1)} %copy-done.17), channel_id=1, source_target_pairs={{0,3},{1,4},{2,5},{3,6},{4,7},{5,0},{6,1},{7,2},{8,11},{9,12},{10,... | collective-permute-start | bytes 393224 | tf_op jit(solution)/shard_map/ppermute | solution.py:270
  106.9 3.6 %collective-permute-start.4 = (bf16[2,8,4096]{2,1,0:T(8,128)(2,1)S(1)}, bf16[2,8,4096]{2,1,0:T(8,128)(2,1)S(1)}, u32[]{:S(2)}, u32[]{:S(2)}) collective-permute-start(bf16[2,8,4096]{2,1,0:T(8,128)(2,1)S(1)} %copy-done.16), channel_id=1, source_target_pairs={{0,4},{1,5},{2,6},{3,7},{4,0},{5,1},{6,2},{7,3},{8,12},{9,13},{10,... | collective-permute-start | bytes 393224 | tf_op jit(solution)/shard_map/ppermute | solution.py:270
  110.6 4.7 %collective-permute-start.5 = (bf16[2,8,4096]{2,1,0:T(8,128)(2,1)S(1)}, bf16[2,8,4096]{2,1,0:T(8,128)(2,1)S(1)}, u32[]{:S(2)}, u32[]{:S(2)}) collective-permute-start(bf16[2,8,4096]{2,1,0:T(8,128)(2,1)S(1)} %copy-done.15), channel_id=1, source_target_pairs={{0,5},{1,6},{2,7},{3,0},{4,1},{5,2},{6,3},{7,4},{8,13},{9,14},{10,... | collective-permute-start | bytes 393224 | tf_op jit(solution)/shard_map/ppermute | solution.py:270
  115.3 0.0 collective-permute-done.1.refs_1_
  115.3 4.6 %collective-permute-start.6 = (bf16[2,8,4096]{2,1,0:T(8,128)(2,1)S(1)}, bf16[2,8,4096]{2,1,0:T(8,128)(2,1)S(1)}, u32[]{:S(2)}, u32[]{:S(2)}) collective-permute-start(bf16[2,8,4096]{2,1,0:T(8,128)(2,1)S(1)} %copy-done.14), channel_id=1, source_target_pairs={{0,6},{1,7},{2,0},{3,1},{4,2},{5,3},{6,4},{7,5},{8,14},{9,15},{10,... | collective-permute-start | bytes 393224 | tf_op jit(solution)/shard_map/ppermute | solution.py:270
  119.9 0.0 collective-permute-done.2.refs_2_
  119.9 3.0 %collective-permute-start.7 = (bf16[2,8,4096]{2,1,0:T(8,128)(2,1)S(1)}, bf16[2,8,4096]{2,1,0:T(8,128)(2,1)S(1)}, u32[]{:S(2)}, u32[]{:S(2)}) collective-permute-start(bf16[2,8,4096]{2,1,0:T(8,128)(2,1)S(1)} %copy-done.13), channel_id=1, source_target_pairs={{0,7},{1,0},{2,1},{3,2},{4,3},{5,4},{6,5},{7,6},{8,15},{9,8},{10,9... | collective-permute-start | bytes 393224 | tf_op jit(solution)/shard_map/ppermute | solution.py:270
  122.9 1.3 cosine_reduce_fusion
  124.2 0.0 collective-permute-done.4.refs_4_
  124.2 2.8 %collective-permute-done.5.refs_5_ = bf16[2,8,4096]{2,1,0:T(8,128)(2,1)S(1)} collective-permute-done((bf16[2,8,4096]{2,1,0:T(8,128)(2,1)S(1)}, bf16[2,8,4096]{2,1,0:T(8,128)(2,1)S(1)}, u32[]{:S(2)}, u32[]{:S(2)}) %collective-permute-start.5) | collective-permute-done | bytes 131104 | tf_op jit(solution)/shard_map/ppermute | solution.py:270
  127.0 6.0 %collective-permute-done.6.refs_6_ = bf16[2,8,4096]{2,1,0:T(8,128)(2,1)S(1)} collective-permute-done((bf16[2,8,4096]{2,1,0:T(8,128)(2,1)S(1)}, bf16[2,8,4096]{2,1,0:T(8,128)(2,1)S(1)}, u32[]{:S(2)}, u32[]{:S(2)}) %collective-permute-start.6) | collective-permute-done | bytes 131104 | tf_op jit(solution)/shard_map/ppermute | solution.py:270
  133.1 1.5 collective-permute-done.7.refs_7_
  134.6 0.6 copy-done.9
  135.2 6.8 %filter1.1 = bf16[2,1024,256]{2,1,0:T(8,128)(2,1)} custom-call(s32[2]{0:T(128)} %pad_add_fusion.where_ref, bf16[2,8,4096]{2,1,0:T(8,128)(2,1)} %get-tuple-element.13.refs_0_.after_ref, bf16[2,8,4096]{2,1,0:T(8,128)(2,1)} %copy-done.3, bf16[2,8,4096]{2,1,0:T(8,128)(2,1)} %copy-done.4, bf16[2,8,4096]{2,1,0:T(8,128)(2,1)} %copy-done.5, ...), custom_call_target="tpu_custom_call" | custom-call | tf_op jit(solution)/shard_map/filter1/pallas_call | solution.py:327
  142.0 9.8 %all-to-all-start.1 = ((bf16[32,64,256]{2,1,0:T(8,128)(2,1)}), bf16[32,64,256]{2,1,0:T(8,128)(2,1)S(1)}, u32[]{:S(2)}, u32[]{:S(2)}) async-start(bf16[32,64,256]{2,1,0:T(8,128)(2,1)} %bitcast.45), calls=%async_computation.1 | async-start | bytes 2097152 | tf_op jit(solution)/shard_map/all_to_all | solution.py:316
  151.8 0.1 copy.15
  152.0 0.2 fusion.14
  152.2 1.0 copy.17.kern_ref
  153.2 0.2 select_reduce_fusion.1
  153.4 0.1 select_reduce_fusion
  153.5 0.1 fusion.24
  153.6 4.2 %fusion.3 = (bf16[16,128,128]{2,1,0:T(8,128)(2,1)S(1)}, bf16[16,128,128]{2,1,0:T(8,128)(2,1)S(1)}) fusion(f32[128,128]{1,0:T(8,128)S(1)} %copy.15, f32[16]{0:T(128)S(1)} %add_multiply_fusion.1, pred[128]{0:T(512)(128)(4,1)S(1)} %fusion.31), kind=kLoop, calls=%fused_computation.6 | loop fusion | flops 2097152 | bytes 1114304 | tf_op jit(solution)/shard_map/convert.4
  157.8 1.1 pad_maximum_fusion.1.weights_ref
  158.9 7.4 %beams0.1.before_ref = f32[2,128,128]{2,1,0:T(8,128)} custom-call(bf16[32,64,256]{2,1,0:T(8,128)(2,1)} %copy-done.1, bf16[16,256,128]{2,1,0:T(8,128)(2,1)} %pad_maximum_fusion.1.weights_ref, f32[16,2,32,128]{3,2,1,0:T(8,128)} %copy.17.kern_ref), custom_call_target="tpu_custom_call" | custom-call | tf_op jit(solution)/shard_map/beams0/pallas_call | solution.py:375
  166.3 13.0 %all-to-all-done.1.spectra_ref = bf16[32,64,256]{2,1,0:T(8,128)(2,1)S(1)} async-done(((bf16[32,64,256]{2,1,0:T(8,128)(2,1)}), bf16[32,64,256]{2,1,0:T(8,128)(2,1)S(1)}, u32[]{:S(2)}, u32[]{:S(2)}) %all-to-all-start.1) | async-done | bytes 1048608 | tf_op jit(solution)/shard_map/all_to_all | solution.py:316
  179.3 1.0 copy-done.2
  180.3 7.4 %beams1.1 = f32[2,128,128]{2,1,0:T(8,128)} custom-call(bf16[32,64,256]{2,1,0:T(8,128)(2,1)} %copy-done.2, bf16[16,256,128]{2,1,0:T(8,128)(2,1)} %pad_maximum_fusion.1.weights_ref, f32[16,2,32,128]{3,2,1,0:T(8,128)} %copy.17.kern_ref, f32[2,128,128]{2,1,0:T(8,128)} %beams0.1.before_ref), custom_call_target="tpu_custom_call" | custom-call | tf_op jit(solution)/shard_map/beams1/pallas_call | solution.py:378
  187.7 5.6 %all-to-all-start.3 = ((f32[16,16,128]{2,1,0:T(8,128)}), f32[16,16,128]{2,1,0:T(8,128)S(1)}, u32[]{:S(2)}, u32[]{:S(2)}) async-start(f32[16,16,128]{2,1,0:T(8,128)} %bitcast.47), calls=%async_computation.3 | async-start | bytes 262144 | tf_op jit(solution)/shard_map/all_to_all | solution.py:383
  193.4 8.4 %all-to-all-done.3 = f32[16,16,128]{2,1,0:T(8,128)S(1)} async-done(((f32[16,16,128]{2,1,0:T(8,128)}), f32[16,16,128]{2,1,0:T(8,128)S(1)}, u32[]{:S(2)}, u32[]{:S(2)}) %all-to-all-start.3) | async-done | bytes 131104 | tf_op jit(solution)/shard_map/all_to_all | solution.py:383
  201.8 0.6 gather_fusion
  202.4 0.2 select_select_fusion
  202.6 21.6 %all_to_all.25 = f32[64,16,128]{2,1,0:T(8,128)S(1)} all-to-all(f32[64,16,128]{2,1,0:T(8,128)S(1)} %select_select_fusion), channel_id=1, replica_groups=mesh['sec'=2,'wide'=32,'narrow'=8] {'wide'}, dimensions={0} | all-to-all | bytes 1048576 | tf_op jit(solution)/shard_map/all_to_all | solution.py:390
  224.3 0.6 multiply_bitcast_fusion
  (62 shorter events, 0.4 us)
Async XLA Ops:
  4.7 33.6 %all-to-all-start = ((bf16[16,8,4096]{2,1,0:T(8,128)(2,1)}), bf16[16,8,4096]{2,1,0:T(8,128)(2,1)S(1)}, u32[]{:S(2)}, u32[]{:S(2)}) async-start(bf16[16,8,4096]{2,1,0:T(8,128)(2,1)} %reshape_squeeze.3), calls=%async_computation | async-start | bytes 2097152 | tf_op jit(solution)/shard_map/all_to_all | solution.py:253
  11.9 3.7 %copy-start.12 = (s32[2]{0:T(128)S(1)}, s32[2]{0:T(128)}, u32[]{:S(2)}) copy-start(s32[2]{0:T(128)} %param.9) | copy-start | bytes 28
  11.9 6.9 %copy-start.11 = (f32[16,256]{1,0:T(8,128)S(1)}, f32[16,256]{1,0:T(8,128)}, u32[]{:S(2)}) copy-start(f32[16,256]{1,0:T(8,128)} %param.7) | copy-start | bytes 49156
  13.3 12.6 %collective-permute-start = (bf16[8,8,4096]{2,1,0:T(8,128)(2,1)}, bf16[8,8,4096]{2,1,0:T(8,128)(2,1)S(1)}, u32[]{:S(2)}, u32[]{:S(2)}) collective-permute-start(bf16[8,8,4096]{2,1,0:T(8,128)(2,1)} %get-tuple-element.26), channel_id=1, source_target_pairs={{0,256},{256,0},{1,257},{257,1},{2,258},{258,2},{3,259},{259,3},{4... | collective-permute-start | bytes 1572872 | tf_op jit(solution)/shard_map/ppermute | solution.py:258
  38.3 1.0 copy-start
  72.9 20.2 %copy-start.20 = (s32[32]{0:T(128)S(1)}, s32[32]{0:T(128)}, u32[]{:S(2)}) copy-start(s32[32]{0:T(128)} %param.10) | copy-start | bytes 388
  72.9 21.6 %copy-start.19 = (bf16[2,8,4096]{2,1,0:T(8,128)(2,1)S(1)}, bf16[2,8,4096]{2,1,0:T(8,128)(2,1)}, u32[]{:S(2)}) copy-start(bf16[2,8,4096]{2,1,0:T(8,128)(2,1)} %get-tuple-element.14) | copy-start | bytes 393220
  72.9 25.9 %copy-start.18 = (bf16[2,8,4096]{2,1,0:T(8,128)(2,1)S(1)}, bf16[2,8,4096]{2,1,0:T(8,128)(2,1)}, u32[]{:S(2)}) copy-start(bf16[2,8,4096]{2,1,0:T(8,128)(2,1)} %get-tuple-element.15) | copy-start | bytes 393220
  72.9 29.7 %copy-start.17 = (bf16[2,8,4096]{2,1,0:T(8,128)(2,1)S(1)}, bf16[2,8,4096]{2,1,0:T(8,128)(2,1)}, u32[]{:S(2)}) copy-start(bf16[2,8,4096]{2,1,0:T(8,128)(2,1)} %get-tuple-element.16) | copy-start | bytes 393220
  72.9 34.0 %copy-start.16 = (bf16[2,8,4096]{2,1,0:T(8,128)(2,1)S(1)}, bf16[2,8,4096]{2,1,0:T(8,128)(2,1)}, u32[]{:S(2)}) copy-start(bf16[2,8,4096]{2,1,0:T(8,128)(2,1)} %get-tuple-element.17) | copy-start | bytes 393220
  72.9 37.6 %copy-start.15 = (bf16[2,8,4096]{2,1,0:T(8,128)(2,1)S(1)}, bf16[2,8,4096]{2,1,0:T(8,128)(2,1)}, u32[]{:S(2)}) copy-start(bf16[2,8,4096]{2,1,0:T(8,128)(2,1)} %get-tuple-element.18) | copy-start | bytes 393220
  73.0 42.4 %copy-start.14 = (bf16[2,8,4096]{2,1,0:T(8,128)(2,1)S(1)}, bf16[2,8,4096]{2,1,0:T(8,128)(2,1)}, u32[]{:S(2)}) copy-start(bf16[2,8,4096]{2,1,0:T(8,128)(2,1)} %get-tuple-element.19) | copy-start | bytes 393220
  73.0 47.0 %copy-start.13 = (bf16[2,8,4096]{2,1,0:T(8,128)(2,1)S(1)}, bf16[2,8,4096]{2,1,0:T(8,128)(2,1)}, u32[]{:S(2)}) copy-start(bf16[2,8,4096]{2,1,0:T(8,128)(2,1)} %get-tuple-element.20) | copy-start | bytes 393220
  79.7 62.3 %all-to-all-start.2 = ((bf16[32,64,256]{2,1,0:T(8,128)(2,1)}), bf16[32,64,256]{2,1,0:T(8,128)(2,1)S(1)}, u32[]{:S(2)}, u32[]{:S(2)}) async-start(bf16[32,64,256]{2,1,0:T(8,128)(2,1)} %bitcast.44), calls=%async_computation.2 | async-start | bytes 2097152 | tf_op jit(solution)/shard_map/all_to_all | solution.py:316
  94.5 20.8 %collective-permute-start.1 = (bf16[2,8,4096]{2,1,0:T(8,128)(2,1)S(1)}, bf16[2,8,4096]{2,1,0:T(8,128)(2,1)S(1)}, u32[]{:S(2)}, u32[]{:S(2)}) collective-permute-start(bf16[2,8,4096]{2,1,0:T(8,128)(2,1)S(1)} %copy-done.19), channel_id=1, source_target_pairs={{0,1},{1,2},{2,3},{3,4},{4,5},{5,6},{6,7},{7,0},{8,9},{9,10},{10,1... | collective-permute-start | bytes 393224 | tf_op jit(solution)/shard_map/ppermute | solution.py:270
  98.8 21.1 %collective-permute-start.2 = (bf16[2,8,4096]{2,1,0:T(8,128)(2,1)S(1)}, bf16[2,8,4096]{2,1,0:T(8,128)(2,1)S(1)}, u32[]{:S(2)}, u32[]{:S(2)}) collective-permute-start(bf16[2,8,4096]{2,1,0:T(8,128)(2,1)S(1)} %copy-done.18), channel_id=1, source_target_pairs={{0,2},{1,3},{2,4},{3,5},{4,6},{5,7},{6,0},{7,1},{8,10},{9,11},{10,... | collective-permute-start | bytes 393224 | tf_op jit(solution)/shard_map/ppermute | solution.py:270
  102.6 21.6 %collective-permute-start.3 = (bf16[2,8,4096]{2,1,0:T(8,128)(2,1)S(1)}, bf16[2,8,4096]{2,1,0:T(8,128)(2,1)S(1)}, u32[]{:S(2)}, u32[]{:S(2)}) collective-permute-start(bf16[2,8,4096]{2,1,0:T(8,128)(2,1)S(1)} %copy-done.17), channel_id=1, source_target_pairs={{0,3},{1,4},{2,5},{3,6},{4,7},{5,0},{6,1},{7,2},{8,11},{9,12},{10,... | collective-permute-start | bytes 393224 | tf_op jit(solution)/shard_map/ppermute | solution.py:270
  106.9 17.3 %collective-permute-start.4 = (bf16[2,8,4096]{2,1,0:T(8,128)(2,1)S(1)}, bf16[2,8,4096]{2,1,0:T(8,128)(2,1)S(1)}, u32[]{:S(2)}, u32[]{:S(2)}) collective-permute-start(bf16[2,8,4096]{2,1,0:T(8,128)(2,1)S(1)} %copy-done.16), channel_id=1, source_target_pairs={{0,4},{1,5},{2,6},{3,7},{4,0},{5,1},{6,2},{7,3},{8,12},{9,13},{10,... | collective-permute-start | bytes 393224 | tf_op jit(solution)/shard_map/ppermute | solution.py:270
  110.6 16.5 %collective-permute-start.5 = (bf16[2,8,4096]{2,1,0:T(8,128)(2,1)S(1)}, bf16[2,8,4096]{2,1,0:T(8,128)(2,1)S(1)}, u32[]{:S(2)}, u32[]{:S(2)}) collective-permute-start(bf16[2,8,4096]{2,1,0:T(8,128)(2,1)S(1)} %copy-done.15), channel_id=1, source_target_pairs={{0,5},{1,6},{2,7},{3,0},{4,1},{5,2},{6,3},{7,4},{8,13},{9,14},{10,... | collective-permute-start | bytes 393224 | tf_op jit(solution)/shard_map/ppermute | solution.py:270
  115.3 19.2 %copy-start.3 = (bf16[2,8,4096]{2,1,0:T(8,128)(2,1)}, bf16[2,8,4096]{2,1,0:T(8,128)(2,1)S(1)}, u32[]{:S(2)}) copy-start(bf16[2,8,4096]{2,1,0:T(8,128)(2,1)S(1)} %collective-permute-done.1.refs_1_) | copy-start | bytes 393220
  115.3 17.8 %collective-permute-start.6 = (bf16[2,8,4096]{2,1,0:T(8,128)(2,1)S(1)}, bf16[2,8,4096]{2,1,0:T(8,128)(2,1)S(1)}, u32[]{:S(2)}, u32[]{:S(2)}) collective-permute-start(bf16[2,8,4096]{2,1,0:T(8,128)(2,1)S(1)} %copy-done.14), channel_id=1, source_target_pairs={{0,6},{1,7},{2,0},{3,1},{4,2},{5,3},{6,4},{7,5},{8,14},{9,15},{10,... | collective-permute-start | bytes 393224 | tf_op jit(solution)/shard_map/ppermute | solution.py:270
  119.9 14.6 %copy-start.4 = (bf16[2,8,4096]{2,1,0:T(8,128)(2,1)}, bf16[2,8,4096]{2,1,0:T(8,128)(2,1)S(1)}, u32[]{:S(2)}) copy-start(bf16[2,8,4096]{2,1,0:T(8,128)(2,1)S(1)} %collective-permute-done.2.refs_2_) | copy-start | bytes 393220
  119.9 14.6 %collective-permute-start.7 = (bf16[2,8,4096]{2,1,0:T(8,128)(2,1)S(1)}, bf16[2,8,4096]{2,1,0:T(8,128)(2,1)S(1)}, u32[]{:S(2)}, u32[]{:S(2)}) collective-permute-start(bf16[2,8,4096]{2,1,0:T(8,128)(2,1)S(1)} %copy-done.13), channel_id=1, source_target_pairs={{0,7},{1,0},{2,1},{3,2},{4,3},{5,4},{6,5},{7,6},{8,15},{9,8},{10,9... | collective-permute-start | bytes 393224 | tf_op jit(solution)/shard_map/ppermute | solution.py:270
  124.2 27.6 %copy-start.10 = (f32[128,64]{0,1:T(8,128)S(1)}, f32[128,64]{0,1:T(8,128)}, u32[]{:S(2)}) copy-start(f32[128,64]{0,1:T(8,128)} %param.8) | copy-start | bytes 98308
  124.2 10.3 %copy-start.5 = (bf16[2,8,4096]{2,1,0:T(8,128)(2,1)}, bf16[2,8,4096]{2,1,0:T(8,128)(2,1)S(1)}, u32[]{:S(2)}) copy-start(bf16[2,8,4096]{2,1,0:T(8,128)(2,1)S(1)} %collective-permute-done.3.refs_3_) | copy-start | bytes 393220
  124.2 10.3 %copy-start.6 = (bf16[2,8,4096]{2,1,0:T(8,128)(2,1)}, bf16[2,8,4096]{2,1,0:T(8,128)(2,1)S(1)}, u32[]{:S(2)}) copy-start(bf16[2,8,4096]{2,1,0:T(8,128)(2,1)S(1)} %collective-permute-done.4.refs_4_) | copy-start | bytes 393220
  127.0 7.5 %copy-start.7 = (bf16[2,8,4096]{2,1,0:T(8,128)(2,1)}, bf16[2,8,4096]{2,1,0:T(8,128)(2,1)S(1)}, u32[]{:S(2)}) copy-start(bf16[2,8,4096]{2,1,0:T(8,128)(2,1)S(1)} %collective-permute-done.5.refs_5_) | copy-start | bytes 393220
  133.1 1.5 copy-start.8
  134.6 0.7 copy-start.9
  142.0 11.2 %copy-start.21 = (s32[32]{0:T(128)S(1)}, s32[32]{0:T(128)}, u32[]{:S(2)}) copy-start(s32[32]{0:T(128)} %param.11) | copy-start | bytes 388
  142.0 15.8 %copy-start.1 = (bf16[32,64,256]{2,1,0:T(8,128)(2,1)}, bf16[32,64,256]{2,1,0:T(8,128)(2,1)S(1)}, u32[]{:S(2)}) copy-start(bf16[32,64,256]{2,1,0:T(8,128)(2,1)S(1)} %all-to-all-done.2.spectra_ref) | copy-start | bytes 3145732
  142.0 37.3 %all-to-all-start.1 = ((bf16[32,64,256]{2,1,0:T(8,128)(2,1)}), bf16[32,64,256]{2,1,0:T(8,128)(2,1)S(1)}, u32[]{:S(2)}, u32[]{:S(2)}) async-start(bf16[32,64,256]{2,1,0:T(8,128)(2,1)} %bitcast.45), calls=%async_computation.1 | async-start | bytes 2097152 | tf_op jit(solution)/shard_map/all_to_all | solution.py:316
  179.3 1.0 copy-start.2
  187.7 14.1 %all-to-all-start.3 = ((f32[16,16,128]{2,1,0:T(8,128)}), f32[16,16,128]{2,1,0:T(8,128)S(1)}, u32[]{:S(2)}, u32[]{:S(2)}) async-start(f32[16,16,128]{2,1,0:T(8,128)} %bitcast.47), calls=%async_computation.3 | async-start | bytes 262144 | tf_op jit(solution)/shard_map/all_to_all | solution.py:383

commit v3 on v1

--- a/solution.py
+++ b/solution.py
@@ -14,20 +14,25 @@
 T_BLOCK = 8
 
 
-def slot_tables(owners, slot_count):
+def class_of_subbands(owners):
     sub_count = owners.shape[0]
     order = jnp.arange(sub_count, dtype=jnp.int32)
-    same = owners[:, None] == owners[None, :]
-    before = order[None, :] < order[:, None]
-    rank = jnp.sum(jnp.where(same & before, 1, 0), axis=1).astype(jnp.int32)
-    lookup = owners * SUBBAND_LIMIT + rank
-    slots = jnp.arange(slot_count, dtype=jnp.int32)
-    match = lookup[None, :] == slots[:, None]
-    subband = jnp.sum(jnp.where(match, order[None, :], 0), axis=1)
-    return subband, jnp.any(match, axis=1)
-
-
-def filter_kernel(volts_ref, taps_ref, table_ref, out_ref, frames, filtered, packed):
+    mate = order + 1 - 2 * (order % 2)
+    is_mate = mate[:, None] == order[None, :]
+    mate_owner = jnp.sum(jnp.where(is_mate, owners[None, :], 0), axis=1)
+    near = (mate_owner[:, None] == owners[None, :]) & ~is_mate
+    near = near | near.T | (order[:, None] == order[None, :])
+    reach = 1
+    while reach < sub_count:
+        step = near.astype(jnp.bfloat16)
+        near = jnp.dot(step, step, preferred_element_type=jnp.float32) > 0.5
+        reach *= 2
+    least = jnp.min(jnp.where(near, order[None, :], sub_count), axis=1)
+    least_of_mate = jnp.min(jnp.where(is_mate, least[None, :], sub_count), axis=1)
+    return jnp.where(least < least_of_mate, 0, 1).astype(jnp.int32)
+
+
+def filter_kernel(class_ref, volts_ref, taps_ref, table_ref, out_ref, frames, filtered, packed):
     source_count, group_size, rows, piece_len = volts_ref.shape
     tap_count, _, chan_count = taps_ref.shape
     block_count = 2
@@ -94,7 +99,7 @@
         @pl.when(block == block_count - 1)
         def _():
             for b in range(block_count):
-                out_ref[sub, :, :, b * frame_count : (b + 1) * frame_count] = (
+                out_ref[class_ref[sub], :, :, b * frame_count : (b + 1) * frame_count] = (
                     packed[b].reshape(chan_count, rows, frame_count).astype(jnp.bfloat16)
                 )
 
@@ -225,11 +230,15 @@
         ],
         axis=1,
     ).astype(jnp.bfloat16)
+    classes = class_of_subbands(owners)
+    group = lax.axis_index("sec") * narrow_count + lax.axis_index("narrow")
+    own_classes = lax.dynamic_slice_in_dim(classes, group * group_size, group_size)
     whole = pl.BlockSpec(memory_space=pltpu.VMEM)
+    scalars = pl.BlockSpec(memory_space=pltpu.SMEM)
     spectra = pl.pallas_call(
         filter_kernel,
         out_shape=jax.ShapeDtypeStruct((group_size, chan_count, rows, length), jnp.bfloat16),
-        in_specs=[whole] * 3,
+        in_specs=[scalars] + [whole] * 3,
         out_specs=whole,
         scratch_shapes=[
             pltpu.VMEM((block_len + tap_count, rows, chan_count), jnp.float32),
@@ -238,15 +247,14 @@
         ],
         compiler_params=pltpu.CompilerParams(vmem_limit_bytes=VMEM_BYTES),
         name="filter",
-    )(volts, taps, table)
+    )(own_classes, volts, taps, table)
 
     spectra = spectra.reshape(wide_count, chan_local, rows, length)
     spectra = lax.all_to_all(spectra, "wide", 0, 0, tiled=True)
 
     wide_index = lax.axis_index("wide")
-    group = lax.axis_index("sec") * narrow_count + lax.axis_index("narrow")
     member = wide_index // chan_groups
-    sub = group * group_size + member
+    sub = group * group_size + jnp.where(own_classes[0] == member, 0, 1)
     channels = (wide_index % chan_groups) * chan_local + jnp.arange(chan_local, dtype=jnp.int32)
 
     frequency = sub.astype(jnp.float32) + channels.astype(jnp.float32) / chan_count
@@ -288,15 +296,27 @@
 
     partial = partial.reshape(source_count, beam_count // narrow_count, block_len)
     partial = lax.all_to_all(partial, together, 0, 0, tiled=True)
-    slot_count = wide_count * SUBBAND_LIMIT
-    slot_sub, filled = slot_tables(owners, slot_count)
-    mine = filled & (slot_sub % group_size == member)
+    order = jnp.arange(sub_count, dtype=jnp.int32)
+    goes = (owners[None, :] == jnp.arange(wide_count)[:, None]) & (classes == member)[None, :]
+    chosen = jnp.sum(jnp.where(goes, order[None, :] // group_size, 0), axis=1)
     outgoing = jnp.where(
-        mine[:, None, None], jnp.take(partial, slot_sub // group_size, axis=0), 0.0
+        jnp.any(goes, axis=1)[:, None, None], jnp.take(partial, chosen, axis=0), 0.0
     )
     arrived = lax.all_to_all(outgoing, "wide", 0, 0, tiled=True)
-    arrived = arrived.reshape(wide_count, SUBBAND_LIMIT, beam_count // narrow_count, block_len)
-    return (jnp.sum(arrived, axis=0) / chan_count)[None]
+    arrived = arrived.reshape(group_size, chan_groups, beam_count // narrow_count, block_len)
+    by_class = jnp.sum(arrived, axis=1) / chan_count
+    owned = owners == wide_index
+    rank = jnp.cumsum(owned.astype(jnp.int32)) - 1
+    shares = [
+        [
+            jnp.any(owned & (rank == slot) & (classes == which)).astype(jnp.float32)
+            for which in range(group_size)
+        ]
+        for slot in range(SUBBAND_LIMIT)
+    ]
+    return jnp.stack(
+        [sum(share * by_class[which] for which, share in enumerate(row)) for row in shares]
+    )[None]
 
 
 def solution(mesh):

time: 188 us -> 184 us (0.979)
  blocking collectives: 22.5 us -> 0 us
  starting transfers between devices: 26.7 us -> 33.2 us
  waiting for transfers between devices: 87.1 us -> 92.1 us
  between operations: 4.07 us -> 6.76 us
  other arithmetic: 12.7 us -> 14.6 us
    all_to_all x1 -> x0, blocking collectives: 22.5 us -> none  [shards(): arrived = lax.all_to_all(outgoing, 'wide', 0, 0, tiled=True)]
    all_to_all x0 -> x1, waiting for transfers between devices: none -> 8.04 us  [shards(): arrived = lax.all_to_all(outgoing, 'wide', 0, 0, tiled=True)]
    all_to_all x0 -> x1, starting transfers between devices: none -> 6.48 us  [shards(): arrived = lax.all_to_all(outgoing, 'wide', 0, 0, tiled=True)]
    all_to_all x1, waiting for transfers between devices: 38.7 us -> 35.8 us  [shards(): volts = lax.all_to_all(volts, together, 0, 0, tiled=True)]
    another operation x2 -> x4, other arithmetic: 6.51 us -> 6.57 us
  transfers between devices with their start and end apart: 3 -> 4, of which waited for: 3 -> 4; matrix products, arithmetic and copies ran while one was open for 8% -> 10% of each run, Pallas kernels for 0% -> 0%
where the time goes in v3:
time: 184 us; the launch traced here: 181 us
  waiting for transfers between devices  92.1 us (50%)
  starting transfers between devices  33.2 us (18%)
  Pallas kernels  22.2 us (12%)
  other arithmetic  14.6 us (8%)
  local copies, waits for them, and re-layouts  11.3 us (6%)
  between operations  6.76 us (4%)
    all_to_all x1, waiting for transfers between devices, shards(): spectra = lax.all_to_all(spectra, 'wide', 0, 0, tiled=True)  39.8 us
    all_to_all x1, waiting for transfers between devices, shards(): volts = lax.all_to_all(volts, together, 0, 0, tiled=True)  35.8 us
    all_to_all x1, starting transfers between devices, shards(): spectra = lax.all_to_all(spectra, 'wide', 0, 0, tiled=True)  13.6 us
    pallas_call x1, Pallas kernels, shards(): pl.pallas_call(filter_kernel, out_shape=jax.ShapeDtypeStruct((group_size,...  12 us
    pallas_call x1, Pallas kernels, shards(): pl.pallas_call(beam_kernel, out_shape=jax.ShapeDtypeStruct((block_count,...  10.2 us
    all_to_all x1, waiting for transfers between devices, shards(): partial = lax.all_to_all(partial, together, 0, 0, tiled=True)  8.44 us
    all_to_all x1, waiting for transfers between devices, shards(): arrived = lax.all_to_all(outgoing, 'wide', 0, 0, tiled=True)  8.04 us
    all_to_all x1, starting transfers between devices, shards(): volts = lax.all_to_all(volts, together, 0, 0, tiled=True)  7.34 us
  transfers between devices with their start and end apart: 4, of which 4 were waited for; matrix products, arithmetic and copies ran while one was open for 10% of the time, Pallas kernels for 0%

profile of v3, /device:TPU:6, one launch (start us, length us, event | category | flops | bytes accessed | tf_op | source)
XLA Modules:
  0.0 181.3 jit_solution(18096811902789017787)
XLA Ops:
  0.0 4.1 %reshape.301 = bf16[32,8,4096]{2,1,0:T(8,128)(2,1)} reshape(bf16[1,32,2,2,2,4096]{5,4,3,2,1,0:T(2,128)(2,1)} %param.6) | data formatting | bytes 4194304 | tf_op jit(solution)/shard_map/reshape | solution.py:204
  4.1 0.0 copy-start.4
  4.1 0.0 copy-start.5
  4.1 0.0 copy-start.3
  4.1 7.3 %all-to-all-start = ((bf16[32,8,4096]{2,1,0:T(8,128)(2,1)}), bf16[32,8,4096]{2,1,0:T(8,128)(2,1)S(1)}, u32[]{:S(2)}, u32[]{:S(2)}) async-start(bf16[32,8,4096]{2,1,0:T(8,128)(2,1)} %reshape.301), calls=%async_computation | async-start | bytes 4194304 | tf_op jit(solution)/shard_map/all_to_all | solution.py:205
  11.5 0.0 copy-done.4
  11.5 0.6 fusion.57
  14.6 0.0 copy-done.5
  14.6 0.1 copy.19
  14.7 0.1 reduce-window.9
  14.8 0.0 copy-done.3
  15.4 0.4 dynamic_update_slice.7
  16.5 0.4 dynamic_update_slice.6
  16.9 0.7 reshape.304.taps_ref
  17.6 0.2 select_reduce_fusion.2
  17.8 0.2 convolution_compare_fusion.4
  18.0 0.2 convolution_compare_fusion.2
  18.3 0.4 fusion.1
  18.7 0.1 compare_reduce_fusion.1
  18.8 0.2 select_reduce_fusion.1
  19.0 0.7 and_reduce_fusion.3
  19.7 0.6 dynamic_slice.3.class_ref
  20.4 0.1 iota_subtract_fusion
  20.4 2.3 %fusion.18 = (bf16[2,256,256]{2,1,0:T(8,128)(2,1)S(1)}, bf16[2,256,256]{2,1,0:T(8,128)(2,1)S(1)}, bf16[2,256,256]{2,1,0:T(8,128)(2,1)S(1)}) fusion(s32[2,256]{1,0:T(2,128)S(1)} %iota_subtract_fusion), kind=kLoop, calls=%fused_computation.37 | loop fusion | flops 2621440 | bytes 788480 | tf_op jit(solution)/shard_map/convert.12
  22.7 1.1 maximum_maximum_fusion.table_ref
  23.8 35.8 %all-to-all-done = bf16[32,8,4096]{2,1,0:T(8,128)(2,1)S(1)} async-done(((bf16[32,8,4096]{2,1,0:T(8,128)(2,1)}), bf16[32,8,4096]{2,1,0:T(8,128)(2,1)S(1)}, u32[]{:S(2)}, u32[]{:S(2)}) %all-to-all-start) | async-done | bytes 2097184 | tf_op jit(solution)/shard_map/all_to_all | solution.py:205
  59.6 0.0 copy-start
  59.6 1.3 copy-done
  60.9 12.0 %filter.1 = bf16[2,256,8,256]{3,2,1,0:T(8,128)(2,1)} custom-call(s32[2]{0:T(128)} %dynamic_slice.3.class_ref, bf16[16,2,8,4096]{3,2,1,0:T(8,128)(2,1)} %bitcast.33, f32[17,8,256]{2,1,0:T(8,128)} %reshape.304.taps_ref, bf16[2,512,512]{2,1,0:T(8,128)(2,1)} %maximum_maximum_fusion.table_ref), custom_call_target="tpu_custom_call" | custom-call | tf_op jit(solution)/shard_map/filter/pallas_call | solution.py:238
  72.8 0.0 copy-start.2
  72.8 0.0 copy-start.6
  72.8 0.0 copy-start.7
  72.8 13.6 %all-to-all-start.1 = ((bf16[32,16,8,256]{3,2,1,0:T(8,128)(2,1)}), bf16[32,16,8,256]{3,2,1,0:T(8,128)(2,1)S(1)}, u32[]{:S(2)}, u32[]{:S(2)}) async-start(bf16[32,16,8,256]{3,2,1,0:T(8,128)(2,1)} %bitcast.34), calls=%async_computation.1 | async-start | bytes 4194304 | tf_op jit(solution)/shard_map/all_to_all | solution.py:253
  86.4 0.0 copy-done.2
  86.5 0.1 copy.21
  86.6 0.0 copy-done.6
  86.7 0.0 copy-done.7
  86.7 0.6 fusion.53
  87.3 0.6 compare_select_fusion.1
  88.0 0.1 add_multiply_fusion
  88.0 0.1 iota_multiply_fusion
  88.1 1.3 cosine_reduce_fusion
  89.4 0.2 fusion.16
  89.6 1.0 copy.22.kern_ref
  90.6 0.1 select_reduce_fusion
  90.7 0.1 copy.23
  90.8 0.1 fusion.35
  90.9 0.1 fusion.24
  91.0 4.2 %fusion.5 = (bf16[16,128,128]{2,1,0:T(8,128)(2,1)S(1)}, bf16[16,128,128]{2,1,0:T(8,128)(2,1)S(1)}) fusion(f32[128,128]{1,0:T(8,128)S(1)} %copy.21, f32[16]{0:T(128)S(1)} %add_multiply_fusion.1, pred[128]{0:T(512)(128)(4,1)S(1)} %fusion.52), kind=kLoop, calls=%fused_computation.13 | loop fusion | flops 2097152 | bytes 1114304 | tf_op jit(solution)/shard_map/convert.5
  95.3 1.1 pad_maximum_fusion.weights_ref
  96.4 39.8 %all-to-all-done.1.spectra_ref = bf16[32,16,8,256]{3,2,1,0:T(8,128)(2,1)S(1)} async-done(((bf16[32,16,8,256]{3,2,1,0:T(8,128)(2,1)}), bf16[32,16,8,256]{3,2,1,0:T(8,128)(2,1)S(1)}, u32[]{:S(2)}, u32[]{:S(2)}) %all-to-all-start.1) | async-done | bytes 2097184 | tf_op jit(solution)/shard_map/all_to_all | solution.py:253
  136.2 0.0 copy-start.1
  136.2 1.3 copy-done.1
  137.5 10.2 %beams.1 = f32[2,128,128]{2,1,0:T(8,128)} custom-call(bf16[32,16,8,256]{3,2,1,0:T(8,128)(2,1)} %copy-done.1, bf16[16,256,128]{2,1,0:T(8,128)(2,1)} %pad_maximum_fusion.weights_ref, f32[16,2,32,128]{3,2,1,0:T(8,128)} %copy.22.kern_ref), custom_call_target="tpu_custom_call" | custom-call | tf_op jit(solution)/shard_map/beams/pallas_call | solution.py:287
  147.8 5.8 %all-to-all-start.2 = ((f32[16,16,128]{2,1,0:T(8,128)}), f32[16,16,128]{2,1,0:T(8,128)S(1)}, u32[]{:S(2)}, u32[]{:S(2)}) async-start(f32[16,16,128]{2,1,0:T(8,128)} %bitcast.35), calls=%async_computation.2 | async-start | bytes 262144 | tf_op jit(solution)/shard_map/all_to_all | solution.py:298
  153.6 8.4 %all-to-all-done.2 = f32[16,16,128]{2,1,0:T(8,128)S(1)} async-done(((f32[16,16,128]{2,1,0:T(8,128)}), f32[16,16,128]{2,1,0:T(8,128)S(1)}, u32[]{:S(2)}, u32[]{:S(2)}) %all-to-all-start.2) | async-done | bytes 131104 | tf_op jit(solution)/shard_map/all_to_all | solution.py:298
  162.1 0.6 gather_fusion
  162.7 0.8 select_select_fusion
  163.5 6.5 %all-to-all-start.3 = ((f32[32,16,128]{2,1,0:T(8,128)}), f32[32,16,128]{2,1,0:T(8,128)S(1)}, u32[]{:S(2)}, u32[]{:S(2)}) async-start(f32[32,16,128]{2,1,0:T(8,128)} %select_select_fusion), calls=%async_computation.3 | async-start | bytes 524288 | tf_op jit(solution)/shard_map/all_to_all | solution.py:305
  172.6 8.0 %all-to-all-done.3 = f32[32,16,128]{2,1,0:T(8,128)S(1)} async-done(((f32[32,16,128]{2,1,0:T(8,128)}), f32[32,16,128]{2,1,0:T(8,128)S(1)}, u32[]{:S(2)}, u32[]{:S(2)}) %all-to-all-start.3) | async-done | bytes 262176 | tf_op jit(solution)/shard_map/all_to_all | solution.py:305
  180.7 0.6 maximum_bitcast_fusion
  (24 shorter events, 0.3 us)
Async XLA Ops:
  4.1 7.4 %copy-start.4 = (s32[2]{0:T(128)S(1)}, s32[2]{0:T(128)}, u32[]{:S(2)}) copy-start(s32[2]{0:T(128)} %param.9) | copy-start | bytes 28
  4.1 10.5 %copy-start.5 = (s32[32]{0:T(128)S(1)}, s32[32]{0:T(128)}, u32[]{:S(2)}) copy-start(s32[32]{0:T(128)} %param.11) | copy-start | bytes 388
  4.1 10.7 %copy-start.3 = (f32[16,256]{1,0:T(8,128)S(1)}, f32[16,256]{1,0:T(8,128)}, u32[]{:S(2)}) copy-start(f32[16,256]{1,0:T(8,128)} %param.7) | copy-start | bytes 49156
  4.1 55.5 %all-to-all-start = ((bf16[32,8,4096]{2,1,0:T(8,128)(2,1)}), bf16[32,8,4096]{2,1,0:T(8,128)(2,1)S(1)}, u32[]{:S(2)}, u32[]{:S(2)}) async-start(bf16[32,8,4096]{2,1,0:T(8,128)(2,1)} %reshape.301), calls=%async_computation | async-start | bytes 4194304 | tf_op jit(solution)/shard_map/all_to_all | solution.py:205
  59.6 1.3 copy-start
  72.8 13.6 %copy-start.2 = (f32[128,64]{0,1:T(8,128)S(1)}, f32[128,64]{0,1:T(8,128)}, u32[]{:S(2)}) copy-start(f32[128,64]{0,1:T(8,128)} %param.8) | copy-start | bytes 98308
  72.8 13.7 %copy-start.6 = (s32[2]{0:T(128)S(1)}, s32[2]{0:T(128)}, u32[]{:S(2)}) copy-start(s32[2]{0:T(128)} %dynamic_slice.3.class_ref) | copy-start | bytes 28
  72.8 13.8 %copy-start.7 = (s32[32]{0:T(128)S(1)}, s32[32]{0:T(128)}, u32[]{:S(2)}) copy-start(s32[32]{0:T(128)} %param.10) | copy-start | bytes 388
  72.8 63.3 %all-to-all-start.1 = ((bf16[32,16,8,256]{3,2,1,0:T(8,128)(2,1)}), bf16[32,16,8,256]{3,2,1,0:T(8,128)(2,1)S(1)}, u32[]{:S(2)}, u32[]{:S(2)}) async-start(bf16[32,16,8,256]{3,2,1,0:T(8,128)(2,1)} %bitcast.34), calls=%async_computation.1 | async-start | bytes 4194304 | tf_op jit(solution)/shard_map/all_to_all | solution.py:253
  136.2 1.4 copy-start.1
  147.8 14.3 %all-to-all-start.2 = ((f32[16,16,128]{2,1,0:T(8,128)}), f32[16,16,128]{2,1,0:T(8,128)S(1)}, u32[]{:S(2)}, u32[]{:S(2)}) async-start(f32[16,16,128]{2,1,0:T(8,128)} %bitcast.35), calls=%async_computation.2 | async-start | bytes 262144 | tf_op jit(solution)/shard_map/all_to_all | solution.py:298
  163.5 17.1 %all-to-all-start.3 = ((f32[32,16,128]{2,1,0:T(8,128)}), f32[32,16,128]{2,1,0:T(8,128)S(1)}, u32[]{:S(2)}, u32[]{:S(2)}) async-start(f32[32,16,128]{2,1,0:T(8,128)} %select_select_fusion), calls=%async_computation.3 | async-start | bytes 524288 | tf_op jit(solution)/shard_map/all_to_all | solution.py:305

commit v4 on v1

v4 whole, which is shorter than its diff:
```python
import math

import jax
import jax.numpy as jnp
from jax import lax
from jax.experimental import pallas as pl
from jax.experimental.pallas import tpu as pltpu
from jax.sharding import PartitionSpec as P

SEG = 16
SUBBAND_LIMIT = 2
MAXD = 128
LEAD = 8
LANES = 128
TWO_PI = 2.0 * math.pi
VMEM_BYTES = 56 * 1024 * 1024


def filter_kernel(
    where_ref, own_ref, left_ref, right_ref, taps_ref, table_ref, out_ref, frames, filtered, packed
):
    sub_count, rows, piece_len = own_ref.shape
    tap_count, _, chan_count = taps_ref.shape
    station_count = table_ref.shape[0]
    pol_count = rows // (2 * station_count)
    quad = 2 * station_count
    spectra = piece_len // chan_count
    halves = chan_count // LANES
    width = pol_count * spectra
    fold = LANES // width
    members = filtered.shape[1] // (spectra * rows)
    fours = chan_count // fold
    zero = jnp.zeros((rows, LANES), jnp.float32)
    follows = jnp.where(where_ref[0] == 0, 0.0, 1.0)

    def one_batch(batch, carry):
        def one_sub(member, inner):
            sub = batch * members + member
            for half in range(halves):
                lanes = slice(half * LANES, half * LANES + LANES)
                taps = [taps_ref[tap, :, lanes] for tap in range(tap_count)]

                def load(ref, frame):
                    low = frame * chan_count + half * LANES
                    if low >= ref.shape[-1]:
                        return zero
                    return ref[sub, :, low : low + LANES].astype(jnp.float32)

                own = [load(own_ref, frame) for frame in range(spectra)]
                early = [load(left_ref, frame) for frame in range(LEAD)]
                early += [frame * follows for frame in own]
                late = own + [load(right_ref, frame) for frame in range(LEAD)]
                for number in range(spectra):
                    source = early[number:] if number < LEAD else late[number - LEAD :]
                    total = taps[0] * source[0]
                    for tap in range(1, tap_count):
                        total = total + taps[tap] * source[tap]
                    at = pl.multiple_of((member * spectra + number) * rows, rows)
                    filtered[half, pl.ds(at, rows), :] = total
            return inner

        lax.fori_loop(0, members, one_sub, 0)
        lane = lax.broadcasted_iota(jnp.int32, (fours, LANES), 1) // width
        for station in range(station_count):
            parts = []
            for member in range(members):
                for pol in range(pol_count):
                    first = member * spectra * rows + (station * pol_count + pol) * 2
                    parts.append(
                        jnp.concatenate(
                            [
                                filtered[half, pl.ds(first + r, spectra, stride=rows), :].astype(
                                    jnp.bfloat16
                                )
                                for r in range(2)
                                for half in range(halves)
                            ],
                            axis=1,
                        )
                    )
            spectrum = lax.dot_general(
                table_ref[station],
                jnp.concatenate(parts, axis=0),
                (((1,), (1,)), ((), ())),
                preferred_element_type=jnp.float32,
            )
            for r in range(2):
                for tile in range(members // fold):
                    blocks = [
                        spectrum[
                            (r * fold + turn) * fours : (r * fold + turn + 1) * fours,
                            tile * LANES : (tile + 1) * LANES,
                        ]
                        for turn in range(fold)
                    ]
                    for member in range(fold):
                        whole = None
                        for turn, block in enumerate(blocks):
                            shift = (turn - member) * width % LANES
                            moved = pltpu.roll(block, shift, 1) if shift else block
                            whole = moved if whole is None else jnp.where(lane == turn, moved, whole)
                        packed[
                            tile * fold + member,
                            pl.ds(station * 2 + r, fours, stride=quad),
                            :,
                        ] = whole
        for member in range(members):
            out_ref[batch * members + member] = packed[member].astype(jnp.bfloat16)
        return carry

    lax.fori_loop(0, sub_count // members, one_batch, 0)


def beam_kernel(
    spectra_ref, tail_ref, weights_ref, kern_ref, order_ref, power_ref, held, held_tail, total
):
    source_count, piece_count, row_count, _ = spectra_ref.shape
    beam_count, block_len = power_ref.shape
    chan_local = weights_ref.shape[0]
    pol_count = 2
    spectra = block_len // piece_count
    width = pol_count * spectra
    fold = LANES // width
    quad = row_count * fold // chan_local
    step_rows = 8
    span = 2 * SEG
    from_time = lax.broadcasted_iota(jnp.int32, (block_len, block_len), 0)
    to_time = lax.broadcasted_iota(jnp.int32, (block_len, block_len), 1)
    from_seg = lax.rem(from_time + block_len - LEAD, block_len) // SEG
    to_seg = lax.rem(to_time + block_len - LEAD, block_len) // SEG
    own_mask = (from_seg == to_seg) | (from_seg + 1 == to_seg)
    cross_mask = to_seg[:spectra] == 0
    no_rows = jnp.zeros((block_len - spectra, block_len), jnp.float32)
    lane = lax.broadcasted_iota(jnp.int32, (source_count * quad, block_len), 1) // spectra
    total[...] = jnp.zeros_like(total)

    def gathered(ref, inner):
        return jnp.concatenate(
            [ref[pl.ds(inner * quad + q, source_count, stride=step_rows), :] for q in range(quad)],
            axis=0,
        )

    def turned(value, shift):
        return pltpu.roll(value, shift % LANES, 1) if shift % LANES else value

    def matrix(real, imag):
        return jnp.concatenate(
            [jnp.concatenate([real, imag], axis=1), jnp.concatenate([-imag, real], axis=1)], axis=0
        ).astype(jnp.bfloat16)

    def one(step, carry):
        at = pl.multiple_of(step * step_rows, step_rows)
        shape = (source_count * step_rows, LANES)
        for piece in range(piece_count):
            held[piece] = (
                spectra_ref[:, piece, pl.ds(at, step_rows), :].astype(jnp.float32).reshape(shape)
            )
        held_tail[...] = tail_ref[:, pl.ds(at, step_rows), :].astype(jnp.float32).reshape(shape)
        for inner in range(step_rows // quad):
            pieces = [gathered(held.at[piece], inner) for piece in range(piece_count)]
            tail = gathered(held_tail, inner)
            for turn in range(fold):
                chan = step * (step_rows // quad * fold) + inner * fold + turn
                parts = []
                for pol in range(pol_count):
                    low = turn * width + pol * spectra
                    whole = turned(pieces[0], -low)
                    for piece in range(1, piece_count):
                        moved = turned(pieces[piece], piece * spectra - low)
                        whole = jnp.where(lane == piece, moved, whole)
                    parts.append(whole.astype(jnp.bfloat16))
                for pol in range(pol_count):
                    parts.append(
                        turned(tail, -(turn * width + pol * spectra)).astype(jnp.bfloat16)
                    )
                beams = jnp.dot(
                    weights_ref[chan],
                    jnp.concatenate(parts, axis=1),
                    preferred_element_type=jnp.float32,
                ).astype(jnp.bfloat16)

                def series(first):
                    return jnp.concatenate(
                        [
                            jnp.concatenate(
                                [
                                    beams[
                                        part * beam_count : (part + 1) * beam_count,
                                        (first + pol) * LANES : (first + pol + 1) * LANES,
                                    ]
                                    for part in range(2)
                                ],
                                axis=1,
                            )
                            for pol in range(pol_count)
                        ],
                        axis=0,
                    )

                kern = [kern_ref[chan, part] for part in range(2)]
                own = [
                    jnp.where(own_mask, jnp.concatenate([part] * (block_len // span), axis=0), 0.0)
                    for part in kern
                ]
                cross = [
                    jnp.concatenate(
                        [
                            jnp.where(
                                cross_mask,
                                jnp.concatenate([part[:LEAD], part[span - LEAD :]], axis=0),
                                0.0,
                            ),
                            no_rows,
                        ],
                        axis=0,
                    )
                    for part in kern
                ]
                clean = jnp.dot(
                    series(0), matrix(*own), preferred_element_type=jnp.float32
                ) + jnp.dot(
                    series(pol_count), matrix(*cross), preferred_element_type=jnp.float32
                )
                square = clean * clean
                both = square[:beam_count] + square[beam_count:]
                total[...] += both[:, :block_len] + both[:, block_len:]
        return carry

    lax.fori_loop(0, row_count // step_rows, one, 0)
    power_ref[...] = jnp.dot(
        total[...],
        order_ref[...],
        precision=lax.Precision.HIGHEST,
        preferred_element_type=jnp.float32,
    )


def shards(voltages, prototype, beam_delays, station_shifts, dm_index, owners):
    wide_count = lax.axis_size("wide")
    narrow_count = lax.axis_size("narrow")
    wide_index = lax.axis_index("wide")
    narrow_index = lax.axis_index("narrow")
    _, sub_count, station_local, pol_count, _, piece_len = voltages.shape
    tap_count, chan_count = prototype.shape
    beam_count, station_count = beam_delays.shape
    rows = station_local * pol_count * 2
    quad = station_local * 2
    spectra = piece_len // chan_count
    block_len = spectra * narrow_count
    chan_local = chan_count // narrow_count
    fold = LANES // (pol_count * spectra)
    fours = chan_count // fold
    members = min(2 * fold, sub_count)
    whole = pl.BlockSpec(memory_space=pltpu.VMEM)
    scalars = pl.BlockSpec(memory_space=pltpu.SMEM)
    params = pltpu.CompilerParams(vmem_limit_bytes=VMEM_BYTES)

    volts = voltages.reshape(sub_count, rows, piece_len)
    ahead = (tap_count - 1 - LEAD) * chan_count + MAXD
    right = lax.ppermute(
        volts[..., :ahead], "narrow", [(i, i - 1) for i in range(1, narrow_count)]
    )
    left = lax.ppermute(
        volts[..., piece_len - LEAD * chan_count :],
        "narrow",
        [(i, (i + 1) % narrow_count) for i in range(narrow_count)],
    )

    flat = prototype.reshape(-1)
    taps = jnp.stack(
        [
            lax.dynamic_update_slice(
                jnp.zeros((tap_count + 1) * chan_count, jnp.float32), flat, (station_shifts[s],)
            ).reshape(tap_count + 1, chan_count)
            for s in range(station_local)
        ],
        axis=1,
    )
    taps = jnp.repeat(taps, 2 * pol_count, axis=1)
    ids = jnp.arange(chan_count, dtype=jnp.int32)
    row_chan = (ids % fours) * fold + ids // fours
    turn = jnp.mod(
        row_chan[None, :, None] * (ids[None, None, :] - station_shifts[:, None, None]), chan_count
    )
    angle = turn.astype(jnp.float32) * (TWO_PI / chan_count)
    scale = 1.0 / math.sqrt(chan_count)
    cosine, sine = jnp.cos(angle) * scale, jnp.sin(angle) * scale
    table = jnp.concatenate(
        [
            jnp.concatenate([cosine, sine], axis=2),
            jnp.concatenate([-sine, cosine], axis=2),
        ],
        axis=1,
    ).astype(jnp.bfloat16)
    packed = pl.pallas_call(
        filter_kernel,
        out_shape=jax.ShapeDtypeStruct((sub_count, fours * quad, LANES), jnp.bfloat16),
        in_specs=[scalars] + [whole] * 5,
        out_specs=whole,
        scratch_shapes=[
            pltpu.VMEM((8, LANES), jnp.float32),
            pltpu.VMEM((chan_count // LANES, members * spectra * rows, LANES), jnp.float32),
            pltpu.VMEM((members, fours * quad, LANES), jnp.float32),
        ],
        compiler_params=params,
        name="filter",
    )(narrow_index.astype(jnp.int32)[None], volts, left, right, taps, table)

    local_rows = fours * quad // narrow_count
    packed = packed.reshape(sub_count * narrow_count, local_rows, LANES)
    packed = lax.all_to_all(packed, ("wide", "narrow"), 0, 0, tiled=True)
    packed = packed.reshape(wide_count, narrow_count, local_rows, LANES)

    early = jnp.arange(LANES) % spectra < LEAD
    tail = jnp.where(early, packed[:, 0], packed[:, narrow_count - 1])
    tail = lax.ppermute(tail, "sec", [(0, 1)])

    sub = wide_index
    channels = narrow_index * chan_local + jnp.arange(chan_local, dtype=jnp.int32)
    frequency = sub.astype(jnp.float32) + channels.astype(jnp.float32) / chan_count
    delays = jnp.transpose(beam_delays.reshape(beam_count, wide_count, station_local), (0, 2, 1))
    delays = jnp.repeat(delays, 2, axis=1).reshape(beam_count, 2 * station_count)
    phase = (TWO_PI * frequency)[:, None, None] * delays[None]
    norm = 1.0 / math.sqrt(station_count)
    cosine, sine = jnp.cos(phase) * norm, jnp.sin(phase) * norm
    is_real = jnp.arange(2 * station_count)[None, None, :] // wide_count % 2 == 0
    weights = jnp.concatenate(
        [jnp.where(is_real, cosine, sine), jnp.where(is_real, -sine, cosine)], axis=1
    ).astype(jnp.bfloat16)

    span = 2 * SEG
    bins = jnp.arange(span, dtype=jnp.int32)
    signed = jnp.where(bins < span // 2, bins, bins - span)
    dm_value = jnp.sum(jnp.where(jnp.arange(sub_count) == sub, dm_index, 0))
    phase_index = dm_value * signed[None, :] * (signed[None, :] + channels[:, None])
    angle_index = jnp.mod(
        phase_index[:, None, :] + 2 * bins[None, :, None] * bins[None, None, :], 2 * span
    )
    angles = angle_index.astype(jnp.float32) * (math.pi / span)
    kern = jnp.stack(
        [jnp.sum(jnp.cos(angles), axis=-1) / span, jnp.sum(jnp.sin(angles), axis=-1) / span],
        axis=1,
    ).astype(jnp.bfloat16)
    times = jnp.arange(block_len, dtype=jnp.int32)
    lag = jnp.mod(times[None, :] - bins[:, None], span)
    pick = (lag[None] == bins[:, None, None]).astype(jnp.bfloat16)
    kern = jnp.einsum("crd,dab->crab", kern, pick, preferred_element_type=jnp.float32)
    order = (jnp.mod(times - LEAD, block_len)[:, None] == times[None, :]).astype(jnp.float32)

    partial = pl.pallas_call(
        beam_kernel,
        out_shape=jax.ShapeDtypeStruct((beam_count, block_len), jnp.float32),
        in_specs=[whole] * 5,
        out_specs=whole,
        scratch_shapes=[
            pltpu.VMEM((narrow_count, wide_count * 8, LANES), jnp.float32),
            pltpu.VMEM((wide_count * 8, LANES), jnp.float32),
            pltpu.VMEM((beam_count, block_len), jnp.float32),
        ],
        compiler_params=params,
        name="beams",
    )(packed, tail, weights, kern, order)

    partial = partial.reshape(narrow_count, beam_count // narrow_count, block_len)
    partial = lax.all_to_all(partial, "narrow", 0, 0, tiled=True)
    share = jnp.sum(partial, axis=0) / chan_count
    subs = jnp.arange(sub_count, dtype=jnp.int32)
    owner = jnp.sum(jnp.where(subs == sub, owners, 0))
    goes = jnp.arange(wide_count, dtype=jnp.int32) == owner
    outgoing = jnp.where(goes[:, None, None], share[None], 0.0)
    arrived = lax.all_to_all(outgoing, "wide", 0, 0, tiled=True)
    owned = owners == wide_index
    rank = jnp.cumsum(owned.astype(jnp.int32)) - 1
    slots = jnp.arange(SUBBAND_LIMIT, dtype=jnp.int32)
    held = owned[None, :] & (rank[None, :] == slots[:, None])
    chosen = jnp.sum(jnp.where(held, subs[None, :], 0), axis=1)
    result = jnp.take(arrived, chosen, axis=0)
    return jnp.where(jnp.any(held, axis=1)[:, None, None], result, 0.0)[None]


def solution(mesh):
    placed = (P("sec", None, "wide", None, None, "narrow"), P(), P(), P("wide"), P(), P())
    return jax.shard_map(
        shards,
        mesh=mesh,
        in_specs=placed,
        out_specs=P("sec", "wide", "narrow", None),
        check_vma=False,
    )
```

time: 188 us -> 169 us (0.90)
  blocking collectives: 22.5 us -> 0 us
  waiting for transfers between devices: 87.1 us -> 68.3 us
  starting transfers between devices: 26.7 us -> 38.4 us
  other arithmetic: 12.7 us -> 21.7 us
  Pallas kernels: 22.2 us -> 25.7 us
    all_to_all x3, waiting for transfers between devices: 87.1 us -> 53.9 us  [the longest x1 36.7 us: shards(): packed = lax.all_to_all(packed, ('wide', 'narrow'), 0, 0, tiled=True)]
    all_to_all x1 -> x0, blocking collectives: 22.5 us -> none  [shards(): arrived = lax.all_to_all(outgoing, 'wide', 0, 0, tiled=True)]
    ppermute x0 -> x3, waiting for transfers between devices: none -> 14.3 us  [the longest x1 14.3 us: shards(): lax.ppermute(volts[..., :ahead], 'narrow', [(i, i - 1) for i in range(1,...]
    ppermute x0 -> x3, starting transfers between devices: none -> 6.25 us  [the longest x1 3.49 us: shards(): lax.ppermute(volts[..., piece_len - LEAD * chan_count:], 'narrow', [(i, (...]
    all_to_all x3, starting transfers between devices: 26.7 us -> 32.1 us  [the longest x1 21.7 us: shards(): packed = lax.all_to_all(packed, ('wide', 'narrow'), 0, 0, tiled=True)]
    another operation x2 -> x4, other arithmetic: 6.51 us -> 11 us
    pallas_call x2, Pallas kernels: 22.2 us -> 25.7 us  [the longest x1 14.1 us: shards(): pl.pallas_call(filter_kernel, out_shape=jax.ShapeDtypeStruct((sub_count,...]
    unnamed x15 -> x17, local copies, waits for them, and re-layouts: 2.67 us -> 0.75 us
  transfers between devices with their start and end apart: 3 -> 6, of which waited for: 3 -> 4; matrix products, arithmetic and copies ran while one was open for 8% -> 15% of each run, Pallas kernels for 0% -> 0%
where the time goes in v4:
time: 169 us; the launch traced here: 168 us
  waiting for transfers between devices  68.3 us (40%)
  starting transfers between devices  38.4 us (23%)
  Pallas kernels  25.7 us (15%)
  other arithmetic  21.7 us (13%)
  local copies, waits for them, and re-layouts  9.11 us (5%)
  between operations  4.16 us (2%)
    all_to_all x1, waiting for transfers between devices, shards(): packed = lax.all_to_all(packed, ('wide', 'narrow'), 0, 0, tiled=True)  36.7 us
    all_to_all x1, starting transfers between devices, shards(): packed = lax.all_to_all(packed, ('wide', 'narrow'), 0, 0, tiled=True)  21.7 us
    ppermute x1, waiting for transfers between devices, shards(): lax.ppermute(volts[..., :ahead], 'narrow', [(i, i - 1) for i in range(1,...  14.3 us
    pallas_call x1, Pallas kernels, shards(): pl.pallas_call(filter_kernel, out_shape=jax.ShapeDtypeStruct((sub_count,...  14.1 us
    pallas_call x1, Pallas kernels, shards(): pl.pallas_call(beam_kernel, out_shape=jax.ShapeDtypeStruct((beam_count, b...  11.6 us
    another operation x4, other arithmetic  11 us
    all_to_all x1, waiting for transfers between devices, shards(): arrived = lax.all_to_all(outgoing, 'wide', 0, 0, tiled=True)  9.7 us
    all_to_all x1, waiting for transfers between devices, shards(): partial = lax.all_to_all(partial, 'narrow', 0, 0, tiled=True)  7.52 us
  transfers between devices with their start and end apart: 6, of which 4 were waited for; matrix products, arithmetic and copies ran while one was open for 15% of the time, Pallas kernels for 0%

profile of v4, /device:TPU:6, one launch (start us, length us, event | category | flops | bytes accessed | tf_op | source)
XLA Modules:
  0.0 167.6 jit_solution(15975840637267228389)
XLA Ops:
  0.0 2.7 %reshape.332.own_ref = bf16[32,8,4096]{2,1,0:T(8,128)(2,1)S(1)} reshape(bf16[1,32,2,2,2,4096]{5,4,3,2,1,0:T(2,128)(2,1)} %param.6) | data formatting | bytes 4194304 | tf_op jit(solution)/shard_map/reshape | solution.py:258
  2.8 0.0 copy-start
  2.8 0.0 copy-start.5
  2.8 0.0 copy-start.4
  2.8 0.1 slice.26
  2.9 3.5 %collective-permute-start = (bf16[32,8,2048]{2,1,0:T(8,128)(2,1)S(1)}, bf16[32,8,2048]{2,1,0:T(8,128)(2,1)}, u32[]{:S(2)}, u32[]{:S(2)}) collective-permute-start(bf16[32,8,2048]{2,1,0:T(8,128)(2,1)S(1)} %slice.26), channel_id=1, source_target_pairs={{0,1},{1,2},{2,3},{3,4},{4,5},{5,6},{6,7},{7,0},{8,9},{9,10},{10,1... | collective-permute-start | bytes 3145736 | tf_op jit(solution)/shard_map/ppermute | solution.py:263
  6.4 1.0 slice.27
  7.4 1.3 collective-permute-start.1
  8.7 0.0 copy-done.5
  8.7 0.6 fusion.42
  11.9 0.0 copy-done.4
  12.6 0.4 dynamic_update_slice.7
  13.0 0.0 copy-done
  13.6 0.4 dynamic_update_slice.6
  14.1 0.7 reshape.334.taps_ref
  14.8 0.1 iota_subtract_fusion
  14.9 2.5 %fusion.16 = (bf16[2,256,256]{2,1,0:T(8,128)(2,1)S(1)}, bf16[2,256,256]{2,1,0:T(8,128)(2,1)S(1)}, bf16[2,256,256]{2,1,0:T(8,128)(2,1)S(1)}) fusion(s32[2,256]{1,0:T(2,128)S(1)} %iota_subtract_fusion, s32[256]{0:T(256)S(1)} %fusion.32), kind=kLoop, calls=%fused_computation.36 | loop fusion | flops 2621440 | bytes 789504 | tf_op jit(solution)/shard_map/convert.12
  17.4 1.1 maximum_maximum_fusion.table_ref
  18.5 14.3 %collective-permute-done.1.right_ref = bf16[32,8,1920]{2,1,0:T(8,128)(2,1)} collective-permute-done((bf16[32,8,1920]{2,1,0:T(8,128)(2,1)}, bf16[32,8,1920]{2,1,0:T(8,128)(2,1)}, u32[]{:S(2)}, u32[]{:S(2)}) %collective-permute-start.1) | collective-permute-done | bytes 983072 | tf_op jit(solution)/shard_map/ppermute | solution.py:260
  32.8 0.0 collective-permute-done.left_ref
  32.8 14.1 %filter.1 = bf16[32,256,128]{2,1,0:T(8,128)(2,1)} custom-call(s32[1]{0:T(128)} %bitcast.1.where_ref, bf16[32,8,4096]{2,1,0:T(8,128)(2,1)} %copy-done, bf16[32,8,2048]{2,1,0:T(8,128)(2,1)} %collective-permute-done.left_ref, bf16[32,8,1920]{2,1,0:T(8,128)(2,1)} %collective-permute-done.1.right_ref, f32[17,8,256]{2,1,0:T(8,128)} %reshape.334.taps_ref, ...), custom_call_target="tpu_custom_call" | custom-call | tf_op jit(solution)/shard_map/filter/pallas_call | solution.py:295
  47.0 0.0 copy-start.3
  47.0 0.0 copy-start.6
  47.0 0.0 copy-start.7
  47.0 21.7 %all-to-all-start = ((bf16[256,32,128]{2,1,0:T(8,128)(2,1)}), bf16[256,32,128]{2,1,0:T(8,128)(2,1)S(1)}, u32[]{:S(2)}, u32[]{:S(2)}) async-start(bf16[256,32,128]{2,1,0:T(8,128)(2,1)} %bitcast.49), calls=%async_computation | async-start | bytes 4194304 | tf_op jit(solution)/shard_map/all_to_all | solution.py:311
  68.7 0.0 copy-done.3
  68.7 0.1 copy.21
  68.8 0.0 copy-done.6
  68.9 0.1 copy.17
  69.0 0.1 reduce-window.8
  69.1 0.0 copy-done.7
  69.1 0.6 fusion.35
  69.7 0.6 compare_select_fusion.1
  70.4 0.6 fusion.34
  71.0 0.1 add_reduce_fusion
  71.1 8.4 %fusion.3 = (bf16[32,128,128]{2,1,0:T(8,128)(2,1)S(1)}, bf16[32,128,128]{2,1,0:T(8,128)(2,1)S(1)}) fusion(f32[128,128]{1,0:T(8,128)S(1)} %copy.21, f32[32]{0:T(128)S(1)} %add_multiply_fusion.1, pred[128]{0:T(512)(128)(4,1)S(1)} %fusion.37), kind=kLoop, calls=%fused_computation.6 | loop fusion | flops 4194304 | bytes 2162944 | tf_op jit(solution)/shard_map/convert.5
  79.6 1.6 pad_maximum_fusion.weights_ref
  81.1 0.1 iota_multiply_fusion
  81.2 0.1 add_multiply_fusion
  81.3 2.5 %cosine_reduce_fusion = (f32[32,32]{1,0:T(8,128)S(1)}, f32[32,32]{1,0:T(8,128)S(1)}) fusion(s32[32,32]{1,0:T(8,128)S(1)} %iota_multiply_fusion, s32[32,32]{1,0:T(8,128)S(1)} %add_multiply_fusion), kind=kLoop, calls=%fused_computation.30 | loop fusion | flops 522240 | bytes 16384 | tf_op jit(solution)/shard_map/reduce_sum | solution.py:341
  83.8 0.3 fusion.14
  84.1 36.7 %all-to-all-done = bf16[256,32,128]{2,1,0:T(8,128)(2,1)S(1)} async-done(((bf16[256,32,128]{2,1,0:T(8,128)(2,1)}), bf16[256,32,128]{2,1,0:T(8,128)(2,1)S(1)}, u32[]{:S(2)}, u32[]{:S(2)}) %all-to-all-start) | async-done | bytes 2097184 | tf_op jit(solution)/shard_map/all_to_all | solution.py:311
  120.8 0.0 copy-start.1
  120.9 1.5 collective-permute-start.2
  122.4 1.6 copy.22.kern_ref
  123.9 0.7 fusion.19.order_ref
  124.7 0.0 collective-permute-done.2.tail_ref
  124.7 0.0 copy-done.1
  124.7 0.0 copy-start.2
  124.7 0.7 copy-done.2
  125.4 11.6 %beams.1 = f32[128,128]{1,0:T(8,128)} custom-call(bf16[32,8,32,128]{3,2,1,0:T(8,128)(2,1)} %bitcast.48, bf16[32,32,128]{2,1,0:T(8,128)(2,1)} %copy-done.2, bf16[32,256,128]{2,1,0:T(8,128)(2,1)} %pad_maximum_fusion.weights_ref, f32[32,2,32,128]{3,2,1,0:T(8,128)} %copy.22.kern_ref, f32[128,128]{1,0:T(8,128)} %fusion.19.order_ref), custom_call_target="tpu_custom_call" | custom-call | tf_op jit(solution)/shard_map/beams/pallas_call | solution.py:350
  137.0 3.3 %all-to-all-start.1 = ((f32[8,16,128]{2,1,0:T(8,128)}), f32[8,16,128]{2,1,0:T(8,128)S(1)}, u32[]{:S(2)}, u32[]{:S(2)}) async-start(f32[8,16,128]{2,1,0:T(8,128)} %bitcast.50), calls=%async_computation.1 | async-start | bytes 131072 | tf_op jit(solution)/shard_map/all_to_all | solution.py:365
  140.3 0.7 iota_compare_fusion.2
  141.0 0.1 select_reduce_fusion
  141.1 7.5 %all-to-all-done.1 = f32[8,16,128]{2,1,0:T(8,128)S(1)} async-done(((f32[8,16,128]{2,1,0:T(8,128)}), f32[8,16,128]{2,1,0:T(8,128)S(1)}, u32[]{:S(2)}, u32[]{:S(2)}) %all-to-all-start.1) | async-done | bytes 65568 | tf_op jit(solution)/shard_map/all_to_all | solution.py:365
  148.7 0.8 broadcast_select_fusion
  149.5 7.0 %all-to-all-start.2 = ((f32[32,16,128]{2,1,0:T(8,128)}), f32[32,16,128]{2,1,0:T(8,128)S(1)}, u32[]{:S(2)}, u32[]{:S(2)}) async-start(f32[32,16,128]{2,1,0:T(8,128)} %broadcast_select_fusion), calls=%async_computation.2 | async-start | bytes 524288 | tf_op jit(solution)/shard_map/all_to_all | solution.py:371
  156.5 0.1 fusion.33
  156.7 9.7 %all-to-all-done.2 = f32[32,16,128]{2,1,0:T(8,128)S(1)} async-done(((f32[32,16,128]{2,1,0:T(8,128)}), f32[32,16,128]{2,1,0:T(8,128)S(1)}, u32[]{:S(2)}, u32[]{:S(2)}) %all-to-all-start.2) | async-done | bytes 262176 | tf_op jit(solution)/shard_map/all_to_all | solution.py:371
  166.4 0.5 gather_fusion
  166.9 0.7 fusion.23
  (26 shorter events, 0.3 us)
Async XLA Ops:
  2.8 10.2 %copy-start = (bf16[32,8,4096]{2,1,0:T(8,128)(2,1)}, bf16[32,8,4096]{2,1,0:T(8,128)(2,1)S(1)}, u32[]{:S(2)}) copy-start(bf16[32,8,4096]{2,1,0:T(8,128)(2,1)S(1)} %reshape.332.own_ref) | copy-start | bytes 6291460
  2.8 6.0 %copy-start.5 = (s32[2]{0:T(128)S(1)}, s32[2]{0:T(128)}, u32[]{:S(2)}) copy-start(s32[2]{0:T(128)} %param.9) | copy-start | bytes 28
  2.8 9.2 %copy-start.4 = (f32[16,256]{1,0:T(8,128)S(1)}, f32[16,256]{1,0:T(8,128)}, u32[]{:S(2)}) copy-start(f32[16,256]{1,0:T(8,128)} %param.7) | copy-start | bytes 49156
  2.9 30.0 %collective-permute-start = (bf16[32,8,2048]{2,1,0:T(8,128)(2,1)S(1)}, bf16[32,8,2048]{2,1,0:T(8,128)(2,1)}, u32[]{:S(2)}, u32[]{:S(2)}) collective-permute-start(bf16[32,8,2048]{2,1,0:T(8,128)(2,1)S(1)} %slice.26), channel_id=1, source_target_pairs={{0,1},{1,2},{2,3},{3,4},{4,5},{5,6},{6,7},{7,0},{8,9},{9,10},{10,1... | collective-permute-start | bytes 3145736 | tf_op jit(solution)/shard_map/ppermute | solution.py:263
  7.4 25.4 %collective-permute-start.1 = (bf16[32,8,1920]{2,1,0:T(8,128)(2,1)}, bf16[32,8,1920]{2,1,0:T(8,128)(2,1)}, u32[]{:S(2)}, u32[]{:S(2)}) collective-permute-start(bf16[32,8,1920]{2,1,0:T(8,128)(2,1)} %slice.27), channel_id=1, source_target_pairs={{1,0},{2,1},{3,2},{4,3},{5,4},{6,5},{7,6},{9,8},{10,9},{11,10},{12... | collective-permute-start | bytes 2949128 | tf_op jit(solution)/shard_map/ppermute | solution.py:260
  47.0 21.8 %copy-start.3 = (f32[128,64]{0,1:T(8,128)S(1)}, f32[128,64]{0,1:T(8,128)}, u32[]{:S(2)}) copy-start(f32[128,64]{0,1:T(8,128)} %param.8) | copy-start | bytes 98308
  47.0 21.9 %copy-start.6 = (s32[32]{0:T(128)S(1)}, s32[32]{0:T(128)}, u32[]{:S(2)}) copy-start(s32[32]{0:T(128)} %param.11) | copy-start | bytes 388
  47.0 22.1 %copy-start.7 = (s32[32]{0:T(128)S(1)}, s32[32]{0:T(128)}, u32[]{:S(2)}) copy-start(s32[32]{0:T(128)} %param.10) | copy-start | bytes 388
  47.0 73.9 %all-to-all-start = ((bf16[256,32,128]{2,1,0:T(8,128)(2,1)}), bf16[256,32,128]{2,1,0:T(8,128)(2,1)S(1)}, u32[]{:S(2)}, u32[]{:S(2)}) async-start(bf16[256,32,128]{2,1,0:T(8,128)(2,1)} %bitcast.49), calls=%async_computation | async-start | bytes 4194304 | tf_op jit(solution)/shard_map/all_to_all | solution.py:311
  120.8 3.8 %copy-start.1 = (bf16[256,32,128]{2,1,0:T(8,128)(2,1)}, bf16[256,32,128]{2,1,0:T(8,128)(2,1)S(1)}, u32[]{:S(2)}) copy-start(bf16[256,32,128]{2,1,0:T(8,128)(2,1)S(1)} %all-to-all-done) | copy-start | bytes 6291460
  120.9 3.8 %collective-permute-start.2 = (bf16[32,32,128]{2,1,0:T(8,128)(2,1)S(1)}, bf16[32,32,128]{2,1,0:T(8,128)(2,1)S(1)}, u32[]{:S(2)}, u32[]{:S(2)}) collective-permute-start(bf16[32,32,128]{2,1,0:T(8,128)(2,1)S(1)} %fusion.17), channel_id=1, source_target_pairs={{0,256},{1,257},{2,258},{3,259},{4,260},{5,261},{6,262},{7,263},{8... | collective-permute-start | bytes 786440 | tf_op jit(solution)/shard_map/ppermute | solution.py:316
  124.7 0.7 copy-start.2
  137.0 11.7 %all-to-all-start.1 = ((f32[8,16,128]{2,1,0:T(8,128)}), f32[8,16,128]{2,1,0:T(8,128)S(1)}, u32[]{:S(2)}, u32[]{:S(2)}) async-start(f32[8,16,128]{2,1,0:T(8,128)} %bitcast.50), calls=%async_computation.1 | async-start | bytes 131072 | tf_op jit(solution)/shard_map/all_to_all | solution.py:365
  149.5 16.9 %all-to-all-start.2 = ((f32[32,16,128]{2,1,0:T(8,128)}), f32[32,16,128]{2,1,0:T(8,128)S(1)}, u32[]{:S(2)}, u32[]{:S(2)}) async-start(f32[32,16,128]{2,1,0:T(8,128)} %broadcast_select_fusion), calls=%async_computation.2 | async-start | bytes 524288 | tf_op jit(solution)/shard_map/all_to_all | solution.py:371

commit v5 on v4

--- a/solution.py
+++ b/solution.py
@@ -13,13 +13,16 @@
 LEAD = 8
 LANES = 128
 TWO_PI = 2.0 * math.pi
+UNROLL = 2
+SHARES = 2
 VMEM_BYTES = 56 * 1024 * 1024
 
 
 def filter_kernel(
-    where_ref, own_ref, left_ref, right_ref, taps_ref, table_ref, out_ref, frames, filtered, packed
+    where_ref, own_ref, left_ref, right_ref, taps_ref, table_ref, *refs
 ):
-    sub_count, rows, piece_len = own_ref.shape
+    out_ref, filtered, packed = refs[-3:]
+    members, rows, piece_len = own_ref.shape
     tap_count, _, chan_count = taps_ref.shape
     station_count = table_ref.shape[0]
     pol_count = rows // (2 * station_count)
@@ -28,87 +31,87 @@
     halves = chan_count // LANES
     width = pol_count * spectra
     fold = LANES // width
-    members = filtered.shape[1] // (spectra * rows)
     fours = chan_count // fold
     zero = jnp.zeros((rows, LANES), jnp.float32)
     follows = jnp.where(where_ref[0] == 0, 0.0, 1.0)
 
-    def one_batch(batch, carry):
-        def one_sub(member, inner):
-            sub = batch * members + member
-            for half in range(halves):
-                lanes = slice(half * LANES, half * LANES + LANES)
-                taps = [taps_ref[tap, :, lanes] for tap in range(tap_count)]
-
-                def load(ref, frame):
-                    low = frame * chan_count + half * LANES
-                    if low >= ref.shape[-1]:
-                        return zero
-                    return ref[sub, :, low : low + LANES].astype(jnp.float32)
-
-                own = [load(own_ref, frame) for frame in range(spectra)]
-                early = [load(left_ref, frame) for frame in range(LEAD)]
-                early += [frame * follows for frame in own]
-                late = own + [load(right_ref, frame) for frame in range(LEAD)]
-                for number in range(spectra):
-                    source = early[number:] if number < LEAD else late[number - LEAD :]
-                    total = taps[0] * source[0]
-                    for tap in range(1, tap_count):
-                        total = total + taps[tap] * source[tap]
-                    at = pl.multiple_of((member * spectra + number) * rows, rows)
-                    filtered[half, pl.ds(at, rows), :] = total
-            return inner
-
-        lax.fori_loop(0, members, one_sub, 0)
-        lane = lax.broadcasted_iota(jnp.int32, (fours, LANES), 1) // width
-        for station in range(station_count):
-            parts = []
-            for member in range(members):
-                for pol in range(pol_count):
-                    first = member * spectra * rows + (station * pol_count + pol) * 2
-                    parts.append(
-                        jnp.concatenate(
-                            [
-                                filtered[half, pl.ds(first + r, spectra, stride=rows), :].astype(
-                                    jnp.bfloat16
-                                )
-                                for r in range(2)
-                                for half in range(halves)
-                            ],
-                            axis=1,
-                        )
+    def one_sub(member, inner):
+        for half in range(halves):
+            lanes = slice(half * LANES, half * LANES + LANES)
+            taps = [taps_ref[tap, :, lanes] for tap in range(tap_count)]
+
+            def load(ref, frame):
+                low = frame * chan_count + half * LANES
+                if low >= ref.shape[-1]:
+                    return zero
+                return ref[member, :, low : low + LANES].astype(jnp.float32)
+
+            own = [load(own_ref, frame) for frame in range(spectra)]
+            early = [load(left_ref, frame) for frame in range(LEAD)]
+            early += [frame * follows for frame in own]
+            late = own + [load(right_ref, frame) for frame in range(LEAD)]
+            for number in range(spectra):
+                source = early[number:] if number < LEAD else late[number - LEAD :]
+                total = taps[0] * source[0]
+                for tap in range(1, tap_count):
+                    total = total + taps[tap] * source[tap]
+                at = pl.multiple_of((member * spectra + number) * rows, rows)
+                filtered[half, pl.ds(at, rows), :] = total
+        return inner
+
+    lax.fori_loop(0, members, one_sub, 0)
+    lane = lax.broadcasted_iota(jnp.int32, (fours, LANES), 1) // width
+    for station in range(station_count):
+        parts = []
+        for member in range(members):
+            for pol in range(pol_count):
+                first = member * spectra * rows + (station * pol_count + pol) * 2
+                parts.append(
+                    jnp.concatenate(
+                        [
+                            filtered[half, pl.ds(first + r, spectra, stride=rows), :].astype(
+                                jnp.bfloat16
+                            )
+                            for r in range(2)
+                            for half in range(halves)
+                        ],
+                        axis=1,
                     )
-            spectrum = lax.dot_general(
-                table_ref[station],
-                jnp.concatenate(parts, axis=0),
-                (((1,), (1,)), ((), ())),
-                preferred_element_type=jnp.float32,
-            )
-            for r in range(2):
-                for tile in range(members // fold):
-                    blocks = [
-                        spectrum[
-                            (r * fold + turn) * fours : (r * fold + turn + 1) * fours,
-                            tile * LANES : (tile + 1) * LANES,
-                        ]
-                        for turn in range(fold)
+                )
+        spectrum = lax.dot_general(
+            table_ref[station],
+            jnp.concatenate(parts, axis=0),
+            (((1,), (1,)), ((), ())),
+            preferred_element_type=jnp.float32,
+        )
+        for r in range(2):
+            for tile in range(members // fold):
+                blocks = [
+                    spectrum[
+                        (r * fold + turn) * fours : (r * fold + turn + 1) * fours,
+                        tile * LANES : (tile + 1) * LANES,
                     ]
-                    for member in range(fold):
-                        whole = None
-                        for turn, block in enumerate(blocks):
-                            shift = (turn - member) * width % LANES
-                            moved = pltpu.roll(block, shift, 1) if shift else block
-                            whole = moved if whole is None else jnp.where(lane == turn, moved, whole)
-                        packed[
-                            tile * fold + member,
-                            pl.ds(station * 2 + r, fours, stride=quad),
-                            :,
-                        ] = whole
-        for member in range(members):
-            out_ref[batch * members + member] = packed[member].astype(jnp.bfloat16)
-        return carry
-
-    lax.fori_loop(0, sub_count // members, one_batch, 0)
+                    for turn in range(fold)
+                ]
+                step = fold // 2
+                while step:
+                    low = (lane // step) % 2 == 0
+                    swapped = list(blocks)
+                    for first in range(fold):
+                        if first // step % 2 == 0:
+                            a, b = blocks[first], blocks[first + step]
+                            swapped[first] = jnp.where(low, a, pltpu.roll(b, step * width, 1))
+                            swapped[first + step] = jnp.where(
+                                low, pltpu.roll(a, LANES - step * width, 1), b
+                            )
+                    blocks = swapped
+                    step //= 2
+                for member, block in enumerate(blocks):
+                    packed[tile * fold + member, :, station * 2 + r] = block.reshape(
+                        fours // 8, 8, LANES
+                    )
+    for member in range(members):
+        out_ref[member] = packed[member].reshape(fours * quad, LANES).astype(jnp.bfloat16)
 
 
 def beam_kernel(
@@ -122,7 +125,7 @@
     width = pol_count * spectra
     fold = LANES // width
     quad = row_count * fold // chan_local
-    step_rows = 8
+    eight = row_count // quad
     span = 2 * SEG
     from_time = lax.broadcasted_iota(jnp.int32, (block_len, block_len), 0)
     to_time = lax.broadcasted_iota(jnp.int32, (block_len, block_len), 1)
@@ -134,9 +137,12 @@
     lane = lax.broadcasted_iota(jnp.int32, (source_count * quad, block_len), 1) // spectra
     total[...] = jnp.zeros_like(total)
 
-    def gathered(ref, inner):
+    def gathered(ref, number):
         return jnp.concatenate(
-            [ref[pl.ds(inner * quad + q, source_count, stride=step_rows), :] for q in range(quad)],
+            [
+                ref[pl.ds(q * eight + number, source_count, stride=row_count), :]
+                for q in range(quad)
+            ],
             axis=0,
         )
 
@@ -148,19 +154,18 @@
             [jnp.concatenate([real, imag], axis=1), jnp.concatenate([-imag, real], axis=1)], axis=0
         ).astype(jnp.bfloat16)
 
+    shape = (source_count * row_count, LANES)
+    for piece in range(piece_count):
+        held[piece] = spectra_ref[:, piece].astype(jnp.float32).reshape(shape)
+    held_tail[...] = tail_ref[...].astype(jnp.float32).reshape(shape)
+
     def one(step, carry):
-        at = pl.multiple_of(step * step_rows, step_rows)
-        shape = (source_count * step_rows, LANES)
-        for piece in range(piece_count):
-            held[piece] = (
-                spectra_ref[:, piece, pl.ds(at, step_rows), :].astype(jnp.float32).reshape(shape)
-            )
-        held_tail[...] = tail_ref[:, pl.ds(at, step_rows), :].astype(jnp.float32).reshape(shape)
-        for inner in range(step_rows // quad):
-            pieces = [gathered(held.at[piece], inner) for piece in range(piece_count)]
-            tail = gathered(held_tail, inner)
+        for inner in range(UNROLL):
+            number = step * UNROLL + inner
+            pieces = [gathered(held.at[piece], number) for piece in range(piece_count)]
+            tail = gathered(held_tail, number)
             for turn in range(fold):
-                chan = step * (step_rows // quad * fold) + inner * fold + turn
+                chan = number * fold + turn
                 parts = []
                 for pol in range(pol_count):
                     low = turn * width + pol * spectra
@@ -226,7 +231,7 @@
                 total[...] += both[:, :block_len] + both[:, block_len:]
         return carry
 
-    lax.fori_loop(0, row_count // step_rows, one, 0)
+    lax.fori_loop(0, eight // UNROLL, one, 0)
     power_ref[...] = jnp.dot(
         total[...],
         order_ref[...],
@@ -250,21 +255,29 @@
     chan_local = chan_count // narrow_count
     fold = LANES // (pol_count * spectra)
     fours = chan_count // fold
-    members = min(2 * fold, sub_count)
+    members = min(2 * fold, sub_count // SHARES)
     whole = pl.BlockSpec(memory_space=pltpu.VMEM)
     scalars = pl.BlockSpec(memory_space=pltpu.SMEM)
     params = pltpu.CompilerParams(vmem_limit_bytes=VMEM_BYTES)
 
     volts = voltages.reshape(sub_count, rows, piece_len)
     ahead = (tap_count - 1 - LEAD) * chan_count + MAXD
-    right = lax.ppermute(
-        volts[..., :ahead], "narrow", [(i, i - 1) for i in range(1, narrow_count)]
-    )
-    left = lax.ppermute(
-        volts[..., piece_len - LEAD * chan_count :],
-        "narrow",
-        [(i, (i + 1) % narrow_count) for i in range(narrow_count)],
-    )
+    share = sub_count // SHARES
+    ends = [
+        (
+            lax.ppermute(
+                volts[i * share : (i + 1) * share, :, piece_len - LEAD * chan_count :],
+                "narrow",
+                [(i, (i + 1) % narrow_count) for i in range(narrow_count)],
+            ),
+            lax.ppermute(
+                volts[i * share : (i + 1) * share, :, :ahead],
+                "narrow",
+                [(i, i - 1) for i in range(1, narrow_count)],
+            ),
+        )
+        for i in range(SHARES)
+    ]
 
     flat = prototype.reshape(-1)
     taps = jnp.stack(
@@ -292,19 +305,45 @@
         ],
         axis=1,
     ).astype(jnp.bfloat16)
-    packed = pl.pallas_call(
-        filter_kernel,
-        out_shape=jax.ShapeDtypeStruct((sub_count, fours * quad, LANES), jnp.bfloat16),
-        in_specs=[scalars] + [whole] * 5,
-        out_specs=whole,
-        scratch_shapes=[
-            pltpu.VMEM((8, LANES), jnp.float32),
-            pltpu.VMEM((chan_count // LANES, members * spectra * rows, LANES), jnp.float32),
-            pltpu.VMEM((members, fours * quad, LANES), jnp.float32),
-        ],
-        compiler_params=params,
-        name="filter",
-    )(narrow_index.astype(jnp.int32)[None], volts, left, right, taps, table)
+    packed = None
+    for i, (left, right) in enumerate(ends):
+        steps = share // members
+
+        def block(length, first):
+            return pl.BlockSpec((members, rows, length), lambda step: (step + first, 0, 0))
+
+        packed = pl.pallas_call(
+            filter_kernel,
+            grid=(steps,),
+            out_shape=jax.ShapeDtypeStruct((sub_count, fours * quad, LANES), jnp.bfloat16),
+            in_specs=[
+                scalars,
+                block(piece_len, i * steps),
+                block(LEAD * chan_count, 0),
+                block(ahead, 0),
+                whole,
+                whole,
+            ]
+            + [pl.BlockSpec(memory_space=pl.ANY)] * min(i, 1),
+            out_specs=pl.BlockSpec(
+                (members, fours * quad, LANES), lambda step, first=i * steps: (step + first, 0, 0)
+            ),
+            scratch_shapes=[
+                pltpu.VMEM((chan_count // LANES, members * spectra * rows, LANES), jnp.float32),
+                pltpu.VMEM((members, fours // 8, quad, 8, LANES), jnp.float32),
+            ],
+            input_output_aliases={6: 0} if i else {},
+            compiler_params=params,
+            name="filter",
+        )(
+            narrow_index.astype(jnp.int32)[None],
+            volts,
+            left,
+            right,
+            taps,
+            table,
+            *([packed] if i else []),
+        )
 
     local_rows = fours * quad // narrow_count
     packed = packed.reshape(sub_count * narrow_count, local_rows, LANES)
@@ -353,8 +392,8 @@
         in_specs=[whole] * 5,
         out_specs=whole,
         scratch_shapes=[
-            pltpu.VMEM((narrow_count, wide_count * 8, LANES), jnp.float32),
-            pltpu.VMEM((wide_count * 8, LANES), jnp.float32),
+            pltpu.VMEM((narrow_count, wide_count * local_rows, LANES), jnp.float32),
+            pltpu.VMEM((wide_count * local_rows, LANES), jnp.float32),
             pltpu.VMEM((beam_count, block_len), jnp.float32),
         ],
         compiler_params=params,
@@ -363,11 +402,11 @@
 
     partial = partial.reshape(narrow_count, beam_count // narrow_count, block_len)
     partial = lax.all_to_all(partial, "narrow", 0, 0, tiled=True)
-    share = jnp.sum(partial, axis=0) / chan_count
+    summed = jnp.sum(partial, axis=0) / chan_count
     subs = jnp.arange(sub_count, dtype=jnp.int32)
     owner = jnp.sum(jnp.where(subs == sub, owners, 0))
     goes = jnp.arange(wide_count, dtype=jnp.int32) == owner
-    outgoing = jnp.where(goes[:, None, None], share[None], 0.0)
+    outgoing = jnp.where(goes[:, None, None], summed[None], 0.0)
     arrived = lax.all_to_all(outgoing, "wide", 0, 0, tiled=True)
     owned = owners == wide_index
     rank = jnp.cumsum(owned.astype(jnp.int32)) - 1

time: 169 us -> 167 us (0.988)
  waiting for transfers between devices: 68.3 us -> 55.1 us
  starting transfers between devices: 38.4 us -> 46.4 us
  local copies, waits for them, and re-layouts: 9.11 us -> 11.7 us
    ppermute x2 -> x4, waiting for transfers between devices: 14.3 us -> 1.12 us  [the longest x2 1.11 us: shards(): lax.ppermute(volts[i * share:(i + 1) * share, :, :ahead], 'narrow', [(i,...]
    ppermute x2 -> x4, starting transfers between devices: 4.77 us -> 10.6 us  [the longest x2 8.02 us: shards(): lax.ppermute(volts[i * share:(i + 1) * share, :, piece_len - LEAD * chan_...]
    all_to_all x1, starting transfers between devices: 21.7 us -> 23.9 us  [shards(): packed = lax.all_to_all(packed, ('wide', 'narrow'), 0, 0, tiled=True)]
    pallas_call x1, Pallas kernels: 11.6 us -> 13.5 us  [shards(): pl.pallas_call(beam_kernel, out_shape=jax.ShapeDtypeStruct((beam_count, b...]
    pallas_call x1 -> x2, Pallas kernels: 14.1 us -> 13.2 us  [shards(): pl.pallas_call(filter_kernel, grid=(steps,), out_shape=jax.ShapeDtypeStru...]
  transfers between devices with their start and end apart: 6 -> 8, of which waited for: 4 -> 4; matrix products, arithmetic and copies ran while one was open for 15% -> 15% of each run, Pallas kernels for 0% -> 4%
where the time goes in v5:
time: 167 us; the launch traced here: 166 us
  waiting for transfers between devices  55.1 us (33%)
  starting transfers between devices  46.4 us (28%)
  Pallas kernels  26.6 us (16%)
  other arithmetic  21.6 us (13%)
  local copies, waits for them, and re-layouts  11.7 us (7%)
  between operations  4.21 us (3%)
    all_to_all x1, waiting for transfers between devices, shards(): packed = lax.all_to_all(packed, ('wide', 'narrow'), 0, 0, tiled=True)  36.8 us
    all_to_all x1, starting transfers between devices, shards(): packed = lax.all_to_all(packed, ('wide', 'narrow'), 0, 0, tiled=True)  23.9 us
    pallas_call x1, Pallas kernels, shards(): pl.pallas_call(beam_kernel, out_shape=jax.ShapeDtypeStruct((beam_count, b...  13.5 us
    pallas_call x2, Pallas kernels, shards(): pl.pallas_call(filter_kernel, grid=(steps,), out_shape=jax.ShapeDtypeStru...  13.2 us
    another operation x4, other arithmetic  11 us
    all_to_all x1, waiting for transfers between devices, shards(): arrived = lax.all_to_all(outgoing, 'wide', 0, 0, tiled=True)  9.68 us
    ppermute x2, starting transfers between devices, shards(): lax.ppermute(volts[i * share:(i + 1) * share, :, piece_len - LEAD * chan_...  8.02 us
    all_to_all x1, waiting for transfers between devices, shards(): partial = lax.all_to_all(partial, 'narrow', 0, 0, tiled=True)  7.52 us
  transfers between devices with their start and end apart: 8, of which 4 were waited for; matrix products, arithmetic and copies ran while one was open for 15% of the time, Pallas kernels for 4%

profile of v5, /device:TPU:6, one launch (start us, length us, event | category | flops | bytes accessed | tf_op | source)
XLA Modules:
  0.0 165.9 jit_solution(746083006054182054)
XLA Ops:
  0.0 2.7 %reshape.332.own_ref = bf16[32,8,4096]{2,1,0:T(8,128)(2,1)S(1)} reshape(bf16[1,32,2,2,2,4096]{5,4,3,2,1,0:T(2,128)(2,1)} %param.6) | data formatting | bytes 4194304 | tf_op jit(solution)/shard_map/reshape | solution.py:263
  2.8 0.0 copy-start
  2.8 0.0 copy-start.7
  2.8 0.0 copy-start.6
  2.8 1.1 fusion.43
  3.9 3.5 %collective-permute-start.2 = (bf16[16,8,2048]{2,1,0:T(8,128)(2,1)}, bf16[16,8,2048]{2,1,0:T(8,128)(2,1)S(1)}, u32[]{:S(2)}, u32[]{:S(2)}) collective-permute-start(bf16[16,8,2048]{2,1,0:T(8,128)(2,1)} %get-tuple-element.11), channel_id=1, source_target_pairs={{0,1},{1,2},{2,3},{3,4},{4,5},{5,6},{6,7},{7,0},{8,9},{9,10},{10,1... | collective-permute-start | bytes 1572872 | tf_op jit(solution)/shard_map/ppermute | solution.py:268
  7.3 1.1 fusion.42
  8.4 1.3 collective-permute-start.3
  9.7 4.6 %collective-permute-start = (bf16[16,8,2048]{2,1,0:T(8,128)(2,1)}, bf16[16,8,2048]{2,1,0:T(8,128)(2,1)S(1)}, u32[]{:S(2)}, u32[]{:S(2)}) collective-permute-start(bf16[16,8,2048]{2,1,0:T(8,128)(2,1)} %get-tuple-element.12), channel_id=1, source_target_pairs={{0,1},{1,2},{2,3},{3,4},{4,5},{5,6},{6,7},{7,0},{8,9},{9,10},{10,1... | collective-permute-start | bytes 1572872 | tf_op jit(solution)/shard_map/ppermute | solution.py:268
  14.2 1.3 collective-permute-start.1
  15.5 0.0 copy-done.7
  15.6 0.6 fusion.44
  18.7 0.1 iota_subtract_fusion
  18.8 0.0 copy-done.6
  19.5 0.4 dynamic_update_slice.6
  19.9 0.0 copy-done
  20.5 0.4 dynamic_update_slice.7
  21.0 0.7 reshape.334.taps_ref
  21.7 2.5 %fusion.16 = (bf16[2,256,256]{2,1,0:T(8,128)(2,1)S(1)}, bf16[2,256,256]{2,1,0:T(8,128)(2,1)S(1)}, bf16[2,256,256]{2,1,0:T(8,128)(2,1)S(1)}) fusion(s32[2,256]{1,0:T(2,128)S(1)} %iota_subtract_fusion, s32[256]{0:T(256)S(1)} %fusion.32), kind=kLoop, calls=%fused_computation.36 | loop fusion | flops 2621440 | bytes 789504 | tf_op jit(solution)/shard_map/convert.12
  24.2 1.1 maximum_maximum_fusion.table_ref
  25.3 0.0 collective-permute-done.3.right_ref
  25.3 0.0 collective-permute-done.2.left_ref
  25.3 0.0 copy-start.2
  25.3 0.8 copy-done.2
  26.1 6.6 %filter.2.refs_0_ = bf16[32,256,128]{2,1,0:T(8,128)(2,1)} custom-call(s32[1]{0:T(128)} %bitcast.1.where_ref, bf16[32,8,4096]{2,1,0:T(8,128)(2,1)} %copy-done, bf16[16,8,2048]{2,1,0:T(8,128)(2,1)} %copy-done.2, bf16[16,8,1920]{2,1,0:T(8,128)(2,1)} %collective-permute-done.3.right_ref, f32[17,8,256]{2,1,0:T(8,128)} %reshape.334.taps_ref, ...), custom_call_target="tpu_custom_call" | custom-call | tf_op jit(solution)/shard_map/filter/pallas_call | solution.py:315
  32.7 1.1 collective-permute-done.1.right_ref
  33.8 0.0 collective-permute-done.left_ref
  33.8 0.8 copy-done.3
  34.6 6.5 %filter.3 = bf16[32,256,128]{2,1,0:T(8,128)(2,1)} custom-call(s32[1]{0:T(128)} %bitcast.1.where_ref, bf16[32,8,4096]{2,1,0:T(8,128)(2,1)} %copy-done, bf16[16,8,2048]{2,1,0:T(8,128)(2,1)} %copy-done.3, bf16[16,8,1920]{2,1,0:T(8,128)(2,1)} %collective-permute-done.1.right_ref, f32[17,8,256]{2,1,0:T(8,128)} %reshape.334.taps_ref, ...), custom_call_target="tpu_custom_call", output_to_operand_aliasing={{}: (6, {})} | custom-call | tf_op jit(solution)/shard_map/filter/pallas_call | solution.py:315
  41.2 23.9 %all-to-all-start = ((bf16[256,32,128]{2,1,0:T(8,128)(2,1)}), bf16[256,32,128]{2,1,0:T(8,128)(2,1)S(1)}, u32[]{:S(2)}, u32[]{:S(2)}) async-start(bf16[256,32,128]{2,1,0:T(8,128)(2,1)} %bitcast.47), calls=%async_computation | async-start | bytes 4194304 | tf_op jit(solution)/shard_map/all_to_all | solution.py:350
  65.1 0.0 copy-done.5
  65.1 0.1 copy.22
  65.2 0.0 copy-done.8
  65.3 0.1 copy.18
  65.4 0.1 reduce-window.8
  65.5 0.0 copy-done.9
  65.5 0.6 fusion.35
  66.1 0.6 compare_select_fusion.1
  66.8 0.6 fusion.34
  67.4 0.1 add_reduce_fusion
  67.5 8.4 %fusion.3 = (bf16[32,128,128]{2,1,0:T(8,128)(2,1)S(1)}, bf16[32,128,128]{2,1,0:T(8,128)(2,1)S(1)}) fusion(f32[128,128]{1,0:T(8,128)S(1)} %copy.22, f32[32]{0:T(128)S(1)} %add_multiply_fusion.1, pred[128]{0:T(512)(128)(4,1)S(1)} %fusion.37), kind=kLoop, calls=%fused_computation.6 | loop fusion | flops 4194304 | bytes 2162944 | tf_op jit(solution)/shard_map/convert.5
  76.0 1.6 pad_maximum_fusion.weights_ref
  77.5 0.1 iota_multiply_fusion
  77.6 0.1 add_multiply_fusion
  77.7 2.5 %cosine_reduce_fusion = (f32[32,32]{1,0:T(8,128)S(1)}, f32[32,32]{1,0:T(8,128)S(1)}) fusion(s32[32,32]{1,0:T(8,128)S(1)} %iota_multiply_fusion, s32[32,32]{1,0:T(8,128)S(1)} %add_multiply_fusion), kind=kLoop, calls=%fused_computation.30 | loop fusion | flops 522240 | bytes 16384 | tf_op jit(solution)/shard_map/reduce_sum | solution.py:380
  80.2 0.3 fusion.14
  80.5 36.8 %all-to-all-done = bf16[256,32,128]{2,1,0:T(8,128)(2,1)S(1)} async-done(((bf16[256,32,128]{2,1,0:T(8,128)(2,1)}), bf16[256,32,128]{2,1,0:T(8,128)(2,1)S(1)}, u32[]{:S(2)}, u32[]{:S(2)}) %all-to-all-start) | async-done | bytes 2097184 | tf_op jit(solution)/shard_map/all_to_all | solution.py:350
  117.3 1.5 collective-permute-start.4
  118.8 1.6 copy.23.kern_ref
  120.4 0.7 fusion.19.order_ref
  121.1 0.0 collective-permute-done.4.tail_ref
  121.2 0.0 copy-done.1
  121.2 0.7 copy-done.4
  121.9 13.5 %beams.1 = f32[128,128]{1,0:T(8,128)} custom-call(bf16[32,8,32,128]{3,2,1,0:T(8,128)(2,1)} %bitcast.49, bf16[32,32,128]{2,1,0:T(8,128)(2,1)} %copy-done.4, bf16[32,256,128]{2,1,0:T(8,128)(2,1)} %pad_maximum_fusion.weights_ref, f32[32,2,32,128]{3,2,1,0:T(8,128)} %copy.23.kern_ref, f32[128,128]{1,0:T(8,128)} %fusion.19.order_ref), custom_call_target="tpu_custom_call" | custom-call | tf_op jit(solution)/shard_map/beams/pallas_call | solution.py:389
  135.3 3.3 %all-to-all-start.1 = ((f32[8,16,128]{2,1,0:T(8,128)}), f32[8,16,128]{2,1,0:T(8,128)S(1)}, u32[]{:S(2)}, u32[]{:S(2)}) async-start(f32[8,16,128]{2,1,0:T(8,128)} %bitcast.50), calls=%async_computation.1 | async-start | bytes 131072 | tf_op jit(solution)/shard_map/all_to_all | solution.py:404
  138.7 0.7 iota_compare_fusion.2
  139.3 0.1 select_reduce_fusion
  139.5 7.5 %all-to-all-done.1 = f32[8,16,128]{2,1,0:T(8,128)S(1)} async-done(((f32[8,16,128]{2,1,0:T(8,128)}), f32[8,16,128]{2,1,0:T(8,128)S(1)}, u32[]{:S(2)}, u32[]{:S(2)}) %all-to-all-start.1) | async-done | bytes 65568 | tf_op jit(solution)/shard_map/all_to_all | solution.py:404
  147.0 0.8 broadcast_select_fusion
  147.8 7.0 %all-to-all-start.2 = ((f32[32,16,128]{2,1,0:T(8,128)}), f32[32,16,128]{2,1,0:T(8,128)S(1)}, u32[]{:S(2)}, u32[]{:S(2)}) async-start(f32[32,16,128]{2,1,0:T(8,128)} %broadcast_select_fusion), calls=%async_computation.2 | async-start | bytes 524288 | tf_op jit(solution)/shard_map/all_to_all | solution.py:410
  154.9 0.1 fusion.33
  155.0 9.7 %all-to-all-done.2 = f32[32,16,128]{2,1,0:T(8,128)S(1)} async-done(((f32[32,16,128]{2,1,0:T(8,128)}), f32[32,16,128]{2,1,0:T(8,128)S(1)}, u32[]{:S(2)}, u32[]{:S(2)}) %all-to-all-start.2) | async-done | bytes 262176 | tf_op jit(solution)/shard_map/all_to_all | solution.py:410
  164.7 0.5 gather_fusion
  165.2 0.7 fusion.23
  (32 shorter events, 0.3 us)
Async XLA Ops:
  2.8 17.1 %copy-start = (bf16[32,8,4096]{2,1,0:T(8,128)(2,1)}, bf16[32,8,4096]{2,1,0:T(8,128)(2,1)S(1)}, u32[]{:S(2)}) copy-start(bf16[32,8,4096]{2,1,0:T(8,128)(2,1)S(1)} %reshape.332.own_ref) | copy-start | bytes 6291460
  2.8 12.8 %copy-start.7 = (s32[2]{0:T(128)S(1)}, s32[2]{0:T(128)}, u32[]{:S(2)}) copy-start(s32[2]{0:T(128)} %param.9) | copy-start | bytes 28
  2.8 16.0 %copy-start.6 = (f32[16,256]{1,0:T(8,128)S(1)}, f32[16,256]{1,0:T(8,128)}, u32[]{:S(2)}) copy-start(f32[16,256]{1,0:T(8,128)} %param.7) | copy-start | bytes 49156
  3.9 21.4 %collective-permute-start.2 = (bf16[16,8,2048]{2,1,0:T(8,128)(2,1)}, bf16[16,8,2048]{2,1,0:T(8,128)(2,1)S(1)}, u32[]{:S(2)}, u32[]{:S(2)}) collective-permute-start(bf16[16,8,2048]{2,1,0:T(8,128)(2,1)} %get-tuple-element.11), channel_id=1, source_target_pairs={{0,1},{1,2},{2,3},{3,4},{4,5},{5,6},{6,7},{7,0},{8,9},{9,10},{10,1... | collective-permute-start | bytes 1572872 | tf_op jit(solution)/shard_map/ppermute | solution.py:268
  8.4 16.9 %collective-permute-start.3 = (bf16[16,8,1920]{2,1,0:T(8,128)(2,1)}, bf16[16,8,1920]{2,1,0:T(8,128)(2,1)}, u32[]{:S(2)}, u32[]{:S(2)}) collective-permute-start(bf16[16,8,1920]{2,1,0:T(8,128)(2,1)} %get-tuple-element.9), channel_id=1, source_target_pairs={{1,0},{2,1},{3,2},{4,3},{5,4},{6,5},{7,6},{9,8},{10,9},{11,10},{12... | collective-permute-start | bytes 1474568 | tf_op jit(solution)/shard_map/ppermute | solution.py:273
  9.7 24.1 %collective-permute-start = (bf16[16,8,2048]{2,1,0:T(8,128)(2,1)}, bf16[16,8,2048]{2,1,0:T(8,128)(2,1)S(1)}, u32[]{:S(2)}, u32[]{:S(2)}) collective-permute-start(bf16[16,8,2048]{2,1,0:T(8,128)(2,1)} %get-tuple-element.12), channel_id=1, source_target_pairs={{0,1},{1,2},{2,3},{3,4},{4,5},{5,6},{6,7},{7,0},{8,9},{9,10},{10,1... | collective-permute-start | bytes 1572872 | tf_op jit(solution)/shard_map/ppermute | solution.py:268
  14.2 19.6 %collective-permute-start.1 = (bf16[16,8,1920]{2,1,0:T(8,128)(2,1)}, bf16[16,8,1920]{2,1,0:T(8,128)(2,1)}, u32[]{:S(2)}, u32[]{:S(2)}) collective-permute-start(bf16[16,8,1920]{2,1,0:T(8,128)(2,1)} %get-tuple-element.10), channel_id=1, source_target_pairs={{1,0},{2,1},{3,2},{4,3},{5,4},{6,5},{7,6},{9,8},{10,9},{11,10},{12... | collective-permute-start | bytes 1474568 | tf_op jit(solution)/shard_map/ppermute | solution.py:273
  25.3 0.8 copy-start.2
  33.8 0.8 copy-start.3
  41.2 23.9 %copy-start.5 = (f32[128,64]{0,1:T(8,128)S(1)}, f32[128,64]{0,1:T(8,128)}, u32[]{:S(2)}) copy-start(f32[128,64]{0,1:T(8,128)} %param.8) | copy-start | bytes 98308
  41.2 24.1 %copy-start.8 = (s32[32]{0:T(128)S(1)}, s32[32]{0:T(128)}, u32[]{:S(2)}) copy-start(s32[32]{0:T(128)} %param.11) | copy-start | bytes 388
  41.2 24.3 %copy-start.9 = (s32[32]{0:T(128)S(1)}, s32[32]{0:T(128)}, u32[]{:S(2)}) copy-start(s32[32]{0:T(128)} %param.10) | copy-start | bytes 388
  41.2 76.1 %all-to-all-start = ((bf16[256,32,128]{2,1,0:T(8,128)(2,1)}), bf16[256,32,128]{2,1,0:T(8,128)(2,1)S(1)}, u32[]{:S(2)}, u32[]{:S(2)}) async-start(bf16[256,32,128]{2,1,0:T(8,128)(2,1)} %bitcast.47), calls=%async_computation | async-start | bytes 4194304 | tf_op jit(solution)/shard_map/all_to_all | solution.py:350
  117.3 3.9 %copy-start.1 = (bf16[256,32,128]{2,1,0:T(8,128)(2,1)}, bf16[256,32,128]{2,1,0:T(8,128)(2,1)S(1)}, u32[]{:S(2)}) copy-start(bf16[256,32,128]{2,1,0:T(8,128)(2,1)S(1)} %all-to-all-done) | copy-start | bytes 6291460
  117.3 3.8 %collective-permute-start.4 = (bf16[32,32,128]{2,1,0:T(8,128)(2,1)S(1)}, bf16[32,32,128]{2,1,0:T(8,128)(2,1)S(1)}, u32[]{:S(2)}, u32[]{:S(2)}) collective-permute-start(bf16[32,32,128]{2,1,0:T(8,128)(2,1)S(1)} %fusion.17), channel_id=1, source_target_pairs={{0,256},{1,257},{2,258},{3,259},{4,260},{5,261},{6,262},{7,263},{8... | collective-permute-start | bytes 786440 | tf_op jit(solution)/shard_map/ppermute | solution.py:355
  121.2 0.7 copy-start.4
  135.3 11.7 %all-to-all-start.1 = ((f32[8,16,128]{2,1,0:T(8,128)}), f32[8,16,128]{2,1,0:T(8,128)S(1)}, u32[]{:S(2)}, u32[]{:S(2)}) async-start(f32[8,16,128]{2,1,0:T(8,128)} %bitcast.50), calls=%async_computation.1 | async-start | bytes 131072 | tf_op jit(solution)/shard_map/all_to_all | solution.py:404
  147.8 16.9 %all-to-all-start.2 = ((f32[32,16,128]{2,1,0:T(8,128)}), f32[32,16,128]{2,1,0:T(8,128)S(1)}, u32[]{:S(2)}, u32[]{:S(2)}) async-start(f32[32,16,128]{2,1,0:T(8,128)} %broadcast_select_fusion), calls=%async_computation.2 | async-start | bytes 524288 | tf_op jit(solution)/shard_map/all_to_all | solution.py:410

commit v6 on v5

--- a/solution.py
+++ b/solution.py
@@ -13,15 +13,17 @@
 LEAD = 8
 LANES = 128
 TWO_PI = 2.0 * math.pi
-UNROLL = 2
+UNROLL = 4
+PITCH = 40
 SHARES = 2
-VMEM_BYTES = 56 * 1024 * 1024
+FILTER_VMEM = 63 * 1024 * 1024
+VMEM_BYTES = 48 * 1024 * 1024
 
 
 def filter_kernel(
-    where_ref, own_ref, left_ref, right_ref, taps_ref, table_ref, *refs
+    where_ref, shifts_ref, own_ref, left_ref, right_ref, prototype_ref, table_ref, *refs
 ):
-    out_ref, filtered, packed = refs[-3:]
+    out_ref, taps_ref, filtered, packed = refs[-4:]
     members, rows, piece_len = own_ref.shape
     tap_count, _, chan_count = taps_ref.shape
     station_count = table_ref.shape[0]
@@ -33,6 +35,26 @@
     fold = LANES // width
     fours = chan_count // fold
     zero = jnp.zeros((rows, LANES), jnp.float32)
+
+    @pl.when(pl.program_id(0) == 0)
+    def _():
+        lane = lax.broadcasted_iota(jnp.int32, prototype_ref.shape[1:], 1)
+        moved = [
+            jnp.where(
+                lane < shifts_ref[station],
+                pltpu.roll(prototype_ref[1], shifts_ref[station], 1),
+                pltpu.roll(prototype_ref[0], shifts_ref[station], 1),
+            )
+            for station in range(station_count)
+        ]
+        row = lax.broadcasted_iota(jnp.int32, (rows, chan_count), 0) // (2 * pol_count)
+        for tap in range(tap_count):
+            whole = jnp.broadcast_to(moved[0][tap : tap + 1], (rows, chan_count))
+            for station in range(1, station_count):
+                other = jnp.broadcast_to(moved[station][tap : tap + 1], (rows, chan_count))
+                whole = jnp.where(row == station, other, whole)
+            taps_ref[tap] = whole
+
     follows = jnp.where(where_ref[0] == 0, 0.0, 1.0)
 
     def one_sub(member, inner):
@@ -140,7 +162,7 @@
     def gathered(ref, number):
         return jnp.concatenate(
             [
-                ref[pl.ds(q * eight + number, source_count, stride=row_count), :]
+                ref[pl.ds(q * eight + number, source_count, stride=PITCH), :]
                 for q in range(quad)
             ],
             axis=0,
@@ -154,10 +176,15 @@
             [jnp.concatenate([real, imag], axis=1), jnp.concatenate([-imag, real], axis=1)], axis=0
         ).astype(jnp.bfloat16)
 
-    shape = (source_count * row_count, LANES)
     for piece in range(piece_count):
-        held[piece] = spectra_ref[:, piece].astype(jnp.float32).reshape(shape)
-    held_tail[...] = tail_ref[...].astype(jnp.float32).reshape(shape)
+        for source in range(source_count):
+            held[piece, source * PITCH : source * PITCH + row_count] = spectra_ref[
+                source, piece
+            ].astype(jnp.float32)
+    for source in range(source_count):
+        held_tail[source * PITCH : source * PITCH + row_count] = tail_ref[source].astype(
+            jnp.float32
+        )
 
     def one(step, carry):
         for inner in range(UNROLL):
@@ -261,17 +288,21 @@
     params = pltpu.CompilerParams(vmem_limit_bytes=VMEM_BYTES)
 
     volts = voltages.reshape(sub_count, rows, piece_len)
+
+    def cut(first, last, low, high):
+        return voltages[0, first:last, :, :, :, low:high].reshape(last - first, rows, high - low)
+
     ahead = (tap_count - 1 - LEAD) * chan_count + MAXD
     share = sub_count // SHARES
     ends = [
         (
             lax.ppermute(
-                volts[i * share : (i + 1) * share, :, piece_len - LEAD * chan_count :],
+                cut(i * share, (i + 1) * share, piece_len - LEAD * chan_count, piece_len),
                 "narrow",
                 [(i, (i + 1) % narrow_count) for i in range(narrow_count)],
             ),
             lax.ppermute(
-                volts[i * share : (i + 1) * share, :, :ahead],
+                cut(i * share, (i + 1) * share, 0, ahead),
                 "narrow",
                 [(i, i - 1) for i in range(1, narrow_count)],
             ),
@@ -279,17 +310,10 @@
         for i in range(SHARES)
     ]
 
-    flat = prototype.reshape(-1)
-    taps = jnp.stack(
-        [
-            lax.dynamic_update_slice(
-                jnp.zeros((tap_count + 1) * chan_count, jnp.float32), flat, (station_shifts[s],)
-            ).reshape(tap_count + 1, chan_count)
-            for s in range(station_local)
-        ],
-        axis=1,
+    filler = -(tap_count + 1) % 8
+    both = jnp.stack(
+        [jnp.pad(prototype, ((0, filler + 1), (0, 0))), jnp.pad(prototype, ((1, filler), (0, 0)))]
     )
-    taps = jnp.repeat(taps, 2 * pol_count, axis=1)
     ids = jnp.arange(chan_count, dtype=jnp.int32)
     row_chan = (ids % fours) * fold + ids // fours
     turn = jnp.mod(
@@ -318,6 +342,7 @@
             out_shape=jax.ShapeDtypeStruct((sub_count, fours * quad, LANES), jnp.bfloat16),
             in_specs=[
                 scalars,
+                scalars,
                 block(piece_len, i * steps),
                 block(LEAD * chan_count, 0),
                 block(ahead, 0),
@@ -329,18 +354,20 @@
                 (members, fours * quad, LANES), lambda step, first=i * steps: (step + first, 0, 0)
             ),
             scratch_shapes=[
+                pltpu.VMEM((tap_count + 1, rows, chan_count), jnp.float32),
                 pltpu.VMEM((chan_count // LANES, members * spectra * rows, LANES), jnp.float32),
                 pltpu.VMEM((members, fours // 8, quad, 8, LANES), jnp.float32),
             ],
-            input_output_aliases={6: 0} if i else {},
-            compiler_params=params,
+            input_output_aliases={7: 0} if i else {},
+            compiler_params=pltpu.CompilerParams(vmem_limit_bytes=FILTER_VMEM),
             name="filter",
         )(
             narrow_index.astype(jnp.int32)[None],
+            station_shifts,
             volts,
             left,
             right,
-            taps,
+            both,
             table,
             *([packed] if i else []),
         )
@@ -392,8 +419,8 @@
         in_specs=[whole] * 5,
         out_specs=whole,
         scratch_shapes=[
-            pltpu.VMEM((narrow_count, wide_count * local_rows, LANES), jnp.float32),
-            pltpu.VMEM((wide_count * local_rows, LANES), jnp.float32),
+            pltpu.VMEM((narrow_count, wide_count * PITCH, LANES), jnp.float32),
+            pltpu.VMEM((wide_count * PITCH, LANES), jnp.float32),
             pltpu.VMEM((beam_count, block_len), jnp.float32),
         ],
         compiler_params=params,

time: 167 us -> 161 us (0.964)
  Pallas kernels: 26.6 us -> 21.7 us
  between operations: 4.21 us -> 0.3 us
  waiting for transfers between devices: 55.1 us -> 58 us
  local copies, waits for them, and re-layouts: 11.7 us -> 13.5 us
  starting transfers between devices: 46.4 us -> 44.7 us
    pallas_call x1, Pallas kernels: 13.5 us -> 8.03 us  [shards(): pl.pallas_call(beam_kernel, out_shape=jax.ShapeDtypeStruct((beam_count, b...]
    another operation x5 -> x6, local copies, waits for them, and re-layouts: 0.13 us -> 5.07 us  [the longest x4 4.98 us: cut(): voltages[0, first:last, :, :, :, low:high]]
    ppermute x4, waiting for transfers between devices: 1.12 us -> 2.89 us  [the longest x2 2.88 us: shards(): lax.ppermute(cut(i * share, (i + 1) * share, 0, ahead), 'narrow', [(i, i...]
    all_to_all x1, starting transfers between devices: 23.9 us -> 22.2 us  [shards(): packed = lax.all_to_all(packed, ('wide', 'narrow'), 0, 0, tiled=True)]
    slice x3 -> x2, local copies, waits for them, and re-layouts: 2.74 us -> 4.11 us  [cut(): voltages[0, first:last, :, :, :, low:high]]
  transfers between devices with their start and end apart: 8 -> 8, of which waited for: 4 -> 6; matrix products, arithmetic and copies ran while one was open for 15% -> 18% of each run, Pallas kernels for 4% -> 4%
where the time goes in v6:
time: 161 us; the launch traced here: 160 us
  waiting for transfers between devices  58 us (36%)
  starting transfers between devices  44.7 us (28%)
  Pallas kernels  21.7 us (13%)
  other arithmetic  21.6 us (13%)
  local copies, waits for them, and re-layouts  13.5 us (8%)
    all_to_all x1, waiting for transfers between devices, shards(): packed = lax.all_to_all(packed, ('wide', 'narrow'), 0, 0, tiled=True)  36.8 us
    all_to_all x1, starting transfers between devices, shards(): packed = lax.all_to_all(packed, ('wide', 'narrow'), 0, 0, tiled=True)  22.2 us
    pallas_call x2, Pallas kernels, shards(): pl.pallas_call(filter_kernel, grid=(steps,), out_shape=jax.ShapeDtypeStru...  13.6 us
    another operation x4, other arithmetic  11 us
    all_to_all x1, waiting for transfers between devices, shards(): arrived = lax.all_to_all(outgoing, 'wide', 0, 0, tiled=True)  10.4 us
    ppermute x2, starting transfers between devices, shards(): lax.ppermute(cut(i * share, (i + 1) * share, piece_len - LEAD * chan_coun...  8.15 us
    pallas_call x1, Pallas kernels, shards(): pl.pallas_call(beam_kernel, out_shape=jax.ShapeDtypeStruct((beam_count, b...  8.03 us
    all_to_all x1, waiting for transfers between devices, shards(): partial = lax.all_to_all(partial, 'narrow', 0, 0, tiled=True)  7.62 us
  transfers between devices with their start and end apart: 8, of which 6 were waited for; matrix products, arithmetic and copies ran while one was open for 18% of the time, Pallas kernels for 4%

profile of v6, /device:TPU:6, one launch (start us, length us, event | category | flops | bytes accessed | tf_op | source)
XLA Modules:
  0.0 160.1 jit_solution(39451738424133982)
XLA Ops:
  0.0 0.0 copy-start.1
  0.0 2.4 %fusion.43 = (bf16[1,16,2,2,2,2048]{5,4,3,2,1,0:T(2,128)(2,1)S(1)}, bf16[1,16,2,2,2,2048]{5,4,3,2,1,0:T(2,128)(2,1)S(1)}) fusion(bf16[1,32,2,2,2,4096]{5,4,3,2,1,0:T(2,128)(2,1)} %param.6), kind=kLoop, calls=%fused_computation.115 | loop fusion | bytes 2097152 | tf_op jit(solution)/shard_map/slice | solution.py:293
  2.5 1.0 reshape_squeeze.14
  3.5 0.0 copy-start.5
  3.5 0.0 copy-start.4
  3.5 3.6 %collective-permute-start.2 = (bf16[16,8,2048]{2,1,0:T(8,128)(2,1)}, bf16[16,8,2048]{2,1,0:T(8,128)(2,1)}, u32[]{:S(2)}, u32[]{:S(2)}) collective-permute-start(bf16[16,8,2048]{2,1,0:T(8,128)(2,1)} %reshape_squeeze.14), channel_id=1, source_target_pairs={{0,1},{1,2},{2,3},{3,4},{4,5},{5,6},{6,7},{7,0},{8,9},{9,10},{10,1... | collective-permute-start | bytes 1572872 | tf_op jit(solution)/shard_map/ppermute | solution.py:299
  7.1 0.0 copy-done.1
  7.1 1.7 %fusion.42 = (bf16[1,16,2,2,2,1920]{5,4,3,2,1,0:T(2,128)(2,1)}, bf16[1,16,2,2,2,1920]{5,4,3,2,1,0:T(2,128)(2,1)S(1)}) fusion(bf16[1,32,2,2,2,4096]{5,4,3,2,1,0:T(2,128)(2,1)S(1)} %copy-done.1), kind=kLoop, calls=%fused_computation.114 | loop fusion | bytes 1966080 | tf_op jit(solution)/shard_map/slice | solution.py:293
  8.7 2.0 %reshape_squeeze.15 = bf16[16,8,1920]{2,1,0:T(8,128)(2,1)} reshape(bf16[1,16,2,2,2,1920]{5,4,3,2,1,0:T(2,128)(2,1)} %get-tuple-element.9) | data formatting | bytes 983040 | tf_op jit(solution)/shard_map/reshape;squeeze | solution.py:293
  10.8 1.3 collective-permute-start.3
  12.0 1.0 reshape_squeeze.12
  13.0 4.5 %collective-permute-start = (bf16[16,8,2048]{2,1,0:T(8,128)(2,1)}, bf16[16,8,2048]{2,1,0:T(8,128)(2,1)}, u32[]{:S(2)}, u32[]{:S(2)}) collective-permute-start(bf16[16,8,2048]{2,1,0:T(8,128)(2,1)} %reshape_squeeze.12), channel_id=1, source_target_pairs={{0,1},{1,2},{2,3},{3,4},{4,5},{5,6},{6,7},{7,0},{8,9},{9,10},{10,1... | collective-permute-start | bytes 1572872 | tf_op jit(solution)/shard_map/ppermute | solution.py:299
  17.6 1.0 reshape_squeeze.13
  18.6 1.3 collective-permute-start.1
  19.9 0.0 copy-done.5
  19.9 0.1 iota_subtract_fusion
  19.9 0.0 copy-done.4
  19.9 0.6 pad_maximum_fusion.1.prototype_ref
  20.6 2.2 %reshape.326.own_ref = bf16[32,8,4096]{2,1,0:T(8,128)(2,1)} reshape(bf16[1,32,2,2,2,4096]{5,4,3,2,1,0:T(2,128)(2,1)S(1)} %copy-done.1) | data formatting | bytes 4194304 | tf_op jit(solution)/shard_map/reshape | solution.py:290
  22.8 2.5 %fusion.16 = (bf16[2,256,256]{2,1,0:T(8,128)(2,1)S(1)}, bf16[2,256,256]{2,1,0:T(8,128)(2,1)S(1)}, bf16[2,256,256]{2,1,0:T(8,128)(2,1)S(1)}) fusion(s32[2,256]{1,0:T(2,128)S(1)} %iota_subtract_fusion, s32[256]{0:T(256)S(1)} %fusion.32), kind=kLoop, calls=%fused_computation.36 | loop fusion | flops 2621440 | bytes 789504 | tf_op jit(solution)/shard_map/convert.12
  25.3 1.1 maximum_maximum_fusion.table_ref
  26.4 0.7 collective-permute-done.3.right_ref
  27.1 0.0 collective-permute-done.2.left_ref
  27.1 6.8 %filter.2.refs_0_ = bf16[32,256,128]{2,1,0:T(8,128)(2,1)} custom-call(s32[1]{0:T(128)} %bitcast.1.where_ref, s32[2]{0:T(128)} %shifts_ref.3, bf16[32,8,4096]{2,1,0:T(8,128)(2,1)} %reshape.326.own_ref, bf16[16,8,2048]{2,1,0:T(8,128)(2,1)} %collective-permute-done.2.left_ref, bf16[16,8,1920]{2,1,0:T(8,128)(2,1)} %collective-permute-done.3.right_ref, ...), custom_call_target="tpu_custom_call" | custom-call | tf_op jit(solution)/shard_map/filter/pallas_call | solution.py:339
  33.9 2.1 %collective-permute-done.1.right_ref = bf16[16,8,1920]{2,1,0:T(8,128)(2,1)S(1)} collective-permute-done((bf16[16,8,1920]{2,1,0:T(8,128)(2,1)}, bf16[16,8,1920]{2,1,0:T(8,128)(2,1)S(1)}, u32[]{:S(2)}, u32[]{:S(2)}) %collective-permute-start.1) | collective-permute-done | bytes 491552 | tf_op jit(solution)/shard_map/ppermute | solution.py:304
  36.1 0.0 collective-permute-done.left_ref
  36.1 0.8 copy-done.2
  36.9 6.8 %filter.3 = bf16[32,256,128]{2,1,0:T(8,128)(2,1)} custom-call(s32[1]{0:T(128)} %bitcast.1.where_ref, s32[2]{0:T(128)} %shifts_ref.3, bf16[32,8,4096]{2,1,0:T(8,128)(2,1)} %reshape.326.own_ref, bf16[16,8,2048]{2,1,0:T(8,128)(2,1)} %collective-permute-done.left_ref, bf16[16,8,1920]{2,1,0:T(8,128)(2,1)} %copy-done.2, ...), custom_call_target="tpu_custom_call", output_to_operand_aliasing={{}: (7, {})} | custom-call | tf_op jit(solution)/shard_map/filter/pallas_call | solution.py:339
  43.7 0.0 copy-start.3
  43.7 0.0 copy-start.7
  43.7 22.2 %all-to-all-start = ((bf16[256,32,128]{2,1,0:T(8,128)(2,1)}), bf16[256,32,128]{2,1,0:T(8,128)(2,1)S(1)}, u32[]{:S(2)}, u32[]{:S(2)}) async-start(bf16[256,32,128]{2,1,0:T(8,128)(2,1)} %bitcast.49), calls=%async_computation | async-start | bytes 4194304 | tf_op jit(solution)/shard_map/all_to_all | solution.py:377
  65.9 0.0 copy-done.3
  65.9 0.1 copy.22
  66.0 0.0 copy-done.6
  66.0 0.1 copy.18
  66.1 0.1 reduce-window.8
  66.2 0.0 copy-done.7
  66.2 0.6 fusion.35
  66.9 0.6 compare_select_fusion.1
  67.5 0.6 fusion.34
  68.2 0.1 add_reduce_fusion
  68.3 8.4 %fusion.3 = (bf16[32,128,128]{2,1,0:T(8,128)(2,1)S(1)}, bf16[32,128,128]{2,1,0:T(8,128)(2,1)S(1)}) fusion(f32[128,128]{1,0:T(8,128)S(1)} %copy.22, f32[32]{0:T(128)S(1)} %add_multiply_fusion.1, pred[128]{0:T(512)(128)(4,1)S(1)} %fusion.37), kind=kLoop, calls=%fused_computation.6 | loop fusion | flops 4194304 | bytes 2162944 | tf_op jit(solution)/shard_map/convert.5
  76.7 1.6 pad_maximum_fusion.weights_ref
  78.3 0.1 iota_multiply_fusion
  78.4 0.1 add_multiply_fusion
  78.4 2.5 %cosine_reduce_fusion = (f32[32,32]{1,0:T(8,128)S(1)}, f32[32,32]{1,0:T(8,128)S(1)}) fusion(s32[32,32]{1,0:T(8,128)S(1)} %iota_multiply_fusion, s32[32,32]{1,0:T(8,128)S(1)} %add_multiply_fusion), kind=kLoop, calls=%fused_computation.30 | loop fusion | flops 522240 | bytes 16384 | tf_op jit(solution)/shard_map/reduce_sum | solution.py:407
  81.0 0.3 fusion.14
  81.3 36.8 %all-to-all-done = bf16[256,32,128]{2,1,0:T(8,128)(2,1)S(1)} async-done(((bf16[256,32,128]{2,1,0:T(8,128)(2,1)}), bf16[256,32,128]{2,1,0:T(8,128)(2,1)S(1)}, u32[]{:S(2)}, u32[]{:S(2)}) %all-to-all-start) | async-done | bytes 2097184 | tf_op jit(solution)/shard_map/all_to_all | solution.py:377
  118.1 1.4 collective-permute-start.4
  119.5 0.6 copy.23.kern_ref
  120.1 0.1 fusion.19.order_ref
  120.2 0.4 collective-permute-done.4.tail_ref
  120.6 0.0 copy-done
  120.6 8.0 %beams.1 = f32[128,128]{1,0:T(8,128)} custom-call(bf16[32,8,32,128]{3,2,1,0:T(8,128)(2,1)S(1)} %bitcast.48, bf16[32,32,128]{2,1,0:T(8,128)(2,1)S(1)} %collective-permute-done.4.tail_ref, bf16[32,256,128]{2,1,0:T(8,128)(2,1)S(1)} %copy-done, f32[32,2,32,128]{3,2,1,0:T(8,128)S(1)} %copy.23.kern_ref, f32[128,128]{1,0:T(8,128)S(1)} %fusion.19.order_ref), custom_call_target="tpu_custom_call" | custom-call | tf_op jit(solution)/shard_map/beams/pallas_call | solution.py:416
  128.7 3.3 %all-to-all-start.1 = ((f32[8,16,128]{2,1,0:T(8,128)}), f32[8,16,128]{2,1,0:T(8,128)S(1)}, u32[]{:S(2)}, u32[]{:S(2)}) async-start(f32[8,16,128]{2,1,0:T(8,128)} %bitcast.16), calls=%async_computation.1 | async-start | bytes 131072 | tf_op jit(solution)/shard_map/all_to_all | solution.py:431
  132.0 0.7 iota_compare_fusion.2
  132.7 0.1 select_reduce_fusion
  132.8 7.6 %all-to-all-done.1 = f32[8,16,128]{2,1,0:T(8,128)S(1)} async-done(((f32[8,16,128]{2,1,0:T(8,128)}), f32[8,16,128]{2,1,0:T(8,128)S(1)}, u32[]{:S(2)}, u32[]{:S(2)}) %all-to-all-start.1) | async-done | bytes 65568 | tf_op jit(solution)/shard_map/all_to_all | solution.py:431
  140.5 0.8 broadcast_select_fusion
  141.2 7.0 %all-to-all-start.2 = ((f32[32,16,128]{2,1,0:T(8,128)}), f32[32,16,128]{2,1,0:T(8,128)S(1)}, u32[]{:S(2)}, u32[]{:S(2)}) async-start(f32[32,16,128]{2,1,0:T(8,128)} %broadcast_select_fusion), calls=%async_computation.2 | async-start | bytes 524288 | tf_op jit(solution)/shard_map/all_to_all | solution.py:437
  148.3 0.1 fusion.33
  148.5 10.4 %all-to-all-done.2 = f32[32,16,128]{2,1,0:T(8,128)S(1)} async-done(((f32[32,16,128]{2,1,0:T(8,128)}), f32[32,16,128]{2,1,0:T(8,128)S(1)}, u32[]{:S(2)}, u32[]{:S(2)}) %all-to-all-start.2) | async-done | bytes 262176 | tf_op jit(solution)/shard_map/all_to_all | solution.py:437
  158.8 0.5 gather_fusion
  159.4 0.7 fusion.23
  (23 shorter events, 0.2 us)
Async XLA Ops:
  0.0 7.1 %copy-start.1 = (bf16[1,32,2,2,2,4096]{5,4,3,2,1,0:T(2,128)(2,1)S(1)}, bf16[1,32,2,2,2,4096]{5,4,3,2,1,0:T(2,128)(2,1)}, u32[]{:S(2)}) copy-start(bf16[1,32,2,2,2,4096]{5,4,3,2,1,0:T(2,128)(2,1)} %param.6) | copy-start | bytes 6291460
  3.5 16.4 %copy-start.5 = (s32[2]{0:T(128)S(1)}, s32[2]{0:T(128)}, u32[]{:S(2)}) copy-start(s32[2]{0:T(128)} %shifts_ref.3) | copy-start | bytes 28
  3.5 16.5 %copy-start.4 = (f32[16,256]{1,0:T(8,128)S(1)}, f32[16,256]{1,0:T(8,128)}, u32[]{:S(2)}) copy-start(f32[16,256]{1,0:T(8,128)} %param.7) | copy-start | bytes 49156
  3.5 23.6 %collective-permute-start.2 = (bf16[16,8,2048]{2,1,0:T(8,128)(2,1)}, bf16[16,8,2048]{2,1,0:T(8,128)(2,1)}, u32[]{:S(2)}, u32[]{:S(2)}) collective-permute-start(bf16[16,8,2048]{2,1,0:T(8,128)(2,1)} %reshape_squeeze.14), channel_id=1, source_target_pairs={{0,1},{1,2},{2,3},{3,4},{4,5},{5,6},{6,7},{7,0},{8,9},{9,10},{10,1... | collective-permute-start | bytes 1572872 | tf_op jit(solution)/shard_map/ppermute | solution.py:299
  10.8 16.3 %collective-permute-start.3 = (bf16[16,8,1920]{2,1,0:T(8,128)(2,1)}, bf16[16,8,1920]{2,1,0:T(8,128)(2,1)}, u32[]{:S(2)}, u32[]{:S(2)}) collective-permute-start(bf16[16,8,1920]{2,1,0:T(8,128)(2,1)} %reshape_squeeze.15), channel_id=1, source_target_pairs={{1,0},{2,1},{3,2},{4,3},{5,4},{6,5},{7,6},{9,8},{10,9},{11,10},{12... | collective-permute-start | bytes 1474568 | tf_op jit(solution)/shard_map/ppermute | solution.py:304
  13.0 23.0 %collective-permute-start = (bf16[16,8,2048]{2,1,0:T(8,128)(2,1)}, bf16[16,8,2048]{2,1,0:T(8,128)(2,1)}, u32[]{:S(2)}, u32[]{:S(2)}) collective-permute-start(bf16[16,8,2048]{2,1,0:T(8,128)(2,1)} %reshape_squeeze.12), channel_id=1, source_target_pairs={{0,1},{1,2},{2,3},{3,4},{4,5},{5,6},{6,7},{7,0},{8,9},{9,10},{10,1... | collective-permute-start | bytes 1572872 | tf_op jit(solution)/shard_map/ppermute | solution.py:299
  18.6 17.5 %collective-permute-start.1 = (bf16[16,8,1920]{2,1,0:T(8,128)(2,1)}, bf16[16,8,1920]{2,1,0:T(8,128)(2,1)S(1)}, u32[]{:S(2)}, u32[]{:S(2)}) collective-permute-start(bf16[16,8,1920]{2,1,0:T(8,128)(2,1)} %reshape_squeeze.13), channel_id=1, source_target_pairs={{1,0},{2,1},{3,2},{4,3},{5,4},{6,5},{7,6},{9,8},{10,9},{11,10},{12... | collective-permute-start | bytes 1474568 | tf_op jit(solution)/shard_map/ppermute | solution.py:304
  36.1 0.8 copy-start.2
  43.7 22.2 %copy-start.3 = (f32[128,64]{0,1:T(8,128)S(1)}, f32[128,64]{0,1:T(8,128)}, u32[]{:S(2)}) copy-start(f32[128,64]{0,1:T(8,128)} %param.8) | copy-start | bytes 98308
  43.7 22.3 %copy-start.6 = (s32[32]{0:T(128)S(1)}, s32[32]{0:T(128)}, u32[]{:S(2)}) copy-start(s32[32]{0:T(128)} %param.11) | copy-start | bytes 388
  43.7 22.5 %copy-start.7 = (s32[32]{0:T(128)S(1)}, s32[32]{0:T(128)}, u32[]{:S(2)}) copy-start(s32[32]{0:T(128)} %param.10) | copy-start | bytes 388
  43.7 74.3 %all-to-all-start = ((bf16[256,32,128]{2,1,0:T(8,128)(2,1)}), bf16[256,32,128]{2,1,0:T(8,128)(2,1)S(1)}, u32[]{:S(2)}, u32[]{:S(2)}) async-start(bf16[256,32,128]{2,1,0:T(8,128)(2,1)} %bitcast.49), calls=%async_computation | async-start | bytes 4194304 | tf_op jit(solution)/shard_map/all_to_all | solution.py:377
  118.0 2.6 %copy-start = (bf16[32,256,128]{2,1,0:T(8,128)(2,1)S(1)}, bf16[32,256,128]{2,1,0:T(8,128)(2,1)}, u32[]{:S(2)}) copy-start(bf16[32,256,128]{2,1,0:T(8,128)(2,1)} %pad_maximum_fusion.weights_ref) | copy-start | bytes 6291460
  118.1 2.6 %collective-permute-start.4 = (bf16[32,32,128]{2,1,0:T(8,128)(2,1)S(1)}, bf16[32,32,128]{2,1,0:T(8,128)(2,1)S(1)}, u32[]{:S(2)}, u32[]{:S(2)}) collective-permute-start(bf16[32,32,128]{2,1,0:T(8,128)(2,1)S(1)} %fusion.17), channel_id=1, source_target_pairs={{0,256},{1,257},{2,258},{3,259},{4,260},{5,261},{6,262},{7,263},{8... | collective-permute-start | bytes 786440 | tf_op jit(solution)/shard_map/ppermute | solution.py:382
  128.7 11.8 %all-to-all-start.1 = ((f32[8,16,128]{2,1,0:T(8,128)}), f32[8,16,128]{2,1,0:T(8,128)S(1)}, u32[]{:S(2)}, u32[]{:S(2)}) async-start(f32[8,16,128]{2,1,0:T(8,128)} %bitcast.16), calls=%async_computation.1 | async-start | bytes 131072 | tf_op jit(solution)/shard_map/all_to_all | solution.py:431
  141.2 17.6 %all-to-all-start.2 = ((f32[32,16,128]{2,1,0:T(8,128)}), f32[32,16,128]{2,1,0:T(8,128)S(1)}, u32[]{:S(2)}, u32[]{:S(2)}) async-start(f32[32,16,128]{2,1,0:T(8,128)} %broadcast_select_fusion), calls=%async_computation.2 | async-start | bytes 524288 | tf_op jit(solution)/shard_map/all_to_all | solution.py:437

commit v7 on v6

--- a/solution.py
+++ b/solution.py
@@ -133,13 +133,15 @@
                         fours // 8, 8, LANES
                     )
     for member in range(members):
-        out_ref[member] = packed[member].reshape(fours * quad, LANES).astype(jnp.bfloat16)
+        out_ref[:, member] = (
+            packed[member].reshape(out_ref.shape[0], -1, LANES).astype(jnp.bfloat16)
+        )
 
 
 def beam_kernel(
     spectra_ref, tail_ref, weights_ref, kern_ref, order_ref, power_ref, held, held_tail, total
 ):
-    source_count, piece_count, row_count, _ = spectra_ref.shape
+    piece_count, source_count, row_count, _ = spectra_ref.shape
     beam_count, block_len = power_ref.shape
     chan_local = weights_ref.shape[0]
     pol_count = 2
@@ -179,7 +181,7 @@
     for piece in range(piece_count):
         for source in range(source_count):
             held[piece, source * PITCH : source * PITCH + row_count] = spectra_ref[
-                source, piece
+                piece, source
             ].astype(jnp.float32)
     for source in range(source_count):
         held_tail[source * PITCH : source * PITCH + row_count] = tail_ref[source].astype(
@@ -288,21 +290,17 @@
     params = pltpu.CompilerParams(vmem_limit_bytes=VMEM_BYTES)
 
     volts = voltages.reshape(sub_count, rows, piece_len)
-
-    def cut(first, last, low, high):
-        return voltages[0, first:last, :, :, :, low:high].reshape(last - first, rows, high - low)
-
     ahead = (tap_count - 1 - LEAD) * chan_count + MAXD
     share = sub_count // SHARES
     ends = [
         (
             lax.ppermute(
-                cut(i * share, (i + 1) * share, piece_len - LEAD * chan_count, piece_len),
+                volts[i * share : (i + 1) * share, :, piece_len - LEAD * chan_count :],
                 "narrow",
                 [(i, (i + 1) % narrow_count) for i in range(narrow_count)],
             ),
             lax.ppermute(
-                cut(i * share, (i + 1) * share, 0, ahead),
+                volts[i * share : (i + 1) * share, :, :ahead],
                 "narrow",
                 [(i, i - 1) for i in range(1, narrow_count)],
             ),
@@ -329,6 +327,7 @@
         ],
         axis=1,
     ).astype(jnp.bfloat16)
+    local_rows = fours * quad // narrow_count
     packed = None
     for i, (left, right) in enumerate(ends):
         steps = share // members
@@ -339,7 +338,9 @@
         packed = pl.pallas_call(
             filter_kernel,
             grid=(steps,),
-            out_shape=jax.ShapeDtypeStruct((sub_count, fours * quad, LANES), jnp.bfloat16),
+            out_shape=jax.ShapeDtypeStruct(
+                (narrow_count, sub_count, local_rows, LANES), jnp.bfloat16
+            ),
             in_specs=[
                 scalars,
                 scalars,
@@ -351,7 +352,8 @@
             ]
             + [pl.BlockSpec(memory_space=pl.ANY)] * min(i, 1),
             out_specs=pl.BlockSpec(
-                (members, fours * quad, LANES), lambda step, first=i * steps: (step + first, 0, 0)
+                (narrow_count, members, local_rows, LANES),
+                lambda step, first=i * steps: (0, step + first, 0, 0),
             ),
             scratch_shapes=[
                 pltpu.VMEM((tap_count + 1, rows, chan_count), jnp.float32),
@@ -372,13 +374,12 @@
             *([packed] if i else []),
         )
 
-    local_rows = fours * quad // narrow_count
     packed = packed.reshape(sub_count * narrow_count, local_rows, LANES)
-    packed = lax.all_to_all(packed, ("wide", "narrow"), 0, 0, tiled=True)
-    packed = packed.reshape(wide_count, narrow_count, local_rows, LANES)
+    packed = lax.all_to_all(packed, ("narrow", "wide"), 0, 0, tiled=True)
+    packed = packed.reshape(narrow_count, wide_count, local_rows, LANES)
 
     early = jnp.arange(LANES) % spectra < LEAD
-    tail = jnp.where(early, packed[:, 0], packed[:, narrow_count - 1])
+    tail = jnp.where(early, packed[0], packed[narrow_count - 1])
     tail = lax.ppermute(tail, "sec", [(0, 1)])
 
     sub = wide_index
@@ -439,9 +440,8 @@
     rank = jnp.cumsum(owned.astype(jnp.int32)) - 1
     slots = jnp.arange(SUBBAND_LIMIT, dtype=jnp.int32)
     held = owned[None, :] & (rank[None, :] == slots[:, None])
-    chosen = jnp.sum(jnp.where(held, subs[None, :], 0), axis=1)
-    result = jnp.take(arrived, chosen, axis=0)
-    return jnp.where(jnp.any(held, axis=1)[:, None, None], result, 0.0)[None]
+    chosen = held[:, :, None, None]
+    return jnp.sum(jnp.where(chosen, arrived[None], 0.0), axis=1)[None]
 
 
 def solution(mesh):

time: 161 us -> 158 us (0.981)
  local copies, waits for them, and re-layouts: 13.5 us -> 6.49 us
  waiting for transfers between devices: 58 us -> 60.9 us
    another operation x5 -> x1, local copies, waits for them, and re-layouts: 5.07 us -> 0.09 us  [the longest x4 4.98 us: cut(): voltages[0, first:last, :, :, :, low:high]]
    ppermute x4, waiting for transfers between devices: 2.89 us -> 7.19 us  [the longest x2 7.18 us: shards(): lax.ppermute(volts[i * share:(i + 1) * share, :, :ahead], 'narrow', [(i,...]
    slice x2, local copies, waits for them, and re-layouts: 4.11 us -> 2.09 us  [the longest x1 1.06 us: shards(): volts[i * share:(i + 1) * share, :, piece_len - LEAD * chan_count:]]
  transfers between devices with their start and end apart: 8 -> 8, of which waited for: 6 -> 6; matrix products, arithmetic and copies ran while one was open for 18% -> 14% of each run, Pallas kernels for 4% -> 4%
where the time goes in v7:
time: 158 us; the launch traced here: 156 us
  waiting for transfers between devices  60.9 us (39%)
  starting transfers between devices  45.2 us (29%)
  Pallas kernels  21.6 us (14%)
  other arithmetic  21.4 us (14%)
  local copies, waits for them, and re-layouts  6.49 us (4%)
    all_to_all x1, waiting for transfers between devices, shards(): packed = lax.all_to_all(packed, ('narrow', 'wide'), 0, 0, tiled=True)  36.4 us
    all_to_all x1, starting transfers between devices, shards(): packed = lax.all_to_all(packed, ('narrow', 'wide'), 0, 0, tiled=True)  21.7 us
    pallas_call x2, Pallas kernels, shards(): pl.pallas_call(filter_kernel, grid=(steps,), out_shape=jax.ShapeDtypeStru...  13.6 us
    another operation x4, other arithmetic  11 us
    all_to_all x1, waiting for transfers between devices, shards(): arrived = lax.all_to_all(outgoing, 'wide', 0, 0, tiled=True)  10 us
    pallas_call x1, Pallas kernels, shards(): pl.pallas_call(beam_kernel, out_shape=jax.ShapeDtypeStruct((beam_count, b...  8.03 us
    ppermute x2, starting transfers between devices, shards(): lax.ppermute(volts[i * share:(i + 1) * share, :, piece_len - LEAD * chan_...  8.02 us
    ppermute x2, waiting for transfers between devices, shards(): lax.ppermute(volts[i * share:(i + 1) * share, :, :ahead], 'narrow', [(i,...  7.18 us
  transfers between devices with their start and end apart: 8, of which 6 were waited for; matrix products, arithmetic and copies ran while one was open for 14% of the time, Pallas kernels for 4%

profile of v7, /device:TPU:6, one launch (start us, length us, event | category | flops | bytes accessed | tf_op | source)
XLA Modules:
  0.0 156.2 jit_solution(8121414154663532051)
XLA Ops:
  0.0 2.7 %reshape.332.own_ref = bf16[32,8,4096]{2,1,0:T(8,128)(2,1)S(1)} reshape(bf16[1,32,2,2,2,4096]{5,4,3,2,1,0:T(2,128)(2,1)} %param.6) | data formatting | bytes 4194304 | tf_op jit(solution)/shard_map/reshape | solution.py:292
  2.8 0.0 copy-start.1
  2.8 0.0 copy-start.5
  2.8 0.0 copy-start.4
  2.8 1.1 fusion.39
  3.8 3.5 %collective-permute-start.2 = (bf16[16,8,2048]{2,1,0:T(8,128)(2,1)}, bf16[16,8,2048]{2,1,0:T(8,128)(2,1)}, u32[]{:S(2)}, u32[]{:S(2)}) collective-permute-start(bf16[16,8,2048]{2,1,0:T(8,128)(2,1)} %get-tuple-element.11), channel_id=1, source_target_pairs={{0,1},{1,2},{2,3},{3,4},{4,5},{5,6},{6,7},{7,0},{8,9},{9,10},{10,1... | collective-permute-start | bytes 1572872 | tf_op jit(solution)/shard_map/ppermute | solution.py:297
  7.3 1.0 fusion.38
  8.4 1.3 collective-permute-start.3
  9.6 4.6 %collective-permute-start = (bf16[16,8,2048]{2,1,0:T(8,128)(2,1)}, bf16[16,8,2048]{2,1,0:T(8,128)(2,1)S(1)}, u32[]{:S(2)}, u32[]{:S(2)}) collective-permute-start(bf16[16,8,2048]{2,1,0:T(8,128)(2,1)} %get-tuple-element.12), channel_id=1, source_target_pairs={{0,1},{1,2},{2,3},{3,4},{4,5},{5,6},{6,7},{7,0},{8,9},{9,10},{10,1... | collective-permute-start | bytes 1572872 | tf_op jit(solution)/shard_map/ppermute | solution.py:297
  14.2 1.3 collective-permute-start.1
  15.5 0.0 copy-done.5
  15.5 0.1 iota_subtract_fusion
  15.6 0.0 copy-done.4
  15.6 0.6 pad_maximum_fusion.1.prototype_ref
  16.2 0.0 copy-done.1
  16.2 2.5 %fusion.16 = (bf16[2,256,256]{2,1,0:T(8,128)(2,1)S(1)}, bf16[2,256,256]{2,1,0:T(8,128)(2,1)S(1)}, bf16[2,256,256]{2,1,0:T(8,128)(2,1)S(1)}) fusion(s32[2,256]{1,0:T(2,128)S(1)} %iota_subtract_fusion, s32[256]{0:T(256)S(1)} %fusion.30), kind=kLoop, calls=%fused_computation.36 | loop fusion | flops 2621440 | bytes 789504 | tf_op jit(solution)/shard_map/convert.12
  18.7 1.1 maximum_maximum_fusion.table_ref
  19.8 4.9 %collective-permute-done.3.right_ref = bf16[16,8,1920]{2,1,0:T(8,128)(2,1)} collective-permute-done((bf16[16,8,1920]{2,1,0:T(8,128)(2,1)}, bf16[16,8,1920]{2,1,0:T(8,128)(2,1)}, u32[]{:S(2)}, u32[]{:S(2)}) %collective-permute-start.3) | collective-permute-done | bytes 491552 | tf_op jit(solution)/shard_map/ppermute | solution.py:302
  24.7 0.0 collective-permute-done.2.left_ref
  24.7 6.8 %filter.2.refs_0_ = bf16[8,32,32,128]{3,2,1,0:T(8,128)(2,1)} custom-call(s32[1]{0:T(128)} %bitcast.1.where_ref, s32[2]{0:T(128)} %shifts_ref.3, bf16[32,8,4096]{2,1,0:T(8,128)(2,1)} %copy-done.1, bf16[16,8,2048]{2,1,0:T(8,128)(2,1)} %collective-permute-done.2.left_ref, bf16[16,8,1920]{2,1,0:T(8,128)(2,1)} %collective-permute-done.3.right_ref, ...), custom_call_target="tpu_custom_call" | custom-call | tf_op jit(solution)/shard_map/filter/pallas_call | solution.py:338
  31.5 2.3 %collective-permute-done.1.right_ref = bf16[16,8,1920]{2,1,0:T(8,128)(2,1)} collective-permute-done((bf16[16,8,1920]{2,1,0:T(8,128)(2,1)}, bf16[16,8,1920]{2,1,0:T(8,128)(2,1)}, u32[]{:S(2)}, u32[]{:S(2)}) %collective-permute-start.1) | collective-permute-done | bytes 491552 | tf_op jit(solution)/shard_map/ppermute | solution.py:302
  33.8 0.0 collective-permute-done.left_ref
  33.8 0.0 copy-start.2
  33.8 0.8 copy-done.2
  34.6 6.8 %filter.3 = bf16[8,32,32,128]{3,2,1,0:T(8,128)(2,1)} custom-call(s32[1]{0:T(128)} %bitcast.1.where_ref, s32[2]{0:T(128)} %shifts_ref.3, bf16[32,8,4096]{2,1,0:T(8,128)(2,1)} %copy-done.1, bf16[16,8,2048]{2,1,0:T(8,128)(2,1)} %copy-done.2, bf16[16,8,1920]{2,1,0:T(8,128)(2,1)} %collective-permute-done.1.right_ref, ...), custom_call_target="tpu_custom_call", output_to_operand_aliasing={{}: (7, {})} | custom-call | tf_op jit(solution)/shard_map/filter/pallas_call | solution.py:338
  41.4 0.0 copy-start.3
  41.4 0.0 copy-start.7
  41.4 21.7 %all-to-all-start = ((bf16[256,32,128]{2,1,0:T(8,128)(2,1)}), bf16[256,32,128]{2,1,0:T(8,128)(2,1)S(1)}, u32[]{:S(2)}, u32[]{:S(2)}) async-start(bf16[256,32,128]{2,1,0:T(8,128)(2,1)} %bitcast.29), calls=%async_computation | async-start | bytes 4194304 | tf_op jit(solution)/shard_map/all_to_all | solution.py:378
  63.1 0.0 copy-done.3
  63.2 0.1 copy.17
  63.3 0.0 copy-done.7
  63.3 0.6 fusion.32
  64.0 0.6 compare_select_fusion
  64.6 8.4 %fusion.3 = (bf16[32,128,128]{2,1,0:T(8,128)(2,1)S(1)}, bf16[32,128,128]{2,1,0:T(8,128)(2,1)S(1)}) fusion(f32[128,128]{1,0:T(8,128)S(1)} %copy.17, f32[32]{0:T(128)S(1)} %add_multiply_fusion.1, pred[128]{0:T(512)(128)(4,1)S(1)} %fusion.34), kind=kLoop, calls=%fused_computation.5 | loop fusion | flops 4194304 | bytes 2162944 | tf_op jit(solution)/shard_map/convert.5
  73.1 1.6 pad_maximum_fusion.weights_ref
  74.6 0.1 iota_multiply_fusion
  74.7 0.1 add_multiply_fusion
  74.8 2.5 %cosine_reduce_fusion = (f32[32,32]{1,0:T(8,128)S(1)}, f32[32,32]{1,0:T(8,128)S(1)}) fusion(s32[32,32]{1,0:T(8,128)S(1)} %iota_multiply_fusion, s32[32,32]{1,0:T(8,128)S(1)} %add_multiply_fusion), kind=kLoop, calls=%fused_computation.30 | loop fusion | flops 522240 | bytes 16384 | tf_op jit(solution)/shard_map/reduce_sum | solution.py:408
  77.3 0.3 fusion.14
  77.6 36.4 %all-to-all-done = bf16[256,32,128]{2,1,0:T(8,128)(2,1)S(1)} async-done(((bf16[256,32,128]{2,1,0:T(8,128)(2,1)}), bf16[256,32,128]{2,1,0:T(8,128)(2,1)S(1)}, u32[]{:S(2)}, u32[]{:S(2)}) %all-to-all-start) | async-done | bytes 2097184 | tf_op jit(solution)/shard_map/all_to_all | solution.py:378
  114.0 0.0 copy-start
  114.1 1.6 %collective-permute-start.4 = (bf16[32,32,128]{2,1,0:T(8,128)(2,1)S(1)}, bf16[32,32,128]{2,1,0:T(8,128)(2,1)S(1)}, u32[]{:S(2)}, u32[]{:S(2)}) collective-permute-start(bf16[32,32,128]{2,1,0:T(8,128)(2,1)S(1)} %slice_select_fusion), channel_id=1, source_target_pairs={{0,256},{1,257},{2,258},{3,259},{4,260},{5,261},{6,262},{7,263},{8... | collective-permute-start | bytes 786440 | tf_op jit(solution)/shard_map/ppermute | solution.py:383
  115.7 0.6 copy.18.kern_ref
  116.3 0.1 fusion.18.order_ref
  116.4 0.2 collective-permute-done.4.tail_ref
  116.6 0.0 copy-done
  116.6 0.0 copy-start.6
  116.6 8.0 %beams.1 = f32[128,128]{1,0:T(8,128)} custom-call(bf16[8,32,32,128]{3,2,1,0:T(8,128)(2,1)S(1)} %bitcast.28, bf16[32,32,128]{2,1,0:T(8,128)(2,1)S(1)} %collective-permute-done.4.tail_ref, bf16[32,256,128]{2,1,0:T(8,128)(2,1)S(1)} %copy-done, f32[32,2,32,128]{3,2,1,0:T(8,128)S(1)} %copy.18.kern_ref, f32[128,128]{1,0:T(8,128)S(1)} %fusion.18.order_ref), custom_call_target="tpu_custom_call" | custom-call | tf_op jit(solution)/shard_map/beams/pallas_call | solution.py:417
  124.7 4.5 %all-to-all-start.1 = ((f32[8,16,128]{2,1,0:T(8,128)}), f32[8,16,128]{2,1,0:T(8,128)S(1)}, u32[]{:S(2)}, u32[]{:S(2)}) async-start(f32[8,16,128]{2,1,0:T(8,128)} %bitcast.14), calls=%async_computation.1 | async-start | bytes 131072 | tf_op jit(solution)/shard_map/all_to_all | solution.py:432
  129.1 0.0 copy-done.6
  129.1 0.6 fusion.31
  129.8 0.6 iota_compare_fusion.2
  130.4 7.1 %all-to-all-done.1 = f32[8,16,128]{2,1,0:T(8,128)S(1)} async-done(((f32[8,16,128]{2,1,0:T(8,128)}), f32[8,16,128]{2,1,0:T(8,128)S(1)}, u32[]{:S(2)}, u32[]{:S(2)}) %all-to-all-start.1) | async-done | bytes 65568 | tf_op jit(solution)/shard_map/all_to_all | solution.py:432
  137.5 0.8 broadcast_select_fusion
  138.3 6.8 %all-to-all-start.2 = ((f32[32,16,128]{2,1,0:T(8,128)}), f32[32,16,128]{2,1,0:T(8,128)S(1)}, u32[]{:S(2)}, u32[]{:S(2)}) async-start(f32[32,16,128]{2,1,0:T(8,128)} %broadcast_select_fusion), calls=%async_computation.2 | async-start | bytes 524288 | tf_op jit(solution)/shard_map/all_to_all | solution.py:438
  145.2 0.1 copy.15
  145.3 0.1 reduce-window.8
  145.3 0.1 add_reduce_fusion
  145.4 10.0 %all-to-all-done.2 = f32[32,16,128]{2,1,0:T(8,128)S(1)} async-done(((f32[32,16,128]{2,1,0:T(8,128)}), f32[32,16,128]{2,1,0:T(8,128)S(1)}, u32[]{:S(2)}, u32[]{:S(2)}) %all-to-all-start.2) | async-done | bytes 262176 | tf_op jit(solution)/shard_map/all_to_all | solution.py:438
  155.5 0.7 select_reduce_fusion
  (18 shorter events, 0.2 us)
Async XLA Ops:
  2.8 13.5 %copy-start.1 = (bf16[32,8,4096]{2,1,0:T(8,128)(2,1)}, bf16[32,8,4096]{2,1,0:T(8,128)(2,1)S(1)}, u32[]{:S(2)}) copy-start(bf16[32,8,4096]{2,1,0:T(8,128)(2,1)S(1)} %reshape.332.own_ref) | copy-start | bytes 6291460
  2.8 12.7 %copy-start.5 = (s32[2]{0:T(128)S(1)}, s32[2]{0:T(128)}, u32[]{:S(2)}) copy-start(s32[2]{0:T(128)} %shifts_ref.3) | copy-start | bytes 28
  2.8 12.8 %copy-start.4 = (f32[16,256]{1,0:T(8,128)S(1)}, f32[16,256]{1,0:T(8,128)}, u32[]{:S(2)}) copy-start(f32[16,256]{1,0:T(8,128)} %param.7) | copy-start | bytes 49156
  3.8 20.9 %collective-permute-start.2 = (bf16[16,8,2048]{2,1,0:T(8,128)(2,1)}, bf16[16,8,2048]{2,1,0:T(8,128)(2,1)}, u32[]{:S(2)}, u32[]{:S(2)}) collective-permute-start(bf16[16,8,2048]{2,1,0:T(8,128)(2,1)} %get-tuple-element.11), channel_id=1, source_target_pairs={{0,1},{1,2},{2,3},{3,4},{4,5},{5,6},{6,7},{7,0},{8,9},{9,10},{10,1... | collective-permute-start | bytes 1572872 | tf_op jit(solution)/shard_map/ppermute | solution.py:297
  8.4 16.3 %collective-permute-start.3 = (bf16[16,8,1920]{2,1,0:T(8,128)(2,1)}, bf16[16,8,1920]{2,1,0:T(8,128)(2,1)}, u32[]{:S(2)}, u32[]{:S(2)}) collective-permute-start(bf16[16,8,1920]{2,1,0:T(8,128)(2,1)} %get-tuple-element.9), channel_id=1, source_target_pairs={{1,0},{2,1},{3,2},{4,3},{5,4},{6,5},{7,6},{9,8},{10,9},{11,10},{12... | collective-permute-start | bytes 1474568 | tf_op jit(solution)/shard_map/ppermute | solution.py:302
  9.6 24.1 %collective-permute-start = (bf16[16,8,2048]{2,1,0:T(8,128)(2,1)}, bf16[16,8,2048]{2,1,0:T(8,128)(2,1)S(1)}, u32[]{:S(2)}, u32[]{:S(2)}) collective-permute-start(bf16[16,8,2048]{2,1,0:T(8,128)(2,1)} %get-tuple-element.12), channel_id=1, source_target_pairs={{0,1},{1,2},{2,3},{3,4},{4,5},{5,6},{6,7},{7,0},{8,9},{9,10},{10,1... | collective-permute-start | bytes 1572872 | tf_op jit(solution)/shard_map/ppermute | solution.py:297
  14.2 19.6 %collective-permute-start.1 = (bf16[16,8,1920]{2,1,0:T(8,128)(2,1)}, bf16[16,8,1920]{2,1,0:T(8,128)(2,1)}, u32[]{:S(2)}, u32[]{:S(2)}) collective-permute-start(bf16[16,8,1920]{2,1,0:T(8,128)(2,1)} %get-tuple-element.10), channel_id=1, source_target_pairs={{1,0},{2,1},{3,2},{4,3},{5,4},{6,5},{7,6},{9,8},{10,9},{11,10},{12... | collective-permute-start | bytes 1474568 | tf_op jit(solution)/shard_map/ppermute | solution.py:302
  33.8 0.8 copy-start.2
  41.4 21.7 %copy-start.3 = (f32[128,64]{0,1:T(8,128)S(1)}, f32[128,64]{0,1:T(8,128)}, u32[]{:S(2)}) copy-start(f32[128,64]{0,1:T(8,128)} %param.8) | copy-start | bytes 98308
  41.4 21.9 %copy-start.7 = (s32[32]{0:T(128)S(1)}, s32[32]{0:T(128)}, u32[]{:S(2)}) copy-start(s32[32]{0:T(128)} %param.10) | copy-start | bytes 388
  41.4 72.6 %all-to-all-start = ((bf16[256,32,128]{2,1,0:T(8,128)(2,1)}), bf16[256,32,128]{2,1,0:T(8,128)(2,1)S(1)}, u32[]{:S(2)}, u32[]{:S(2)}) async-start(bf16[256,32,128]{2,1,0:T(8,128)(2,1)} %bitcast.29), calls=%async_computation | async-start | bytes 4194304 | tf_op jit(solution)/shard_map/all_to_all | solution.py:378
  114.0 2.6 %copy-start = (bf16[32,256,128]{2,1,0:T(8,128)(2,1)S(1)}, bf16[32,256,128]{2,1,0:T(8,128)(2,1)}, u32[]{:S(2)}) copy-start(bf16[32,256,128]{2,1,0:T(8,128)(2,1)} %pad_maximum_fusion.weights_ref) | copy-start | bytes 6291460
  114.1 2.6 %collective-permute-start.4 = (bf16[32,32,128]{2,1,0:T(8,128)(2,1)S(1)}, bf16[32,32,128]{2,1,0:T(8,128)(2,1)S(1)}, u32[]{:S(2)}, u32[]{:S(2)}) collective-permute-start(bf16[32,32,128]{2,1,0:T(8,128)(2,1)S(1)} %slice_select_fusion), channel_id=1, source_target_pairs={{0,256},{1,257},{2,258},{3,259},{4,260},{5,261},{6,262},{7,263},{8... | collective-permute-start | bytes 786440 | tf_op jit(solution)/shard_map/ppermute | solution.py:383
  116.6 12.5 %copy-start.6 = (s32[32]{0:T(128)S(1)}, s32[32]{0:T(128)}, u32[]{:S(2)}) copy-start(s32[32]{0:T(128)} %param.11) | copy-start | bytes 388
  124.7 12.8 %all-to-all-start.1 = ((f32[8,16,128]{2,1,0:T(8,128)}), f32[8,16,128]{2,1,0:T(8,128)S(1)}, u32[]{:S(2)}, u32[]{:S(2)}) async-start(f32[8,16,128]{2,1,0:T(8,128)} %bitcast.14), calls=%async_computation.1 | async-start | bytes 131072 | tf_op jit(solution)/shard_map/all_to_all | solution.py:432
  138.3 17.1 %all-to-all-start.2 = ((f32[32,16,128]{2,1,0:T(8,128)}), f32[32,16,128]{2,1,0:T(8,128)S(1)}, u32[]{:S(2)}, u32[]{:S(2)}) async-start(f32[32,16,128]{2,1,0:T(8,128)} %broadcast_select_fusion), calls=%async_computation.2 | async-start | bytes 524288 | tf_op jit(solution)/shard_map/all_to_all | solution.py:438

commit v8 on v7

--- a/solution.py
+++ b/solution.py
@@ -13,7 +13,7 @@
 LEAD = 8
 LANES = 128
 TWO_PI = 2.0 * math.pi
-UNROLL = 4
+UNROLL = 8
 PITCH = 40
 SHARES = 2
 FILTER_VMEM = 63 * 1024 * 1024
@@ -81,7 +81,7 @@
                 filtered[half, pl.ds(at, rows), :] = total
         return inner
 
-    lax.fori_loop(0, members, one_sub, 0)
+    lax.fori_loop(0, members, one_sub, 0, unroll=2)
     lane = lax.broadcasted_iota(jnp.int32, (fours, LANES), 1) // width
     for station in range(station_count):
         parts = []

time: 158 us -> 157 us (level)
  no operation moved by 1% of the time
where the time goes in v8:
time: 157 us; the launch traced here: 155 us
  waiting for transfers between devices  61 us (39%)
  starting transfers between devices  45.2 us (29%)
  other arithmetic  21.4 us (14%)
  Pallas kernels  20.6 us (13%)
  local copies, waits for them, and re-layouts  6.49 us (4%)
    all_to_all x1, waiting for transfers between devices, shards(): packed = lax.all_to_all(packed, ('narrow', 'wide'), 0, 0, tiled=True)  36.4 us
    all_to_all x1, starting transfers between devices, shards(): packed = lax.all_to_all(packed, ('narrow', 'wide'), 0, 0, tiled=True)  21.7 us
    pallas_call x2, Pallas kernels, shards(): pl.pallas_call(filter_kernel, grid=(steps,), out_shape=jax.ShapeDtypeStru...  13.4 us
    another operation x4, other arithmetic  11 us
    all_to_all x1, waiting for transfers between devices, shards(): arrived = lax.all_to_all(outgoing, 'wide', 0, 0, tiled=True)  10 us
    ppermute x2, starting transfers between devices, shards(): lax.ppermute(volts[i * share:(i + 1) * share, :, piece_len - LEAD * chan_...  8.02 us
    ppermute x2, waiting for transfers between devices, shards(): lax.ppermute(volts[i * share:(i + 1) * share, :, :ahead], 'narrow', [(i,...  7.28 us
    pallas_call x1, Pallas kernels, shards(): pl.pallas_call(beam_kernel, out_shape=jax.ShapeDtypeStruct((beam_count, b...  7.2 us
  transfers between devices with their start and end apart: 8, of which 6 were waited for; matrix products, arithmetic and copies ran while one was open for 14% of the time, Pallas kernels for 4%

profile of v8, /device:TPU:6, one launch (start us, length us, event | category | flops | bytes accessed | tf_op | source)
XLA Modules:
  0.0 155.3 jit_solution(12612579326138760500)
XLA Ops:
  0.0 2.7 %reshape.332.own_ref = bf16[32,8,4096]{2,1,0:T(8,128)(2,1)S(1)} reshape(bf16[1,32,2,2,2,4096]{5,4,3,2,1,0:T(2,128)(2,1)} %param.6) | data formatting | bytes 4194304 | tf_op jit(solution)/shard_map/reshape | solution.py:292
  2.8 0.0 copy-start.1
  2.8 0.0 copy-start.5
  2.8 0.0 copy-start.4
  2.8 1.1 fusion.39
  3.8 3.5 %collective-permute-start.2 = (bf16[16,8,2048]{2,1,0:T(8,128)(2,1)}, bf16[16,8,2048]{2,1,0:T(8,128)(2,1)}, u32[]{:S(2)}, u32[]{:S(2)}) collective-permute-start(bf16[16,8,2048]{2,1,0:T(8,128)(2,1)} %get-tuple-element.11), channel_id=1, source_target_pairs={{0,1},{1,2},{2,3},{3,4},{4,5},{5,6},{6,7},{7,0},{8,9},{9,10},{10,1... | collective-permute-start | bytes 1572872 | tf_op jit(solution)/shard_map/ppermute | solution.py:297
  7.3 1.0 fusion.38
  8.4 1.3 collective-permute-start.3
  9.6 4.6 %collective-permute-start = (bf16[16,8,2048]{2,1,0:T(8,128)(2,1)}, bf16[16,8,2048]{2,1,0:T(8,128)(2,1)S(1)}, u32[]{:S(2)}, u32[]{:S(2)}) collective-permute-start(bf16[16,8,2048]{2,1,0:T(8,128)(2,1)} %get-tuple-element.12), channel_id=1, source_target_pairs={{0,1},{1,2},{2,3},{3,4},{4,5},{5,6},{6,7},{7,0},{8,9},{9,10},{10,1... | collective-permute-start | bytes 1572872 | tf_op jit(solution)/shard_map/ppermute | solution.py:297
  14.2 1.3 collective-permute-start.1
  15.5 0.0 copy-done.5
  15.5 0.1 iota_subtract_fusion
  15.6 0.0 copy-done.4
  15.6 0.6 pad_maximum_fusion.1.prototype_ref
  16.2 0.0 copy-done.1
  16.2 2.5 %fusion.16 = (bf16[2,256,256]{2,1,0:T(8,128)(2,1)S(1)}, bf16[2,256,256]{2,1,0:T(8,128)(2,1)S(1)}, bf16[2,256,256]{2,1,0:T(8,128)(2,1)S(1)}) fusion(s32[2,256]{1,0:T(2,128)S(1)} %iota_subtract_fusion, s32[256]{0:T(256)S(1)} %fusion.30), kind=kLoop, calls=%fused_computation.36 | loop fusion | flops 2621440 | bytes 789504 | tf_op jit(solution)/shard_map/convert.12
  18.7 1.1 maximum_maximum_fusion.table_ref
  19.8 4.9 %collective-permute-done.3.right_ref = bf16[16,8,1920]{2,1,0:T(8,128)(2,1)} collective-permute-done((bf16[16,8,1920]{2,1,0:T(8,128)(2,1)}, bf16[16,8,1920]{2,1,0:T(8,128)(2,1)}, u32[]{:S(2)}, u32[]{:S(2)}) %collective-permute-start.3) | collective-permute-done | bytes 491552 | tf_op jit(solution)/shard_map/ppermute | solution.py:302
  24.7 0.0 collective-permute-done.2.left_ref
  24.7 6.7 %filter.2.refs_0_ = bf16[8,32,32,128]{3,2,1,0:T(8,128)(2,1)} custom-call(s32[1]{0:T(128)} %bitcast.1.where_ref, s32[2]{0:T(128)} %shifts_ref.3, bf16[32,8,4096]{2,1,0:T(8,128)(2,1)} %copy-done.1, bf16[16,8,2048]{2,1,0:T(8,128)(2,1)} %collective-permute-done.2.left_ref, bf16[16,8,1920]{2,1,0:T(8,128)(2,1)} %collective-permute-done.3.right_ref, ...), custom_call_target="tpu_custom_call" | custom-call | tf_op jit(solution)/shard_map/filter/pallas_call | solution.py:338
  31.4 2.4 %collective-permute-done.1.right_ref = bf16[16,8,1920]{2,1,0:T(8,128)(2,1)} collective-permute-done((bf16[16,8,1920]{2,1,0:T(8,128)(2,1)}, bf16[16,8,1920]{2,1,0:T(8,128)(2,1)}, u32[]{:S(2)}, u32[]{:S(2)}) %collective-permute-start.1) | collective-permute-done | bytes 491552 | tf_op jit(solution)/shard_map/ppermute | solution.py:302
  33.8 0.0 collective-permute-done.left_ref
  33.8 0.0 copy-start.2
  33.8 0.8 copy-done.2
  34.6 6.7 %filter.3 = bf16[8,32,32,128]{3,2,1,0:T(8,128)(2,1)} custom-call(s32[1]{0:T(128)} %bitcast.1.where_ref, s32[2]{0:T(128)} %shifts_ref.3, bf16[32,8,4096]{2,1,0:T(8,128)(2,1)} %copy-done.1, bf16[16,8,2048]{2,1,0:T(8,128)(2,1)} %copy-done.2, bf16[16,8,1920]{2,1,0:T(8,128)(2,1)} %collective-permute-done.1.right_ref, ...), custom_call_target="tpu_custom_call", output_to_operand_aliasing={{}: (7, {})} | custom-call | tf_op jit(solution)/shard_map/filter/pallas_call | solution.py:338
  41.3 0.0 copy-start.3
  41.3 0.0 copy-start.7
  41.3 21.7 %all-to-all-start = ((bf16[256,32,128]{2,1,0:T(8,128)(2,1)}), bf16[256,32,128]{2,1,0:T(8,128)(2,1)S(1)}, u32[]{:S(2)}, u32[]{:S(2)}) async-start(bf16[256,32,128]{2,1,0:T(8,128)(2,1)} %bitcast.29), calls=%async_computation | async-start | bytes 4194304 | tf_op jit(solution)/shard_map/all_to_all | solution.py:378
  63.0 0.0 copy-done.3
  63.1 0.1 copy.17
  63.2 0.0 copy-done.7
  63.2 0.6 fusion.32
  63.9 0.6 compare_select_fusion
  64.5 8.4 %fusion.3 = (bf16[32,128,128]{2,1,0:T(8,128)(2,1)S(1)}, bf16[32,128,128]{2,1,0:T(8,128)(2,1)S(1)}) fusion(f32[128,128]{1,0:T(8,128)S(1)} %copy.17, f32[32]{0:T(128)S(1)} %add_multiply_fusion.1, pred[128]{0:T(512)(128)(4,1)S(1)} %fusion.34), kind=kLoop, calls=%fused_computation.5 | loop fusion | flops 4194304 | bytes 2162944 | tf_op jit(solution)/shard_map/convert.5
  73.0 1.6 pad_maximum_fusion.weights_ref
  74.5 0.1 iota_multiply_fusion
  74.6 0.1 add_multiply_fusion
  74.7 2.5 %cosine_reduce_fusion = (f32[32,32]{1,0:T(8,128)S(1)}, f32[32,32]{1,0:T(8,128)S(1)}) fusion(s32[32,32]{1,0:T(8,128)S(1)} %iota_multiply_fusion, s32[32,32]{1,0:T(8,128)S(1)} %add_multiply_fusion), kind=kLoop, calls=%fused_computation.30 | loop fusion | flops 522240 | bytes 16384 | tf_op jit(solution)/shard_map/reduce_sum | solution.py:408
  77.2 0.3 fusion.14
  77.5 36.4 %all-to-all-done = bf16[256,32,128]{2,1,0:T(8,128)(2,1)S(1)} async-done(((bf16[256,32,128]{2,1,0:T(8,128)(2,1)}), bf16[256,32,128]{2,1,0:T(8,128)(2,1)S(1)}, u32[]{:S(2)}, u32[]{:S(2)}) %all-to-all-start) | async-done | bytes 2097184 | tf_op jit(solution)/shard_map/all_to_all | solution.py:378
  113.9 0.0 copy-start
  114.0 1.6 %collective-permute-start.4 = (bf16[32,32,128]{2,1,0:T(8,128)(2,1)S(1)}, bf16[32,32,128]{2,1,0:T(8,128)(2,1)S(1)}, u32[]{:S(2)}, u32[]{:S(2)}) collective-permute-start(bf16[32,32,128]{2,1,0:T(8,128)(2,1)S(1)} %slice_select_fusion), channel_id=1, source_target_pairs={{0,256},{1,257},{2,258},{3,259},{4,260},{5,261},{6,262},{7,263},{8... | collective-permute-start | bytes 786440 | tf_op jit(solution)/shard_map/ppermute | solution.py:383
  115.6 0.6 copy.18.kern_ref
  116.2 0.1 fusion.18.order_ref
  116.3 0.2 collective-permute-done.4.tail_ref
  116.5 0.0 copy-done
  116.5 0.0 copy-start.6
  116.5 7.2 %beams.1 = f32[128,128]{1,0:T(8,128)} custom-call(bf16[8,32,32,128]{3,2,1,0:T(8,128)(2,1)S(1)} %bitcast.28, bf16[32,32,128]{2,1,0:T(8,128)(2,1)S(1)} %collective-permute-done.4.tail_ref, bf16[32,256,128]{2,1,0:T(8,128)(2,1)S(1)} %copy-done, f32[32,2,32,128]{3,2,1,0:T(8,128)S(1)} %copy.18.kern_ref, f32[128,128]{1,0:T(8,128)S(1)} %fusion.18.order_ref), custom_call_target="tpu_custom_call" | custom-call | tf_op jit(solution)/shard_map/beams/pallas_call | solution.py:417
  123.7 4.5 %all-to-all-start.1 = ((f32[8,16,128]{2,1,0:T(8,128)}), f32[8,16,128]{2,1,0:T(8,128)S(1)}, u32[]{:S(2)}, u32[]{:S(2)}) async-start(f32[8,16,128]{2,1,0:T(8,128)} %bitcast.14), calls=%async_computation.1 | async-start | bytes 131072 | tf_op jit(solution)/shard_map/all_to_all | solution.py:432
  128.2 0.0 copy-done.6
  128.2 0.6 fusion.31
  128.8 0.6 iota_compare_fusion.2
  129.5 7.1 %all-to-all-done.1 = f32[8,16,128]{2,1,0:T(8,128)S(1)} async-done(((f32[8,16,128]{2,1,0:T(8,128)}), f32[8,16,128]{2,1,0:T(8,128)S(1)}, u32[]{:S(2)}, u32[]{:S(2)}) %all-to-all-start.1) | async-done | bytes 65568 | tf_op jit(solution)/shard_map/all_to_all | solution.py:432
  136.6 0.8 broadcast_select_fusion
  137.4 6.8 %all-to-all-start.2 = ((f32[32,16,128]{2,1,0:T(8,128)}), f32[32,16,128]{2,1,0:T(8,128)S(1)}, u32[]{:S(2)}, u32[]{:S(2)}) async-start(f32[32,16,128]{2,1,0:T(8,128)} %broadcast_select_fusion), calls=%async_computation.2 | async-start | bytes 524288 | tf_op jit(solution)/shard_map/all_to_all | solution.py:438
  144.2 0.1 copy.15
  144.3 0.1 reduce-window.8
  144.4 0.1 add_reduce_fusion
  144.5 10.0 %all-to-all-done.2 = f32[32,16,128]{2,1,0:T(8,128)S(1)} async-done(((f32[32,16,128]{2,1,0:T(8,128)}), f32[32,16,128]{2,1,0:T(8,128)S(1)}, u32[]{:S(2)}, u32[]{:S(2)}) %all-to-all-start.2) | async-done | bytes 262176 | tf_op jit(solution)/shard_map/all_to_all | solution.py:438
  154.5 0.7 select_reduce_fusion
  (18 shorter events, 0.2 us)
Async XLA Ops:
  2.8 13.5 %copy-start.1 = (bf16[32,8,4096]{2,1,0:T(8,128)(2,1)}, bf16[32,8,4096]{2,1,0:T(8,128)(2,1)S(1)}, u32[]{:S(2)}) copy-start(bf16[32,8,4096]{2,1,0:T(8,128)(2,1)S(1)} %reshape.332.own_ref) | copy-start | bytes 6291460
  2.8 12.7 %copy-start.5 = (s32[2]{0:T(128)S(1)}, s32[2]{0:T(128)}, u32[]{:S(2)}) copy-start(s32[2]{0:T(128)} %shifts_ref.3) | copy-start | bytes 28
  2.8 12.8 %copy-start.4 = (f32[16,256]{1,0:T(8,128)S(1)}, f32[16,256]{1,0:T(8,128)}, u32[]{:S(2)}) copy-start(f32[16,256]{1,0:T(8,128)} %param.7) | copy-start | bytes 49156
  3.8 20.9 %collective-permute-start.2 = (bf16[16,8,2048]{2,1,0:T(8,128)(2,1)}, bf16[16,8,2048]{2,1,0:T(8,128)(2,1)}, u32[]{:S(2)}, u32[]{:S(2)}) collective-permute-start(bf16[16,8,2048]{2,1,0:T(8,128)(2,1)} %get-tuple-element.11), channel_id=1, source_target_pairs={{0,1},{1,2},{2,3},{3,4},{4,5},{5,6},{6,7},{7,0},{8,9},{9,10},{10,1... | collective-permute-start | bytes 1572872 | tf_op jit(solution)/shard_map/ppermute | solution.py:297
  8.4 16.3 %collective-permute-start.3 = (bf16[16,8,1920]{2,1,0:T(8,128)(2,1)}, bf16[16,8,1920]{2,1,0:T(8,128)(2,1)}, u32[]{:S(2)}, u32[]{:S(2)}) collective-permute-start(bf16[16,8,1920]{2,1,0:T(8,128)(2,1)} %get-tuple-element.9), channel_id=1, source_target_pairs={{1,0},{2,1},{3,2},{4,3},{5,4},{6,5},{7,6},{9,8},{10,9},{11,10},{12... | collective-permute-start | bytes 1474568 | tf_op jit(solution)/shard_map/ppermute | solution.py:302
  9.6 24.1 %collective-permute-start = (bf16[16,8,2048]{2,1,0:T(8,128)(2,1)}, bf16[16,8,2048]{2,1,0:T(8,128)(2,1)S(1)}, u32[]{:S(2)}, u32[]{:S(2)}) collective-permute-start(bf16[16,8,2048]{2,1,0:T(8,128)(2,1)} %get-tuple-element.12), channel_id=1, source_target_pairs={{0,1},{1,2},{2,3},{3,4},{4,5},{5,6},{6,7},{7,0},{8,9},{9,10},{10,1... | collective-permute-start | bytes 1572872 | tf_op jit(solution)/shard_map/ppermute | solution.py:297
  14.2 19.6 %collective-permute-start.1 = (bf16[16,8,1920]{2,1,0:T(8,128)(2,1)}, bf16[16,8,1920]{2,1,0:T(8,128)(2,1)}, u32[]{:S(2)}, u32[]{:S(2)}) collective-permute-start(bf16[16,8,1920]{2,1,0:T(8,128)(2,1)} %get-tuple-element.10), channel_id=1, source_target_pairs={{1,0},{2,1},{3,2},{4,3},{5,4},{6,5},{7,6},{9,8},{10,9},{11,10},{12... | collective-permute-start | bytes 1474568 | tf_op jit(solution)/shard_map/ppermute | solution.py:302
  33.8 0.8 copy-start.2
  41.3 21.7 %copy-start.3 = (f32[128,64]{0,1:T(8,128)S(1)}, f32[128,64]{0,1:T(8,128)}, u32[]{:S(2)}) copy-start(f32[128,64]{0,1:T(8,128)} %param.8) | copy-start | bytes 98308
  41.3 21.9 %copy-start.7 = (s32[32]{0:T(128)S(1)}, s32[32]{0:T(128)}, u32[]{:S(2)}) copy-start(s32[32]{0:T(128)} %param.10) | copy-start | bytes 388
  41.3 72.6 %all-to-all-start = ((bf16[256,32,128]{2,1,0:T(8,128)(2,1)}), bf16[256,32,128]{2,1,0:T(8,128)(2,1)S(1)}, u32[]{:S(2)}, u32[]{:S(2)}) async-start(bf16[256,32,128]{2,1,0:T(8,128)(2,1)} %bitcast.29), calls=%async_computation | async-start | bytes 4194304 | tf_op jit(solution)/shard_map/all_to_all | solution.py:378
  113.9 2.6 %copy-start = (bf16[32,256,128]{2,1,0:T(8,128)(2,1)S(1)}, bf16[32,256,128]{2,1,0:T(8,128)(2,1)}, u32[]{:S(2)}) copy-start(bf16[32,256,128]{2,1,0:T(8,128)(2,1)} %pad_maximum_fusion.weights_ref) | copy-start | bytes 6291460
  114.0 2.6 %collective-permute-start.4 = (bf16[32,32,128]{2,1,0:T(8,128)(2,1)S(1)}, bf16[32,32,128]{2,1,0:T(8,128)(2,1)S(1)}, u32[]{:S(2)}, u32[]{:S(2)}) collective-permute-start(bf16[32,32,128]{2,1,0:T(8,128)(2,1)S(1)} %slice_select_fusion), channel_id=1, source_target_pairs={{0,256},{1,257},{2,258},{3,259},{4,260},{5,261},{6,262},{7,263},{8... | collective-permute-start | bytes 786440 | tf_op jit(solution)/shard_map/ppermute | solution.py:383
  116.5 11.7 %copy-start.6 = (s32[32]{0:T(128)S(1)}, s32[32]{0:T(128)}, u32[]{:S(2)}) copy-start(s32[32]{0:T(128)} %param.11) | copy-start | bytes 388
  123.7 12.8 %all-to-all-start.1 = ((f32[8,16,128]{2,1,0:T(8,128)}), f32[8,16,128]{2,1,0:T(8,128)S(1)}, u32[]{:S(2)}, u32[]{:S(2)}) async-start(f32[8,16,128]{2,1,0:T(8,128)} %bitcast.14), calls=%async_computation.1 | async-start | bytes 131072 | tf_op jit(solution)/shard_map/all_to_all | solution.py:432
  137.4 17.2 %all-to-all-start.2 = ((f32[32,16,128]{2,1,0:T(8,128)}), f32[32,16,128]{2,1,0:T(8,128)S(1)}, u32[]{:S(2)}, u32[]{:S(2)}) async-start(f32[32,16,128]{2,1,0:T(8,128)} %broadcast_select_fusion), calls=%async_computation.2 | async-start | bytes 524288 | tf_op jit(solution)/shard_map/all_to_all | solution.py:438
